TPU v7x, 32 devices: a whole 2x2x4 slice. The times are simulated.
32 devices in a mesh: src: 4 (over z), tgt: 8 (over y, x, core).
Axes of the slice: x: 2, y: 2, z: 4, core: 2. Of those that a mesh axis runs over, the one named last changes fastest.
Arguments:
- src_emb: bfloat16 [8192, 1024], P(('src', 'tgt')), may hold values from 0 to 500, as said below
- tgt_emb: bfloat16 [4096, 1024], P('tgt'), may hold values from 0 to 500, as said below
- pair_list: int32 [32, 8], P('src'), may hold values from 0 to 15, as said below
- fwd_idx: int32 [8192, 16], P('src'), may hold values from 0 to 4095, as said below
- bwd_idx: int32 [4096, 16], P('tgt'), may hold values from 0 to 8191, as said below
Outputs:
- src_best: float32 [8192], P(('src', 'tgt'))
- tgt_best: float32 [4096], P('tgt')
Inputs may be any that keep to these rules, and one draw needn't show every extreme that they name: src_emb entries are positive. tgt_emb entries are positive. `pair_list`: each row names 8 distinct target blocks in ascending order. Row b names block c whenever c mod 32 equals b, so every target block is named. All 2 blocks of one tgt index, the same for every row, are named in every row. `fwd_idx`: entry [i, k] is a target row of a block named in row i // 256 of pair_list; entries may repeat. `bwd_idx`: entry [j, k] is a source row of a block whose pair_list row names block j // 256; entries may repeat.
All inputs are finite; a program needn't handle non-finite values.
Results may differ from a plain program's by a relative error of at most 0.00091.
Values may be sent and summed in bfloat16 or wider, within the bound.
No kernel may reach another device: no remote copies, remote signals or barrier semaphores. Data moves between devices by JAX's collectives and lax.ppermute only.
A program may use at most 64 MiB of HBM per device.

v0:
```python
import jax
import jax.numpy as jnp
from jax import lax
from jax.sharding import PartitionSpec as P

BLOCK = 256
SB_DEV = 1


def unit_rows(values):
    wide = values.astype(jnp.float32)
    factor = lax.rsqrt(jnp.sum(wide * wide, axis=1, keepdims=True) + 1e-06)
    return (wide * factor).astype(jnp.bfloat16)


def body(src_emb, tgt_emb, pair_list, fwd_idx, bwd_idx):
    src_pos = lax.axis_index("src")
    tgt_pos = lax.axis_index("tgt")
    tgt_count = lax.axis_size("tgt")
    src_unit = unit_rows(src_emb)
    tgt_unit = unit_rows(tgt_emb)
    width = src_unit.shape[1]
    probes = pair_list.shape[1]
    neighbours = fwd_idx.shape[1]
    src_rows_dev = src_unit.shape[0]
    tgt_rows_dev = tgt_unit.shape[0]
    every_tgt = lax.all_gather(tgt_unit, "tgt", axis=0, tiled=True)
    every_list = lax.all_gather(bwd_idx, "tgt", axis=0, tiled=True)
    total_blocks = every_tgt.shape[0] // BLOCK
    every_tile = every_tgt.reshape(total_blocks, BLOCK, width)
    list_tiles = every_list.reshape(total_blocks, BLOCK, neighbours)
    own_lists = lax.dynamic_slice_in_dim(pair_list, tgt_pos * SB_DEV, SB_DEV, 0)
    own_fwd = lax.dynamic_slice_in_dim(fwd_idx, tgt_pos * src_rows_dev, src_rows_dev, 0).reshape(
        SB_DEV, BLOCK, neighbours
    )
    own_first = (src_pos * tgt_count + tgt_pos) * SB_DEV
    src_tiles = src_unit.reshape(SB_DEV, BLOCK, width)

    def block_scores(position):
        return jnp.einsum(
            "id,pjd->pij",
            src_tiles[position],
            every_tile[own_lists[position]],
            preferred_element_type=jnp.float32,
        )

    bwd_part = jnp.zeros((total_blocks, BLOCK), jnp.float32)
    position = 0
    scores = block_scores(position)
    listed = own_lists[position]
    fwd_near = own_fwd[position]
    fwd_hit = (fwd_near // BLOCK)[None, :, :] == listed[:, None, None]
    fwd_value = jnp.take_along_axis(
        scores, jnp.broadcast_to(fwd_near % BLOCK, (probes, BLOCK, neighbours)), axis=2
    )
    fwd_pieces = [jnp.sum(jnp.where(fwd_hit, fwd_value, 0.0), axis=(0, 2)) / neighbours]
    bwd_near = list_tiles[listed]
    bwd_hit = bwd_near // BLOCK == own_first + position
    bwd_value = jnp.take_along_axis(jnp.swapaxes(scores, 1, 2), bwd_near % BLOCK, axis=2)
    bwd_part = bwd_part.at[listed].add(jnp.sum(jnp.where(bwd_hit, bwd_value, 0.0), axis=2))
    tgt_terms = lax.psum_scatter(bwd_part.reshape(-1), "tgt", scatter_dimension=0, tiled=True)
    bwd_mean = lax.psum(tgt_terms, "src") / neighbours
    bwd_every = lax.all_gather(bwd_mean, "tgt", axis=0, tiled=True).reshape(total_blocks, BLOCK)
    tgt_peak = jnp.zeros((total_blocks, BLOCK), jnp.float32)
    position = 0
    scores = block_scores(position)
    listed = own_lists[position]
    ratio = 2.0 * scores / (fwd_pieces[position][None, :, None] + bwd_every[listed][:, None, :])
    src_pieces = jnp.max(ratio, axis=(0, 2))
    tgt_peak = tgt_peak.at[listed].max(jnp.max(ratio, axis=1))
    every_best = lax.pmax(tgt_peak.reshape(-1), ("src", "tgt"))
    tgt_best = lax.dynamic_slice_in_dim(every_best, tgt_pos * tgt_rows_dev, tgt_rows_dev, 0)
    return (src_pieces, tgt_best)


def solution(mesh):
    return jax.shard_map(
        body,
        mesh=mesh,
        in_specs=(
            P(("src", "tgt"), None),
            P("tgt", None),
            P("src", None),
            P("src", None),
            P("tgt", None),
        ),
        out_specs=(P(("src", "tgt")), P("tgt")),
        check_vma=False,
    )
```

profile of v0, /device:TPU:0, one launch (start us, length us, event | category | flops | bytes accessed | tf_op | source)
XLA Modules:
  0.0 815.1 jit_solution(12946152549853882488)
XLA Ops:
  7.2 1.6 fusion
  8.8 2.5 fusion.1
  11.4 11.0 %all_gather.10 = s32[4096,16]{0,1:T(8,128)S(1)} all-gather(s32[512,16]{0,1:T(8,128)} %param.11), channel_id=1, replica_groups=mesh['src'=4,'tgt'=8] {'tgt'}, dimensions={0}, use_global_device_ids=true | all-gather | bytes 294912 | tf_op jit(solution)/shard_map/all_gather | solution.py:28
  22.4 0.7 fusion.25
  23.1 0.6 gather_fusion.1
  24.4 1.3 add_select_fusion.3
  25.8 0.7 broadcast_compare_fusion
  26.9 1.0 reshape.145
  27.9 0.6 dynamic-slice
  29.1 1.2 fusion.26
  30.5 38.1 %all-gather.3.cloned.1.call-done = bf16[4096,1024]{1,0:T(8,128)(2,1)} async-done(((bf16[512,1024]{1,0:T(8,128)(2,1)}), bf16[4096,1024]{1,0:T(8,128)(2,1)}) %all-gather.3.cloned.1.call-update) | async-done | bytes 8388624 | tf_op jit(solution)/shard_map/all_gather | solution.py:27
  68.6 6.2 gather_fusion
  74.8 3.6 fusion.7
  78.4 321.5 %gather_fusion.4 = f32[32768]{0:T(1024)S(1)} fusion(f32[8,256,256]{2,1,0:T(8,128)S(1)} %fusion.7, s32[32768]{0:T(1024)S(1)} %reshape.150), kind=kCustom, calls=%fused_computation.1.clone | custom fusion | bytes 655360 | tf_op jit(solution)/shard_map/jit(take_along_axis)/gather | solution.py:59
  400.7 0.8 scatter_custom_fusion
  401.4 23.5 %all-reduce = f32[4096]{0:T(1024)S(1)} all-reduce(f32[4096]{0:T(1024)S(1)} %bitcast.44), channel_id=2, replica_groups=mesh['src'=4,'tgt'=8] {'tgt'}, use_global_device_ids=true, to_apply=%region_5.7.clone | all-reduce | flops 4096 | bytes 32768
  425.0 11.7 %psum.7 = f32[512]{0:T(512)S(1)} all-reduce(f32[512]{0:T(512)S(1)} %dynamic-slice.1), channel_id=1, replica_groups=mesh['src'=4,'tgt'=8] {'src'}, use_global_device_ids=true, to_apply=%region_6.8 | all-reduce | flops 512 | bytes 4096 | tf_op jit(solution)/shard_map/psum | solution.py:62
  436.7 8.9 %all-gather = f32[8,1,512]{2,1,0:T(1,128)S(1)} all-gather(f32[1,1,512]{2,1,0:T(1,128)S(1)} %bitcast.46), channel_id=1, replica_groups=mesh['src'=4,'tgt'=8] {'tgt'}, dimensions={0}, use_global_device_ids=true | all-gather | bytes 18432 | tf_op jit(solution)/shard_map/all_gather | solution.py:63
  445.6 1.3 gather_fusion.2
  446.9 320.9 %gather_fusion.3 = f32[32768]{0:T(1024)S(1)} fusion(f32[8,256,256]{1,2,0:T(8,128)S(1)} %bitcast.38, s32[32768]{0:T(1024)S(1)} %copy-done), kind=kCustom, calls=%fused_computation.clone | custom fusion | bytes 655360 | tf_op jit(solution)/shard_map/jit(take_along_axis)/gather | solution.py:53
  768.6 1.2 fusion.4
  769.9 0.7 scatter_custom_fusion.1
  770.6 37.0 %pmax.7 = f32[4096]{0:T(1024)S(1)} all-reduce(f32[4096]{0:T(1024)S(1)} %bitcast.45), channel_id=1, replica_groups=mesh['src'=4,'tgt'=8] {'src','tgt'}, use_global_device_ids=true, to_apply=%region_10.12 | all-reduce | flops 4096 | bytes 32768 | tf_op jit(solution)/shard_map/pmax | solution.py:71
  807.6 0.7 dynamic_slice.11
  (58 shorter events, 3.1 us)
Async XLA Ops:
  7.2 20.7 %copy-start.15 = (u32[32]{0:T(128)S(1)}, u32[32]{0:T(128)}, u32[]{:S(2)}) copy-start(u32[32]{0:T(128)} %constant.147) | copy-start | bytes 388
  7.2 23.1 %copy-start.3 = (bf16[256,1024]{1,0:T(8,128)(2,1)S(1)}, bf16[256,1024]{1,0:T(8,128)(2,1)}, u32[]{:S(2)}) copy-start(bf16[256,1024]{1,0:T(8,128)(2,1)} %param.7) | copy-start | bytes 1572868
  7.2 61.4 %all-gather.3.cloned.1.call-start = ((), (), s32[]{:S(2)}) async-start(), calls=%async_computation | async-start | bytes 9437184 | tf_op jit(solution)/shard_map/all_gather | solution.py:27
  23.1 6.0 copy-start.14
  23.1 45.5 %copy-start.12 = (s32[1024]{0:T(1024)}, s32[1024]{0:T(1024)S(1)}, u32[]{:S(2)}) copy-start(s32[1024]{0:T(1024)S(1)} %pad_clamp_fusion) | copy-start | bytes 12292
  23.7 44.9 %copy-start.1 = (s32[8,256,16]{1,2,0:T(8,128)}, s32[8,256,16]{1,2,0:T(8,128)S(1)}, u32[]{:S(2)}) copy-start(s32[8,256,16]{1,2,0:T(8,128)S(1)} %gather_fusion.1) | copy-start | bytes 393220
  26.5 42.1 %copy-start.4 = (s32[256,16]{0,1:T(8,128)}, s32[256,16]{0,1:T(8,128)S(1)}, u32[]{:S(2)}) copy-start(s32[256,16]{0,1:T(8,128)S(1)} %get-tuple-element.8) | copy-start | bytes 49156
  26.5 42.1 %copy-start.9 = (pred[256,16]{0,1:T(8,128)(4,1)}, pred[256,16]{0,1:T(8,128)(4,1)S(1)}, u32[]{:S(2)}) copy-start(pred[256,16]{0,1:T(8,128)(4,1)S(1)} %get-tuple-element.7) | copy-start | bytes 12292
  26.5 42.1 %copy-start.6 = (s32[256,16]{0,1:T(8,128)}, s32[256,16]{0,1:T(8,128)S(1)}, u32[]{:S(2)}) copy-start(s32[256,16]{0,1:T(8,128)S(1)} %broadcast_add_fusion) | copy-start | bytes 49156
  78.4 322.1 %copy-start.2 = (s32[8,256,16]{1,2,0:T(8,128)S(1)}, s32[8,256,16]{1,2,0:T(8,128)}, u32[]{:S(2)}) copy-start(s32[8,256,16]{1,2,0:T(8,128)} %copy-done.1) | copy-start | bytes 393220
  399.9 47.0 %copy-start = (s32[32768]{0:T(1024)S(1)}, s32[32768]{0:T(1024)}, u32[]{:S(2)}) copy-start(s32[32768]{0:T(1024)} %reshape.145) | copy-start | bytes 393220
  446.9 321.6 %copy-start.5 = (s32[256,16]{0,1:T(8,128)S(1)}, s32[256,16]{0,1:T(8,128)}, u32[]{:S(2)}) copy-start(s32[256,16]{0,1:T(8,128)} %copy-done.4) | copy-start | bytes 49156
  446.9 321.6 %copy-start.7 = (s32[256,16]{0,1:T(8,128)S(1)}, s32[256,16]{0,1:T(8,128)}, u32[]{:S(2)}) copy-start(s32[256,16]{0,1:T(8,128)} %copy-done.6) | copy-start | bytes 49156
  446.9 321.6 %copy-start.8 = (s32[256,16]{0,1:T(8,128)S(1)}, s32[256,16]{0,1:T(8,128)}, u32[]{:S(2)}) copy-start(s32[256,16]{0,1:T(8,128)} %get-tuple-element.5) | copy-start | bytes 49156
  446.9 321.6 %copy-start.10 = (pred[256,16]{0,1:T(8,128)(4,1)S(1)}, pred[256,16]{0,1:T(8,128)(4,1)}, u32[]{:S(2)}) copy-start(pred[256,16]{0,1:T(8,128)(4,1)} %copy-done.9) | copy-start | bytes 12292
  446.9 321.6 %copy-start.13 = (s32[8]{0:T(128)S(1)}, s32[8]{0:T(128)}, u32[]{:S(2)}) copy-start(s32[8]{0:T(128)} %fusion.26) | copy-start | bytes 100
  446.9 321.7 %copy-start.11 = (f32[8,256]{1,0:T(8,128)S(1)}, f32[8,256]{1,0:T(8,128)}, u32[]{:S(2)}) copy-start(f32[8,256]{1,0:T(8,128)} %gather_fusion.2) | copy-start | bytes 24580
Sparse Core Ops, SparseCore 0:
  11.5 57.0 all-gather.2
where the time goes:
time: 816 us; the launch traced here: 815 us
  local copies, waits for them, and re-layouts  656 us (80%)
  blocking collectives  92 us (11%)
  waiting for transfers between devices  38.1 us (5%)
  between operations  15 us (2%)
  other arithmetic  10.2 us (1%)
    gather x5, local copies, waits for them, and re-layouts, body(): jnp.take_along_axis(scores, jnp.broadcast_to(fwd_near % BLOCK, (probes, B...  323 us
    gather x5, local copies, waits for them, and re-layouts, body(): jnp.take_along_axis(jnp.swapaxes(scores, 1, 2), bwd_near % BLOCK, axis=2)  323 us
    all_gather x1, waiting for transfers between devices, body(): every_tgt = lax.all_gather(tgt_unit, 'tgt', axis=0, tiled=True)  38.1 us
    pmax x1, blocking collectives, body(): every_best = lax.pmax(tgt_peak.reshape(-1), ('src', 'tgt'))  37 us
    unnamed x1, blocking collectives  23.5 us
  transfers between devices with their start and end apart: 1, of which 1 were waited for; matrix products, arithmetic and copies ran while one was open for 1% of the time, Pallas kernels for 0%

commit v1 on v0

v1 whole, which is shorter than its diff:
```python
import functools

import jax
import jax.numpy as jnp
from jax import lax
from jax.experimental import pallas as pl
from jax.experimental.pallas import tpu as pltpu
from jax.sharding import PartitionSpec as P

BLOCK = 256
LANES = 128
PAIR = 2 * BLOCK
ROWS_CONTRACT = (((1,), (1,)), ((), ()))
VMEM = pl.BlockSpec(memory_space=pltpu.VMEM)
SMEM = pl.BlockSpec(memory_space=pltpu.SMEM)


def unit_rows(values):
    wide = values.astype(jnp.float32)
    factor = lax.rsqrt(jnp.sum(wide * wide, axis=1, keepdims=True) + 1e-06)
    return (wide * factor).astype(jnp.bfloat16)


def params(flops, bytes_accessed, **more):
    return dict(
        compiler_params=pltpu.CompilerParams(vmem_limit_bytes=32 * 2**20, **more),
        cost_estimate=pl.CostEstimate(flops=flops, bytes_accessed=bytes_accessed, transcendentals=0),
    )


def prepare_kernel(
    slots, own_ref, sibling_ref, pairs_ref, fwd_ref, bwd_own_ref, bwd_sibling_ref, unit_ref, fwd_at_ref, bwd_at_ref, listed_ref
):
    src_pos = lax.axis_index("src")
    tgt_pos = lax.axis_index("tgt")
    tgt_count = lax.axis_size("tgt")
    rows = own_ref.shape[0]

    def normalise(ref, base):
        def step(i, _):
            at = pl.multiple_of(i * 64, 64)
            unit_ref[pl.ds(base + at, 64), :] = unit_rows(ref[pl.ds(at, 64), :])
            return 0

        lax.fori_loop(0, rows // 64, step, 0)

    normalise(own_ref, 0)
    normalise(sibling_ref, rows)

    for group in range(fwd_at_ref.shape[0]):
        parts = []
        for g in range(8):
            slot, half = (group * 8 + g) // 2, g % 2
            first = lax.bitwise_xor(tgt_pos, 2 * slot) * BLOCK + half * LANES
            parts.append(fwd_ref[:, pl.ds(pl.multiple_of(first, LANES), LANES)])
        near = jnp.concatenate(parts, axis=0)
        chip = lax.bitwise_xor(near // rows, tgt_pos)
        at = jnp.where(chip < 2, chip * rows + near % rows, -1)
        fwd_at_ref[group] = at.T
    tiles = rows // LANES
    for group in range(bwd_at_ref.shape[0]):
        parts = []
        for g in range(8):
            tile = group * 8 + g
            ref = bwd_own_ref if tile < tiles else bwd_sibling_ref
            parts.append(ref[:, (tile % tiles) * LANES : (tile % tiles + 1) * LANES])
        near = jnp.concatenate(parts, axis=0)
        block = near // BLOCK - src_pos * tgt_count
        inside = (block >= 0) & (block < tgt_count)
        peer = lax.bitwise_xor(jnp.where(inside, block, 0), tgt_pos)
        inside = inside & (lax.bitwise_and(peer, 1) == 0)
        at = jnp.where(inside, (peer // 2) * BLOCK + near % BLOCK, -1)
        bwd_at_ref[group] = at.T
    blocks = 2 * rows // BLOCK
    for slot in range(slots):
        row = lax.bitwise_xor(tgt_pos, 2 * slot)
        named = [pairs_ref[row, k] for k in range(pairs_ref.shape[1])]
        for p in range(blocks):
            owner = lax.bitwise_xor(tgt_pos, p // (blocks // 2))
            block = owner * (blocks // 2) + p % (blocks // 2)
            hit = jnp.int32(0)
            for name in named:
                hit = hit | (name == block).astype(jnp.int32)
            listed_ref[slot * blocks + p] = hit


def score_kernel(slot, finish, halves, *refs):
    chunk_refs = refs[:halves]
    unit_ref, fwd_at_ref, bwd_at_ref = refs[halves : halves + 3]
    if finish:
        fwd_before, bwd_before = refs[halves + 3 : halves + 5]
        scores_ref, fwd_ref, bwd_ref, turned_ref, fwd_got, bwd_got = refs[halves + 5 :]
    else:
        scores_ref, fwd_ref, bwd_ref, turned_ref, fwd_got, bwd_got = refs[halves + 3 :]
    unit = jnp.concatenate([unit_rows(ref[...]) for ref in chunk_refs], axis=0)
    scores_ref[...] = lax.dot_general(unit, unit_ref[...], ROWS_CONTRACT, preferred_element_type=jnp.float32)
    turned_ref[...] = lax.dot_general(unit_ref[...], unit, ROWS_CONTRACT, preferred_element_type=jnp.float32)
    columns = unit_ref.shape[0] // LANES
    lane_tile = lax.broadcasted_iota(jnp.int32, (8, LANES), 1) // 16

    def gather(q, _):
        at = pl.multiple_of(q * 8, 8)
        near = fwd_at_ref[(2 * slot) // 8, pl.ds(at, 8), :]
        low, high = near & (LANES - 1), near >> 7
        got = jnp.zeros((8, LANES), jnp.float32)
        for half in range(2):
            mine = jnp.where(lane_tile == (2 * slot + half) % 8, high, -1)
            for c in range(columns):
                piece = scores_ref[pl.ds(half * LANES + at, 8), c * LANES : (c + 1) * LANES]
                got = jnp.where(mine == c, jnp.take_along_axis(piece, low, axis=1), got)
        fwd_got[pl.ds(at, 8), :] = got
        for group in range(bwd_at_ref.shape[0]):
            near = bwd_at_ref[group, pl.ds(at, 8), :]
            low, high = near & (LANES - 1), near >> 7
            got = jnp.zeros((8, LANES), jnp.float32)
            for g in range(8):
                mine = jnp.where(lane_tile == g, high, -1)
                for c in range(2):
                    piece = turned_ref[pl.ds((group * 8 + g) * LANES + at, 8), c * LANES : (c + 1) * LANES]
                    got = jnp.where(mine == 2 * slot + c, jnp.take_along_axis(piece, low, axis=1), got)
            bwd_got[group, pl.ds(at, 8), :] = got
        return 0

    lax.fori_loop(0, LANES // 8, gather, 0, unroll=2)
    first = (2 * slot) % 8 * 16
    fwd = fwd_got[...].T[first : first + 32].reshape(2, 16, LANES).sum(axis=1)
    bwd = [bwd_got[group].T.reshape(8, 16, LANES).sum(axis=1) for group in range(bwd_at_ref.shape[0])]
    bwd = bwd[0] if len(bwd) == 1 else jnp.concatenate(bwd, axis=0)
    if finish:
        before = fwd_before.shape[0]
        fwd_ref[:before, :] = fwd_before[...]
        fwd_ref[before:, :] = fwd
        bwd_ref[...] = bwd + bwd_before[...]
    else:
        fwd_ref[...] = fwd
        bwd_ref[...] = bwd


def margin_kernel(slots, columns, *refs):
    score_refs = refs[:slots]
    fwd_ref, bwd_ref, listed_ref, src_ref, tgt_ref, wide_ref, row_ref, col_ref = refs[slots:]
    blocks = columns // BLOCK
    row_ref[...] = jnp.zeros_like(row_ref)
    col_ref[...] = jnp.zeros_like(col_ref)
    for g in range(2 * slots):
        wide_ref[g * LANES : (g + 1) * LANES, :] = jnp.broadcast_to(fwd_ref[g : g + 1, :], (LANES, LANES)).T

    for slot in range(slots):
        scores_ref = score_refs[slot]

        def tile(p, _, slot=slot, scores_ref=scores_ref):
            @pl.when(listed_ref[slot * blocks + p] != 0)
            def _():
                bwd = [jnp.broadcast_to(bwd_ref[pl.ds(2 * p + c, 1), :], (8, LANES)) for c in range(2)]

                def rows(i, peak):
                    at = pl.multiple_of(i * 8, 8)
                    fwd = wide_ref[pl.ds(slot * BLOCK + at, 8), :]
                    best = row_ref[pl.ds(slot * BLOCK + at, 8), :]
                    peak = list(peak)
                    for c in range(2):
                        score = scores_ref[pl.ds(at, 8), pl.ds(pl.multiple_of(p * BLOCK + c * LANES, LANES), LANES)]
                        total = fwd + bwd[c]
                        inverse = pl.reciprocal(total, approx=True)
                        inverse = inverse * (2.0 - total * inverse)
                        ratio = score * inverse
                        best = jnp.maximum(best, ratio)
                        peak[c] = jnp.maximum(peak[c], ratio)
                    row_ref[pl.ds(slot * BLOCK + at, 8), :] = best
                    return tuple(peak)

                zero = jnp.zeros((8, LANES), jnp.float32)
                peak = lax.fori_loop(0, BLOCK // 8, rows, (zero, zero), unroll=8)
                for c in range(2):
                    where = pl.ds(pl.multiple_of(p * BLOCK + c * LANES, LANES), LANES)
                    col_ref[:, where] = jnp.maximum(col_ref[:, where], peak[c])

            return 0

        lax.fori_loop(0, blocks, tile, 0)
    for g in range(2 * slots):
        src_ref[g : g + 1, :] = 32.0 * jnp.max(row_ref[g * LANES : (g + 1) * LANES, :].T, axis=0, keepdims=True)
    for c in range(columns // LANES):
        tgt_ref[c : c + 1, :] = 32.0 * jnp.max(col_ref[:, c * LANES : (c + 1) * LANES], axis=0, keepdims=True)


def swap(value, axis, mask):
    count = lax.axis_size(axis)
    return lax.ppermute(value, axis, [(i, i ^ mask) for i in range(count)])


def turn_slots(value, bit):
    slots = value.shape[0] // 2
    return value.reshape(slots // (2 * bit), 2, bit * 2, LANES)[:, ::-1].reshape(value.shape)


def body(src_emb, tgt_emb, pair_list, fwd_idx, bwd_idx):
    tgt_count = lax.axis_size("tgt")
    src_count = lax.axis_size("src")
    slots = tgt_count // 2
    rows, width = tgt_emb.shape
    columns = 2 * rows
    tgt_bits = [1 << b for b in range(1, tgt_count.bit_length() - 1)]
    src_bits = [1 << b for b in range(src_count.bit_length() - 1)]

    upper, lower = src_emb[: BLOCK // 2], src_emb[BLOCK // 2 :]
    x_upper = swap(upper, "tgt", 2)
    y_lower = swap(lower, "tgt", 4)
    x_lower = swap(lower, "tgt", 2)
    y_upper = swap(upper, "tgt", 4)
    far_upper = swap(x_upper, "tgt", 4)
    far_lower = swap(y_lower, "tgt", 2)
    chunks = [(src_emb,), (x_upper, x_lower), (y_upper, y_lower), (far_upper, far_lower)]
    for bit in tgt_bits[2:]:
        chunks += [tuple(swap(part, "tgt", bit) for part in held) for held in chunks]

    sibling_emb = swap(tgt_emb, "tgt", 1)
    bwd_lists = bwd_idx.T
    sibling_lists = swap(bwd_lists, "tgt", 1)
    lists = jax.ShapeDtypeStruct((-(-slots // 4), LANES, LANES), jnp.int32)
    bwd_shape = jax.ShapeDtypeStruct((columns // (8 * LANES), LANES, LANES), jnp.int32)
    unit, fwd_at, bwd_at, listed = pl.pallas_call(
        functools.partial(prepare_kernel, slots),
        out_shape=(
            jax.ShapeDtypeStruct((columns, width), jnp.bfloat16),
            lists,
            bwd_shape,
            jax.ShapeDtypeStruct((slots * columns // BLOCK,), jnp.int32),
        ),
        in_specs=[VMEM, VMEM, SMEM, VMEM, VMEM, VMEM],
        out_specs=(VMEM, VMEM, VMEM, SMEM),
        name="prepare",
        **params(columns * width * 6, columns * width * 4),
    )(tgt_emb, sibling_emb, pair_list, fwd_idx.T, bwd_lists, sibling_lists)

    scores, fwd_parts, bwd_parts = [], [], []
    for slot in range(slots):
        finish = slot == slots - 1
        halves = len(chunks[slot])
        args = [*chunks[slot], unit, fwd_at, bwd_at]
        if finish:
            args += [jnp.concatenate(fwd_parts, axis=0), sum(bwd_parts[1:], bwd_parts[0])]
        score, fwd, bwd = pl.pallas_call(
            functools.partial(score_kernel, slot, finish, halves),
            out_shape=(
                jax.ShapeDtypeStruct((BLOCK, columns), jnp.float32),
                jax.ShapeDtypeStruct((2 * slots if finish else 2, LANES), jnp.float32),
                jax.ShapeDtypeStruct((columns // LANES, LANES), jnp.float32),
            ),
            in_specs=[VMEM] * len(args),
            out_specs=(VMEM, VMEM, VMEM),
            scratch_shapes=[
                pltpu.VMEM((columns, BLOCK), jnp.float32),
                pltpu.VMEM((LANES, LANES), jnp.float32),
                pltpu.VMEM(bwd_shape.shape, jnp.float32),
            ],
            name=f"score_{slot}",
            **params(4 * BLOCK * columns * width, BLOCK * columns * 4),
        )(*args)
        scores.append(score)
        fwd_parts.append(fwd)
        bwd_parts.append(bwd)

    def turn_pair(value):
        half = value.shape[0] // 2
        return jnp.concatenate([value[half:], value[:half]], axis=0)

    bwd = bwd + turn_pair(swap(bwd, "tgt", 1))
    for bit in tgt_bits:
        fwd = fwd + turn_slots(swap(fwd, "tgt", bit), bit // 2)
    for bit in src_bits:
        bwd = bwd + swap(bwd, "src", bit)

    src_best, tgt_best = pl.pallas_call(
        functools.partial(margin_kernel, slots, columns),
        out_shape=(
            jax.ShapeDtypeStruct((2 * slots, LANES), jnp.float32),
            jax.ShapeDtypeStruct((columns // LANES, LANES), jnp.float32),
        ),
        in_specs=[VMEM] * (slots + 2) + [SMEM],
        out_specs=(VMEM, VMEM),
        scratch_shapes=[
            pltpu.VMEM((slots * BLOCK, LANES), jnp.float32),
            pltpu.VMEM((slots * BLOCK, LANES), jnp.float32),
            pltpu.VMEM((8, columns), jnp.float32),
        ],
        name="margins",
        **params(slots * BLOCK * columns * 10, slots * BLOCK * columns * 4),
    )(*scores, fwd, bwd, listed)

    half = columns // LANES // 2
    tgt_best = jnp.maximum(tgt_best[:half], swap(tgt_best[half:], "tgt", 1))
    for bit in src_bits:
        tgt_best = jnp.maximum(tgt_best, swap(tgt_best, "src", bit))
    for bit in reversed(tgt_bits):
        keep = src_best.shape[0] // 2
        src_best = jnp.maximum(src_best[:keep], swap(src_best[keep:], "tgt", bit))
    return src_best.reshape(-1), tgt_best.reshape(-1)


def solution(mesh):
    return jax.shard_map(
        body,
        mesh=mesh,
        in_specs=(
            P(("src", "tgt"), None),
            P("tgt", None),
            P("src", None),
            P("src", None),
            P("tgt", None),
        ),
        out_specs=(P(("src", "tgt")), P("tgt")),
        check_vma=False,
    )
```

time: 816 us -> 57 us (0.07)
  local copies, waits for them, and re-layouts: 656 us -> 6.86 us
  blocking collectives: 92 us -> 0 us
  waiting for transfers between devices: 38.1 us -> 12.3 us
  starting transfers between devices: 0.04 us -> 19.5 us
  Pallas kernels: 0 us -> 16.1 us
  between operations: 15 us -> 0.79 us
  other arithmetic: 10.2 us -> 1.2 us
    gather x13 -> x0, local copies, waits for them, and re-layouts: 654 us -> none  [the longest x5 323 us: body(): jnp.take_along_axis(scores, jnp.broadcast_to(fwd_near % BLOCK, (probes, B...]
    all_gather x1 -> x0, waiting for transfers between devices: 38.1 us -> none  [body(): every_tgt = lax.all_gather(tgt_unit, 'tgt', axis=0, tiled=True)]
    pmax x1 -> x0, blocking collectives: 37 us -> none  [body(): every_best = lax.pmax(tgt_peak.reshape(-1), ('src', 'tgt'))]
    unnamed x1 -> x0, blocking collectives: 23.5 us -> none
    all_gather x2 -> x0, blocking collectives: 19.8 us -> none  [the longest x1 11 us: body(): every_list = lax.all_gather(bwd_idx, 'tgt', axis=0, tiled=True)]
    ppermute x0 -> x18, starting transfers between devices: none -> 19.5 us  [swap(): return lax.ppermute(value, axis, [(i, i ^ mask) for i in range(count)])]
    pallas_call x0 -> x6, Pallas kernels: none -> 16.1 us  [the longest x4 10.7 us: body(): pl.pallas_call(functools.partial(score_kernel, slot, finish, halves), out...]
    ppermute x0 -> x18, waiting for transfers between devices: none -> 12.3 us  [swap(): return lax.ppermute(value, axis, [(i, i ^ mask) for i in range(count)])]
  transfers between devices with their start and end apart: 1 -> 18, of which waited for: 1 -> 11; matrix products, arithmetic and copies ran while one was open for 1% -> 3% of each run, Pallas kernels for 0% -> 20%
where the time goes in v1:
time: 57 us; the launch traced here: 56.8 us
  starting transfers between devices  19.5 us (34%)
  Pallas kernels  16.1 us (28%)
  waiting for transfers between devices  12.3 us (22%)
  local copies, waits for them, and re-layouts  6.86 us (12%)
  other arithmetic  1.2 us (2%)
  between operations  0.79 us (1%)
    ppermute x18, starting transfers between devices, swap(): return lax.ppermute(value, axis, [(i, i ^ mask) for i in range(count)])  19.5 us
    ppermute x18, waiting for transfers between devices, swap(): return lax.ppermute(value, axis, [(i, i ^ mask) for i in range(count)])  12.3 us
    pallas_call x4, Pallas kernels, body(): pl.pallas_call(functools.partial(score_kernel, slot, finish, halves), out...  10.7 us
    unnamed x14, local copies, waits for them, and re-layouts  5.77 us
    pallas_call x1, Pallas kernels, body(): pl.pallas_call(functools.partial(prepare_kernel, slots), out_shape=(jax.S...  3.19 us
    pallas_call x1, Pallas kernels, body(): pl.pallas_call(functools.partial(margin_kernel, slots, columns), out_shap...  2.29 us
    reshape x2, other arithmetic, body(): return (src_best.reshape(-1), tgt_best.reshape(-1))  1.15 us
  transfers between devices with their start and end apart: 18, of which 11 were waited for; matrix products, arithmetic and copies ran while one was open for 3% of the time, Pallas kernels for 20%

profile of v1, /device:TPU:0, one launch (start us, length us, event | category | flops | bytes accessed | tf_op | source)
XLA Modules:
  0.0 56.8 jit_solution(4632448936148998258)
XLA Ops:
  1.2 1.1 %fusion = (bf16[128,1024]{1,0:T(8,128)(2,1)S(1)}, bf16[128,1024]{1,0:T(8,128)(2,1)S(1)}) fusion(bf16[256,1024]{1,0:T(8,128)(2,1)} %refs_0_.1), kind=kLoop, calls=%fused_computation.7 | loop fusion | bytes 1048576 | tf_op jit(solution)/shard_map/slice | solution.py:206
  2.2 2.6 %collective-permute-start.5 = (bf16[128,1024]{1,0:T(8,128)(2,1)S(1)}, bf16[128,1024]{1,0:T(8,128)(2,1)S(1)}, u32[]{:S(2)}, u32[]{:S(2)}) collective-permute-start(bf16[128,1024]{1,0:T(8,128)(2,1)S(1)} %get-tuple-element.38), channel_id=1, source_target_pairs={{0,4},{1,5},{2,6},{3,7},{4,0},{5,1},{6,2},{7,3},{8,12},{9,13},{10,... | collective-permute-start | bytes 786440 | tf_op jit(solution)/shard_map/ppermute | solution.py:189
  4.9 1.5 %collective-permute-start.2 = (bf16[128,1024]{1,0:T(8,128)(2,1)S(1)}, bf16[128,1024]{1,0:T(8,128)(2,1)S(1)}, u32[]{:S(2)}, u32[]{:S(2)}) collective-permute-start(bf16[128,1024]{1,0:T(8,128)(2,1)S(1)} %get-tuple-element.39), channel_id=1, source_target_pairs={{0,2},{1,3},{2,0},{3,1},{4,6},{5,7},{6,4},{7,5},{8,10},{9,11},{10,... | collective-permute-start | bytes 786440 | tf_op jit(solution)/shard_map/ppermute | solution.py:189
  6.9 1.4 %collective-permute-done.1.bwd_sibling_ref = s32[16,512]{1,0:T(8,128)S(1)} collective-permute-done((s32[16,512]{1,0:T(8,128)}, s32[16,512]{1,0:T(8,128)S(1)}, u32[]{:S(2)}, u32[]{:S(2)}) %collective-permute-start.1) | collective-permute-done | bytes 32800 | tf_op jit(solution)/shard_map/ppermute | solution.py:189
  8.4 3.6 %collective-permute-done.5.refs_1_ = bf16[128,1024]{1,0:T(8,128)(2,1)S(1)} collective-permute-done((bf16[128,1024]{1,0:T(8,128)(2,1)S(1)}, bf16[128,1024]{1,0:T(8,128)(2,1)S(1)}, u32[]{:S(2)}, u32[]{:S(2)}) %collective-permute-start.5) | collective-permute-done | bytes 262176 | tf_op jit(solution)/shard_map/ppermute | solution.py:189
  12.0 1.9 %collective-permute-start.7 = (bf16[128,1024]{1,0:T(8,128)(2,1)S(1)}, bf16[128,1024]{1,0:T(8,128)(2,1)S(1)}, u32[]{:S(2)}, u32[]{:S(2)}) collective-permute-start(bf16[128,1024]{1,0:T(8,128)(2,1)S(1)} %collective-permute-done.5.refs_1_), channel_id=1, source_target_pairs={{0,2},{1,3},{2,0},{3,1},{4,6},{5,7},{6,4},{7,5},{8,10},{9,11},{10,... | collective-permute-start | bytes 786440 | tf_op jit(solution)/shard_map/ppermute | solution.py:189
  14.0 1.5 %collective-permute-start.6 = (bf16[128,1024]{1,0:T(8,128)(2,1)S(1)}, bf16[128,1024]{1,0:T(8,128)(2,1)S(1)}, u32[]{:S(2)}, u32[]{:S(2)}) collective-permute-start(bf16[128,1024]{1,0:T(8,128)(2,1)S(1)} %collective-permute-done.2.refs_0_), channel_id=1, source_target_pairs={{0,4},{1,5},{2,6},{3,7},{4,0},{5,1},{6,2},{7,3},{8,12},{9,13},{10,... | collective-permute-start | bytes 786440 | tf_op jit(solution)/shard_map/ppermute | solution.py:189
  15.5 1.2 %copy-done.2 = bf16[512,1024]{1,0:T(8,128)(2,1)S(1)} copy-done((bf16[512,1024]{1,0:T(8,128)(2,1)S(1)}, bf16[512,1024]{1,0:T(8,128)(2,1)}, u32[]{:S(2)}) %copy-start.2) | copy-done | bytes 1048600
  16.7 0.9 %copy-done.4 = s32[2048,16]{0,1:T(8,128)S(1)} copy-done((s32[2048,16]{0,1:T(8,128)S(1)}, s32[2048,16]{0,1:T(8,128)}, u32[]{:S(2)}) %copy-start.4) | copy-done | bytes 131096
  19.1 3.2 %prepare.1 = (bf16[1024,1024]{1,0:T(8,128)(2,1)S(1)}, s32[1,128,128]{2,1,0:T(8,128)S(1)}, s32[1,128,128]{2,1,0:T(8,128)S(1)}, s32[16]{0:T(128)S(1)}) custom-call(bf16[512,1024]{1,0:T(8,128)(2,1)S(1)} %copy-done.2, bf16[512,1024]{1,0:T(8,128)(2,1)S(1)} %collective-permute-done.sibling_ref, s32[8,8]{1,0:T(8,128)S(1)} %copy-done.6, s32[16,2048]{1,0:T(8,128)S(1)} %bitcast.10, ...), custom_call_target="tpu_custom_call" | custom-call | flops 6291456 | bytes 4194304 | tf_op jit(solution)/shard_map/prepare/pallas_call | solution.py:222
  22.3 2.7 %score_0.1 = (f32[256,1024]{1,0:T(8,128)S(1)}, f32[2,128]{1,0:T(2,128)S(1)}, f32[8,128]{1,0:T(8,128)S(1)}) custom-call(bf16[256,1024]{1,0:T(8,128)(2,1)S(1)} %copy-done.3, bf16[1024,1024]{1,0:T(8,128)(2,1)S(1)} %get-tuple-element.20.refs_1_.refs_2_, s32[1,128,128]{2,1,0:T(8,128)S(1)} %get-tuple-element.21.refs_2_.refs_3_, ...), custom_call_target="tpu_custom_call" | custom-call | flops 1073741824 | bytes 1048576 | tf_op jit(solution)/shard_map/score_0/pallas_call | solution.py:243
  24.9 2.7 %score_2.1 = (f32[256,1024]{1,0:T(8,128)S(1)}, f32[2,128]{1,0:T(2,128)S(1)}, f32[8,128]{1,0:T(8,128)S(1)}) custom-call(bf16[128,1024]{1,0:T(8,128)(2,1)S(1)} %collective-permute-done.4.refs_0_, bf16[128,1024]{1,0:T(8,128)(2,1)S(1)} %collective-permute-done.5.refs_1_, bf16[1024,1024]{1,0:T(8,128)(2,1)S(1)} %get-tuple-element.20.refs_1_.refs_2_, ...), custom_call_target="tpu_custom_call" | custom-call | flops 1073741824 | bytes 1048576 | tf_op jit(solution)/shard_map/score_2/pallas_call | solution.py:243
  27.6 2.7 %score_1.1 = (f32[256,1024]{1,0:T(8,128)S(1)}, f32[2,128]{1,0:T(2,128)S(1)}, f32[8,128]{1,0:T(8,128)S(1)}) custom-call(bf16[128,1024]{1,0:T(8,128)(2,1)S(1)} %collective-permute-done.2.refs_0_, bf16[128,1024]{1,0:T(8,128)(2,1)S(1)} %collective-permute-done.3.refs_1_, bf16[1024,1024]{1,0:T(8,128)(2,1)S(1)} %get-tuple-element.20.refs_1_.refs_2_, ...), custom_call_target="tpu_custom_call" | custom-call | flops 1073741824 | bytes 1048576 | tf_op jit(solution)/shard_map/score_1/pallas_call | solution.py:243
  30.4 2.7 %score_3.1 = (f32[256,1024]{1,0:T(8,128)S(1)}, f32[8,128]{1,0:T(8,128)S(1)}, f32[8,128]{1,0:T(8,128)S(1)}) custom-call(bf16[128,1024]{1,0:T(8,128)(2,1)S(1)} %collective-permute-done.6.refs_0_, bf16[128,1024]{1,0:T(8,128)(2,1)S(1)} %collective-permute-done.7.refs_1_, bf16[1024,1024]{1,0:T(8,128)(2,1)S(1)} %get-tuple-element.20.refs_1_.refs_2_, ...), custom_call_target="tpu_custom_call" | custom-call | flops 1073741824 | bytes 1048576 | tf_op jit(solution)/shard_map/score_3/pallas_call | solution.py:243
  33.0 1.0 %copy-done = f32[256,1024]{1,0:T(8,128)} copy-done((f32[256,1024]{1,0:T(8,128)}, f32[256,1024]{1,0:T(8,128)S(1)}, u32[]{:S(2)}) %copy-start) | copy-done | bytes 1048600
  35.2 1.6 %collective-permute-start.11 = (f32[8,128]{1,0:T(8,128)S(1)}, f32[8,128]{1,0:T(8,128)S(1)}, u32[]{:S(2)}, u32[]{:S(2)}) collective-permute-start(f32[8,128]{1,0:T(8,128)S(1)} %maximum_add_fusion), channel_id=1, source_target_pairs={{0,8},{8,0},{16,24},{24,16},{1,9},{9,1},{17,25},{25,17},{2,10},{10... | collective-permute-start | bytes 12296 | tf_op jit(solution)/shard_map/ppermute | solution.py:189
  38.9 2.6 %collective-permute-start.12 = (f32[8,128]{1,0:T(8,128)S(1)}, f32[8,128]{1,0:T(8,128)S(1)}, u32[]{:S(2)}, u32[]{:S(2)}) collective-permute-start(f32[8,128]{1,0:T(8,128)S(1)} %add.26), channel_id=1, source_target_pairs={{0,16},{8,24},{16,0},{24,8},{1,17},{9,25},{17,1},{25,9},{2,18},{10... | collective-permute-start | bytes 12296 | tf_op jit(solution)/shard_map/ppermute | solution.py:189
  41.5 1.9 %collective-permute-done.12 = f32[8,128]{1,0:T(8,128)S(1)} collective-permute-done((f32[8,128]{1,0:T(8,128)S(1)}, f32[8,128]{1,0:T(8,128)S(1)}, u32[]{:S(2)}, u32[]{:S(2)}) %collective-permute-start.12) | collective-permute-done | bytes 4128 | tf_op jit(solution)/shard_map/ppermute | solution.py:189
  43.4 1.2 %copy-done.1 = f32[256,1024]{1,0:T(8,128)S(1)} copy-done((f32[256,1024]{1,0:T(8,128)S(1)}, f32[256,1024]{1,0:T(8,128)}, u32[]{:S(2)}) %copy-start.1) | copy-done | bytes 1048600
  44.6 2.3 %margins.1 = (f32[8,128]{1,0:T(8,128)S(1)}, f32[8,128]{1,0:T(8,128)S(1)}) custom-call(f32[256,1024]{1,0:T(8,128)S(1)} %get-tuple-element.23.refs_0_, f32[256,1024]{1,0:T(8,128)S(1)} %get-tuple-element.24.refs_1_, f32[256,1024]{1,0:T(8,128)S(1)} %get-tuple-element.25.refs_2_, f32[256,1024]{1,0:T(8,128)S(1)} %copy-done.1, f32[8,128]{1,0:T(8,128)S(1)} %add.24.refs_4_, ...), custom_call_target="tpu_custom_call" | custom-call | flops 10485760 | bytes 4194304 | tf_op jit(solution)/shard_map/margins/pallas_call | solution.py:274
  48.1 1.7 %collective-permute-start.16 = (f32[4,128]{1,0:T(4,128)S(1)}, f32[4,128]{1,0:T(4,128)S(1)}, u32[]{:S(2)}, u32[]{:S(2)}) collective-permute-start(f32[4,128]{1,0:T(4,128)S(1)} %slice_maximum_fusion), channel_id=1, source_target_pairs={{0,8},{8,0},{16,24},{24,16},{1,9},{9,1},{17,25},{25,17},{2,10},{10... | collective-permute-start | bytes 6152 | tf_op jit(solution)/shard_map/ppermute | solution.py:189
  49.8 0.8 %collective-permute-done.13 = f32[4,128]{1,0:T(4,128)S(1)} collective-permute-done((f32[4,128]{1,0:T(4,128)S(1)}, f32[4,128]{1,0:T(4,128)S(1)}, u32[]{:S(2)}, u32[]{:S(2)}) %collective-permute-start.13) | collective-permute-done | bytes 2080 | tf_op jit(solution)/shard_map/ppermute | solution.py:189
  51.7 2.6 %collective-permute-start.17 = (f32[4,128]{1,0:T(4,128)S(1)}, f32[4,128]{1,0:T(4,128)S(1)}, u32[]{:S(2)}, u32[]{:S(2)}) collective-permute-start(f32[4,128]{1,0:T(4,128)S(1)} %max.18), channel_id=1, source_target_pairs={{0,16},{8,24},{16,0},{24,8},{1,17},{9,25},{17,1},{25,9},{2,18},{10... | collective-permute-start | bytes 6152 | tf_op jit(solution)/shard_map/ppermute | solution.py:189
  54.9 1.3 %collective-permute-done.17 = f32[4,128]{1,0:T(4,128)S(1)} collective-permute-done((f32[4,128]{1,0:T(4,128)S(1)}, f32[4,128]{1,0:T(4,128)S(1)}, u32[]{:S(2)}, u32[]{:S(2)}) %collective-permute-start.17) | collective-permute-done | bytes 2080 | tf_op jit(solution)/shard_map/ppermute | solution.py:189
  (51 shorter events, 9.3 us)
Async XLA Ops:
  0.6 21.6 %copy-start.3 = (bf16[256,1024]{1,0:T(8,128)(2,1)S(1)}, bf16[256,1024]{1,0:T(8,128)(2,1)}, u32[]{:S(2)}) copy-start(bf16[256,1024]{1,0:T(8,128)(2,1)} %refs_0_.1) | copy-start | bytes 1572868
  0.6 14.8 %collective-permute-start = (bf16[512,1024]{1,0:T(8,128)(2,1)}, bf16[512,1024]{1,0:T(8,128)(2,1)S(1)}, u32[]{:S(2)}, u32[]{:S(2)}) collective-permute-start(bf16[512,1024]{1,0:T(8,128)(2,1)} %own_ref.1), channel_id=1, source_target_pairs={{0,1},{1,0},{2,3},{3,2},{4,5},{5,4},{6,7},{7,6},{8,9},{9,8},{10,11... | collective-permute-start | bytes 3145736 | tf_op jit(solution)/shard_map/ppermute | solution.py:189
  2.2 9.8 %collective-permute-start.5 = (bf16[128,1024]{1,0:T(8,128)(2,1)S(1)}, bf16[128,1024]{1,0:T(8,128)(2,1)S(1)}, u32[]{:S(2)}, u32[]{:S(2)}) collective-permute-start(bf16[128,1024]{1,0:T(8,128)(2,1)S(1)} %get-tuple-element.38), channel_id=1, source_target_pairs={{0,4},{1,5},{2,6},{3,7},{4,0},{5,1},{6,2},{7,3},{8,12},{9,13},{10,... | collective-permute-start | bytes 786440 | tf_op jit(solution)/shard_map/ppermute | solution.py:189
  4.9 9.2 %collective-permute-start.2 = (bf16[128,1024]{1,0:T(8,128)(2,1)S(1)}, bf16[128,1024]{1,0:T(8,128)(2,1)S(1)}, u32[]{:S(2)}, u32[]{:S(2)}) collective-permute-start(bf16[128,1024]{1,0:T(8,128)(2,1)S(1)} %get-tuple-element.39), channel_id=1, source_target_pairs={{0,2},{1,3},{2,0},{3,1},{4,6},{5,7},{6,4},{7,5},{8,10},{9,11},{10,... | collective-permute-start | bytes 786440 | tf_op jit(solution)/shard_map/ppermute | solution.py:189
  6.4 18.6 %collective-permute-start.4 = (bf16[128,1024]{1,0:T(8,128)(2,1)S(1)}, bf16[128,1024]{1,0:T(8,128)(2,1)S(1)}, u32[]{:S(2)}, u32[]{:S(2)}) collective-permute-start(bf16[128,1024]{1,0:T(8,128)(2,1)S(1)} %get-tuple-element.39), channel_id=1, source_target_pairs={{0,4},{1,5},{2,6},{3,7},{4,0},{5,1},{6,2},{7,3},{8,12},{9,13},{10,... | collective-permute-start | bytes 786440 | tf_op jit(solution)/shard_map/ppermute | solution.py:189
  6.9 1.4 %collective-permute-start.1 = (s32[16,512]{1,0:T(8,128)}, s32[16,512]{1,0:T(8,128)S(1)}, u32[]{:S(2)}, u32[]{:S(2)}) collective-permute-start(s32[16,512]{1,0:T(8,128)} %bitcast.11), channel_id=1, source_target_pairs={{0,1},{1,0},{2,3},{3,2},{4,5},{5,4},{6,7},{7,6},{8,9},{9,8},{10,11... | collective-permute-start | bytes 98312 | tf_op jit(solution)/shard_map/ppermute | solution.py:189
  8.3 19.3 %collective-permute-start.3 = (bf16[128,1024]{1,0:T(8,128)(2,1)S(1)}, bf16[128,1024]{1,0:T(8,128)(2,1)S(1)}, u32[]{:S(2)}, u32[]{:S(2)}) collective-permute-start(bf16[128,1024]{1,0:T(8,128)(2,1)S(1)} %get-tuple-element.38), channel_id=1, source_target_pairs={{0,2},{1,3},{2,0},{3,1},{4,6},{5,7},{6,4},{7,5},{8,10},{9,11},{10,... | collective-permute-start | bytes 786440 | tf_op jit(solution)/shard_map/ppermute | solution.py:189
  12.0 18.3 %collective-permute-start.7 = (bf16[128,1024]{1,0:T(8,128)(2,1)S(1)}, bf16[128,1024]{1,0:T(8,128)(2,1)S(1)}, u32[]{:S(2)}, u32[]{:S(2)}) collective-permute-start(bf16[128,1024]{1,0:T(8,128)(2,1)S(1)} %collective-permute-done.5.refs_1_), channel_id=1, source_target_pairs={{0,2},{1,3},{2,0},{3,1},{4,6},{5,7},{6,4},{7,5},{8,10},{9,11},{10,... | collective-permute-start | bytes 786440 | tf_op jit(solution)/shard_map/ppermute | solution.py:189
  14.0 16.3 %collective-permute-start.6 = (bf16[128,1024]{1,0:T(8,128)(2,1)S(1)}, bf16[128,1024]{1,0:T(8,128)(2,1)S(1)}, u32[]{:S(2)}, u32[]{:S(2)}) collective-permute-start(bf16[128,1024]{1,0:T(8,128)(2,1)S(1)} %collective-permute-done.2.refs_0_), channel_id=1, source_target_pairs={{0,4},{1,5},{2,6},{3,7},{4,0},{5,1},{6,2},{7,3},{8,12},{9,13},{10,... | collective-permute-start | bytes 786440 | tf_op jit(solution)/shard_map/ppermute | solution.py:189
  15.5 1.2 %copy-start.2 = (bf16[512,1024]{1,0:T(8,128)(2,1)S(1)}, bf16[512,1024]{1,0:T(8,128)(2,1)}, u32[]{:S(2)}) copy-start(bf16[512,1024]{1,0:T(8,128)(2,1)} %own_ref.1) | copy-start | bytes 3145732
  16.7 0.9 %copy-start.4 = (s32[2048,16]{0,1:T(8,128)S(1)}, s32[2048,16]{0,1:T(8,128)}, u32[]{:S(2)}) copy-start(s32[2048,16]{0,1:T(8,128)} %param.8) | copy-start | bytes 393220
  17.6 0.8 %copy-start.5 = (s32[512,16]{0,1:T(8,128)S(1)}, s32[512,16]{0,1:T(8,128)}, u32[]{:S(2)}) copy-start(s32[512,16]{0,1:T(8,128)} %param.9) | copy-start | bytes 98308
  33.0 1.0 %copy-start = (f32[256,1024]{1,0:T(8,128)}, f32[256,1024]{1,0:T(8,128)S(1)}, u32[]{:S(2)}) copy-start(f32[256,1024]{1,0:T(8,128)S(1)} %get-tuple-element.32.refs_3_) | copy-start | bytes 3145732
  34.0 1.2 %collective-permute-start.10 = (f32[8,128]{1,0:T(8,128)S(1)}, f32[8,128]{1,0:T(8,128)S(1)}, u32[]{:S(2)}, u32[]{:S(2)}) collective-permute-start(f32[8,128]{1,0:T(8,128)S(1)} %get-tuple-element.34), channel_id=1, source_target_pairs={{0,1},{1,0},{2,3},{3,2},{4,5},{5,4},{6,7},{7,6},{8,9},{9,8},{10,11... | collective-permute-start | bytes 12296 | tf_op jit(solution)/shard_map/ppermute | solution.py:189
  34.0 3.6 %collective-permute-start.8 = (f32[8,128]{1,0:T(8,128)S(1)}, f32[8,128]{1,0:T(8,128)S(1)}, u32[]{:S(2)}, u32[]{:S(2)}) collective-permute-start(f32[8,128]{1,0:T(8,128)S(1)} %get-tuple-element.33), channel_id=1, source_target_pairs={{0,2},{1,3},{2,0},{3,1},{4,6},{5,7},{6,4},{7,5},{8,10},{9,11},{10,... | collective-permute-start | bytes 12296 | tf_op jit(solution)/shard_map/ppermute | solution.py:189
  35.2 3.7 %collective-permute-start.11 = (f32[8,128]{1,0:T(8,128)S(1)}, f32[8,128]{1,0:T(8,128)S(1)}, u32[]{:S(2)}, u32[]{:S(2)}) collective-permute-start(f32[8,128]{1,0:T(8,128)S(1)} %maximum_add_fusion), channel_id=1, source_target_pairs={{0,8},{8,0},{16,24},{24,16},{1,9},{9,1},{17,25},{25,17},{2,10},{10... | collective-permute-start | bytes 12296 | tf_op jit(solution)/shard_map/ppermute | solution.py:189
  37.6 3.8 %collective-permute-start.9 = (f32[8,128]{1,0:T(8,128)S(1)}, f32[8,128]{1,0:T(8,128)S(1)}, u32[]{:S(2)}, u32[]{:S(2)}) collective-permute-start(f32[8,128]{1,0:T(8,128)S(1)} %add.23), channel_id=1, source_target_pairs={{0,4},{1,5},{2,6},{3,7},{4,0},{5,1},{6,2},{7,3},{8,12},{9,13},{10,... | collective-permute-start | bytes 12296 | tf_op jit(solution)/shard_map/ppermute | solution.py:189
  38.9 4.5 %collective-permute-start.12 = (f32[8,128]{1,0:T(8,128)S(1)}, f32[8,128]{1,0:T(8,128)S(1)}, u32[]{:S(2)}, u32[]{:S(2)}) collective-permute-start(f32[8,128]{1,0:T(8,128)S(1)} %add.26), channel_id=1, source_target_pairs={{0,16},{8,24},{16,0},{24,8},{1,17},{9,25},{17,1},{25,9},{2,18},{10... | collective-permute-start | bytes 12296 | tf_op jit(solution)/shard_map/ppermute | solution.py:189
  43.4 1.2 %copy-start.1 = (f32[256,1024]{1,0:T(8,128)S(1)}, f32[256,1024]{1,0:T(8,128)}, u32[]{:S(2)}) copy-start(f32[256,1024]{1,0:T(8,128)} %copy-done) | copy-start | bytes 3145732
  46.9 1.2 %collective-permute-start.15 = (f32[4,128]{1,0:T(4,128)S(1)}, f32[4,128]{1,0:T(4,128)S(1)}, u32[]{:S(2)}, u32[]{:S(2)}) collective-permute-start(f32[4,128]{1,0:T(4,128)S(1)} %slice.39), channel_id=1, source_target_pairs={{0,1},{1,0},{2,3},{3,2},{4,5},{5,4},{6,7},{7,6},{8,9},{9,8},{10,11... | collective-permute-start | bytes 6152 | tf_op jit(solution)/shard_map/ppermute | solution.py:189
  47.0 3.7 %collective-permute-start.13 = (f32[4,128]{1,0:T(4,128)S(1)}, f32[4,128]{1,0:T(4,128)S(1)}, u32[]{:S(2)}, u32[]{:S(2)}) collective-permute-start(f32[4,128]{1,0:T(4,128)S(1)} %slice.35), channel_id=1, source_target_pairs={{0,4},{1,5},{2,6},{3,7},{4,0},{5,1},{6,2},{7,3},{8,12},{9,13},{10,... | collective-permute-start | bytes 6152 | tf_op jit(solution)/shard_map/ppermute | solution.py:189
  48.1 3.6 %collective-permute-start.16 = (f32[4,128]{1,0:T(4,128)S(1)}, f32[4,128]{1,0:T(4,128)S(1)}, u32[]{:S(2)}, u32[]{:S(2)}) collective-permute-start(f32[4,128]{1,0:T(4,128)S(1)} %slice_maximum_fusion), channel_id=1, source_target_pairs={{0,8},{8,0},{16,24},{24,16},{1,9},{9,1},{17,25},{25,17},{2,10},{10... | collective-permute-start | bytes 6152 | tf_op jit(solution)/shard_map/ppermute | solution.py:189
  50.7 3.7 %collective-permute-start.14 = (f32[2,128]{1,0:T(2,128)S(1)}, f32[2,128]{1,0:T(2,128)S(1)}, u32[]{:S(2)}, u32[]{:S(2)}) collective-permute-start(f32[2,128]{1,0:T(2,128)S(1)} %slice.37), channel_id=1, source_target_pairs={{0,2},{1,3},{2,0},{3,1},{4,6},{5,7},{6,4},{7,5},{8,10},{9,11},{10,... | collective-permute-start | bytes 3080 | tf_op jit(solution)/shard_map/ppermute | solution.py:189
  51.7 4.5 %collective-permute-start.17 = (f32[4,128]{1,0:T(4,128)S(1)}, f32[4,128]{1,0:T(4,128)S(1)}, u32[]{:S(2)}, u32[]{:S(2)}) collective-permute-start(f32[4,128]{1,0:T(4,128)S(1)} %max.18), channel_id=1, source_target_pairs={{0,16},{8,24},{16,0},{24,8},{1,17},{9,25},{17,1},{25,9},{2,18},{10... | collective-permute-start | bytes 6152 | tf_op jit(solution)/shard_map/ppermute | solution.py:189
  (1 other events, 0.7 us)

commit v2 on v1

--- a/solution.py
+++ b/solution.py
@@ -23,30 +23,27 @@
 
 def params(flops, bytes_accessed, **more):
     return dict(
-        compiler_params=pltpu.CompilerParams(vmem_limit_bytes=32 * 2**20, **more),
+        compiler_params=pltpu.CompilerParams(vmem_limit_bytes=16 * 2**20, **more),
         cost_estimate=pl.CostEstimate(flops=flops, bytes_accessed=bytes_accessed, transcendentals=0),
     )
 
 
-def prepare_kernel(
-    slots, own_ref, sibling_ref, pairs_ref, fwd_ref, bwd_own_ref, bwd_sibling_ref, unit_ref, fwd_at_ref, bwd_at_ref, listed_ref
-):
+def normalise_kernel(own_ref, sibling_ref, unit_ref):
+    rows = own_ref.shape[0]
+    for i, ref in enumerate((own_ref, sibling_ref)):
+
+        def step(j, _, i=i, ref=ref):
+            at = pl.multiple_of(j * 64, 64)
+            unit_ref[pl.ds(i * rows + at, 64), :] = unit_rows(ref[pl.ds(at, 64), :])
+            return 0
+
+        lax.fori_loop(0, rows // 64, step, 0)
+
+
+def lists_kernel(slots, rows, pairs_ref, fwd_ref, bwd_own_ref, bwd_sibling_ref, fwd_at_ref, bwd_at_ref, listed_ref):
     src_pos = lax.axis_index("src")
     tgt_pos = lax.axis_index("tgt")
     tgt_count = lax.axis_size("tgt")
-    rows = own_ref.shape[0]
-
-    def normalise(ref, base):
-        def step(i, _):
-            at = pl.multiple_of(i * 64, 64)
-            unit_ref[pl.ds(base + at, 64), :] = unit_rows(ref[pl.ds(at, 64), :])
-            return 0
-
-        lax.fori_loop(0, rows // 64, step, 0)
-
-    normalise(own_ref, 0)
-    normalise(sibling_ref, rows)
-
     for group in range(fwd_at_ref.shape[0]):
         parts = []
         for g in range(8):
@@ -84,14 +81,12 @@
             listed_ref[slot * blocks + p] = hit
 
 
-def score_kernel(slot, finish, halves, *refs):
-    chunk_refs = refs[:halves]
-    unit_ref, fwd_at_ref, bwd_at_ref = refs[halves : halves + 3]
-    if finish:
-        fwd_before, bwd_before = refs[halves + 3 : halves + 5]
-        scores_ref, fwd_ref, bwd_ref, turned_ref, fwd_got, bwd_got = refs[halves + 5 :]
-    else:
-        scores_ref, fwd_ref, bwd_ref, turned_ref, fwd_got, bwd_got = refs[halves + 3 :]
+def score_kernel(slot, earlier, halves, *refs):
+    chunk_refs, refs = refs[:halves], refs[halves:]
+    unit_ref, fwd_at_ref, bwd_at_ref, *refs = refs
+    fwd_before, refs = refs[:earlier], refs[earlier:]
+    bwd_before, refs = refs[:earlier], refs[earlier:]
+    scores_ref, fwd_ref, bwd_ref, turned_ref, fwd_got, bwd_got = refs
     unit = jnp.concatenate([unit_rows(ref[...]) for ref in chunk_refs], axis=0)
     scores_ref[...] = lax.dot_general(unit, unit_ref[...], ROWS_CONTRACT, preferred_element_type=jnp.float32)
     turned_ref[...] = lax.dot_general(unit_ref[...], unit, ROWS_CONTRACT, preferred_element_type=jnp.float32)
@@ -126,14 +121,12 @@
     fwd = fwd_got[...].T[first : first + 32].reshape(2, 16, LANES).sum(axis=1)
     bwd = [bwd_got[group].T.reshape(8, 16, LANES).sum(axis=1) for group in range(bwd_at_ref.shape[0])]
     bwd = bwd[0] if len(bwd) == 1 else jnp.concatenate(bwd, axis=0)
-    if finish:
-        before = fwd_before.shape[0]
-        fwd_ref[:before, :] = fwd_before[...]
-        fwd_ref[before:, :] = fwd
-        bwd_ref[...] = bwd + bwd_before[...]
-    else:
-        fwd_ref[...] = fwd
-        bwd_ref[...] = bwd
+    for i, ref in enumerate(fwd_before):
+        fwd_ref[2 * i : 2 * i + 2, :] = ref[...]
+    for ref in bwd_before:
+        bwd = bwd + ref[...]
+    fwd_ref[2 * earlier :, :] = fwd
+    bwd_ref[...] = bwd
 
 
 def margin_kernel(slots, columns, *refs):
@@ -203,48 +196,42 @@
     tgt_bits = [1 << b for b in range(1, tgt_count.bit_length() - 1)]
     src_bits = [1 << b for b in range(src_count.bit_length() - 1)]
 
-    upper, lower = src_emb[: BLOCK // 2], src_emb[BLOCK // 2 :]
-    x_upper = swap(upper, "tgt", 2)
-    y_lower = swap(lower, "tgt", 4)
-    x_lower = swap(lower, "tgt", 2)
-    y_upper = swap(upper, "tgt", 4)
-    far_upper = swap(x_upper, "tgt", 4)
-    far_lower = swap(y_lower, "tgt", 2)
-    chunks = [(src_emb,), (x_upper, x_lower), (y_upper, y_lower), (far_upper, far_lower)]
-    for bit in tgt_bits[2:]:
-        chunks += [tuple(swap(part, "tgt", bit) for part in held) for held in chunks]
+    along_x = swap(src_emb, "tgt", 2)
+    along_y = swap(src_emb, "tgt", 4)
 
     sibling_emb = swap(tgt_emb, "tgt", 1)
     bwd_lists = bwd_idx.T
     sibling_lists = swap(bwd_lists, "tgt", 1)
-    lists = jax.ShapeDtypeStruct((-(-slots // 4), LANES, LANES), jnp.int32)
+
+    unit = pl.pallas_call(
+        normalise_kernel,
+        out_shape=jax.ShapeDtypeStruct((columns, width), jnp.bfloat16),
+        in_specs=[VMEM, VMEM],
+        out_specs=VMEM,
+        name="normalise",
+        **params(1000, 1000),
+    )(tgt_emb, sibling_emb)
     bwd_shape = jax.ShapeDtypeStruct((columns // (8 * LANES), LANES, LANES), jnp.int32)
-    unit, fwd_at, bwd_at, listed = pl.pallas_call(
-        functools.partial(prepare_kernel, slots),
+    fwd_at, bwd_at, listed = pl.pallas_call(
+        functools.partial(lists_kernel, slots, rows),
         out_shape=(
-            jax.ShapeDtypeStruct((columns, width), jnp.bfloat16),
-            lists,
+            jax.ShapeDtypeStruct((-(-slots // 4), LANES, LANES), jnp.int32),
             bwd_shape,
             jax.ShapeDtypeStruct((slots * columns // BLOCK,), jnp.int32),
         ),
-        in_specs=[VMEM, VMEM, SMEM, VMEM, VMEM, VMEM],
-        out_specs=(VMEM, VMEM, VMEM, SMEM),
-        name="prepare",
-        **params(columns * width * 6, columns * width * 4),
-    )(tgt_emb, sibling_emb, pair_list, fwd_idx.T, bwd_lists, sibling_lists)
-
-    scores, fwd_parts, bwd_parts = [], [], []
-    for slot in range(slots):
-        finish = slot == slots - 1
-        halves = len(chunks[slot])
-        args = [*chunks[slot], unit, fwd_at, bwd_at]
-        if finish:
-            args += [jnp.concatenate(fwd_parts, axis=0), sum(bwd_parts[1:], bwd_parts[0])]
-        score, fwd, bwd = pl.pallas_call(
-            functools.partial(score_kernel, slot, finish, halves),
+        in_specs=[SMEM, VMEM, VMEM, VMEM],
+        out_specs=(VMEM, VMEM, SMEM),
+        name="lists",
+        **params(1000, 1000),
+    )(pair_list, fwd_idx.T, bwd_lists, sibling_lists)
+
+    def score(slot, blocks, before=()):
+        args = [*blocks, unit, fwd_at, bwd_at, *before]
+        return pl.pallas_call(
+            functools.partial(score_kernel, slot, len(before) // 2, len(blocks)),
             out_shape=(
                 jax.ShapeDtypeStruct((BLOCK, columns), jnp.float32),
-                jax.ShapeDtypeStruct((2 * slots if finish else 2, LANES), jnp.float32),
+                jax.ShapeDtypeStruct((len(before) + 2, LANES), jnp.float32),
                 jax.ShapeDtypeStruct((columns // LANES, LANES), jnp.float32),
             ),
             in_specs=[VMEM] * len(args),
@@ -255,12 +242,23 @@
                 pltpu.VMEM(bwd_shape.shape, jnp.float32),
             ],
             name=f"score_{slot}",
-            **params(4 * BLOCK * columns * width, BLOCK * columns * 4),
+            **(params(4 * BLOCK * columns * width, BLOCK * columns * 4) if slot else params(1000, 1000)),
         )(*args)
-        scores.append(score)
-        fwd_parts.append(fwd)
-        bwd_parts.append(bwd)
-
+
+    done = [score(0, (src_emb,))]
+    along_x, along_y, *done[0] = lax.optimization_barrier((along_x, along_y, *done[0]))
+    far_upper = swap(along_x[: BLOCK // 2], "tgt", 4)
+    far_lower = swap(along_y[BLOCK // 2 :], "tgt", 2)
+    blocks = [(src_emb,), (along_x,), (along_y,), (far_upper, far_lower)]
+    for bit in tgt_bits[2:]:
+        blocks += [tuple(swap(part, "tgt", bit) for part in held) for held in blocks]
+    for slot in range(1, slots):
+        before = ()
+        if slot == slots - 1:
+            before = [d[1] for d in done] + [d[2] for d in done]
+        done.append(score(slot, blocks[slot], before))
+    scores = [d[0] for d in done]
+    fwd, bwd = done[-1][1:]
     def turn_pair(value):
         half = value.shape[0] // 2
         return jnp.concatenate([value[half:], value[:half]], axis=0)

time: 57 us -> 53.4 us (0.937)
  waiting for transfers between devices: 12.3 us -> 9.22 us
  local copies, waits for them, and re-layouts: 6.86 us -> 5.84 us
    ppermute x18 -> x16, waiting for transfers between devices: 12.3 us -> 9.22 us  [swap(): return lax.ppermute(value, axis, [(i, i ^ mask) for i in range(count)])]
    slice x1 -> x2, local copies, waits for them, and re-layouts: 1.06 us -> 0.04 us  [the longest x1 0.02 us: body(): far_lower = swap(along_y[BLOCK // 2:], 'tgt', 2)]
    ppermute x18 -> x16, starting transfers between devices: 19.5 us -> 19.8 us  [swap(): return lax.ppermute(value, axis, [(i, i ^ mask) for i in range(count)])]
    pallas_call x5 -> x6, Pallas kernels: 13.9 us -> 13.8 us  [the longest x4 10.6 us: score(): pl.pallas_call(functools.partial(score_kernel, slot, len(before) // 2, le...]
  transfers between devices with their start and end apart: 18 -> 16, of which waited for: 11 -> 10; matrix products, arithmetic and copies ran while one was open for 3% -> 1% of each run, Pallas kernels for 20% -> 21%
where the time goes in v2:
time: 53.4 us; the launch traced here: 53 us
  starting transfers between devices  19.8 us (37%)
  Pallas kernels  16.2 us (30%)
  waiting for transfers between devices  9.22 us (17%)
  local copies, waits for them, and re-layouts  5.84 us (11%)
  other arithmetic  1.19 us (2%)
  between operations  0.77 us (1%)
    ppermute x16, starting transfers between devices, swap(): return lax.ppermute(value, axis, [(i, i ^ mask) for i in range(count)])  19.8 us
    pallas_call x4, Pallas kernels, score(): pl.pallas_call(functools.partial(score_kernel, slot, len(before) // 2, le...  10.6 us
    ppermute x16, waiting for transfers between devices, swap(): return lax.ppermute(value, axis, [(i, i ^ mask) for i in range(count)])  9.22 us
    unnamed x14, local copies, waits for them, and re-layouts  5.78 us
    pallas_call x1, Pallas kernels, body(): pl.pallas_call(functools.partial(margin_kernel, slots, columns), out_shap...  2.4 us
    pallas_call x1, Pallas kernels, body(): pl.pallas_call(normalise_kernel, out_shape=jax.ShapeDtypeStruct((columns,...  1.84 us
    pallas_call x1, Pallas kernels, body(): pl.pallas_call(functools.partial(lists_kernel, slots, rows), out_shape=(j...  1.36 us
    reshape x2, other arithmetic, body(): return (src_best.reshape(-1), tgt_best.reshape(-1))  1.15 us
  transfers between devices with their start and end apart: 16, of which 10 were waited for; matrix products, arithmetic and copies ran while one was open for 1% of the time, Pallas kernels for 21%

profile of v2, /device:TPU:0, one launch (start us, length us, event | category | flops | bytes accessed | tf_op | source)
XLA Modules:
  0.0 53.0 jit_solution(14543463107008623395)
XLA Ops:
  1.1 2.6 %collective-permute-start = (bf16[256,1024]{1,0:T(8,128)(2,1)}, bf16[256,1024]{1,0:T(8,128)(2,1)S(1)}, u32[]{:S(2)}, u32[]{:S(2)}) collective-permute-start(bf16[256,1024]{1,0:T(8,128)(2,1)} %refs_0_.1), channel_id=1, source_target_pairs={{0,2},{1,3},{2,0},{3,1},{4,6},{5,7},{6,4},{7,5},{8,10},{9,11},{10,... | collective-permute-start | bytes 1572872 | tf_op jit(solution)/shard_map/ppermute | solution.py:182
  3.7 1.5 %collective-permute-start.1 = (bf16[256,1024]{1,0:T(8,128)(2,1)}, bf16[256,1024]{1,0:T(8,128)(2,1)S(1)}, u32[]{:S(2)}, u32[]{:S(2)}) collective-permute-start(bf16[256,1024]{1,0:T(8,128)(2,1)} %refs_0_.1), channel_id=1, source_target_pairs={{0,4},{1,5},{2,6},{3,7},{4,0},{5,1},{6,2},{7,3},{8,12},{9,13},{10,... | collective-permute-start | bytes 1572872 | tf_op jit(solution)/shard_map/ppermute | solution.py:182
  5.2 1.4 %collective-permute-done.3.bwd_sibling_ref = s32[16,512]{1,0:T(8,128)S(1)} collective-permute-done((s32[16,512]{1,0:T(8,128)}, s32[16,512]{1,0:T(8,128)S(1)}, u32[]{:S(2)}, u32[]{:S(2)}) %collective-permute-start.3) | collective-permute-done | bytes 32800 | tf_op jit(solution)/shard_map/ppermute | solution.py:182
  9.0 1.4 %lists.1 = (s32[1,128,128]{2,1,0:T(8,128)S(1)}, s32[1,128,128]{2,1,0:T(8,128)S(1)}, s32[16]{0:T(128)S(1)}) custom-call(s32[8,8]{1,0:T(8,128)S(1)} %copy-done.6, s32[16,2048]{1,0:T(8,128)S(1)} %bitcast.10, s32[16,512]{1,0:T(8,128)S(1)} %bitcast.12, s32[16,512]{1,0:T(8,128)S(1)} %collective-permute-done.3.bwd_sibling_ref), custom_call_target="tpu_custom_call" | custom-call | flops 1000 | bytes 1000 | tf_op jit(solution)/shard_map/lists/pallas_call | solution.py:215
  10.4 1.2 %copy-done.2 = bf16[512,1024]{1,0:T(8,128)(2,1)S(1)} copy-done((bf16[512,1024]{1,0:T(8,128)(2,1)S(1)}, bf16[512,1024]{1,0:T(8,128)(2,1)}, u32[]{:S(2)}) %copy-start.2) | copy-done | bytes 1048600
  11.6 1.8 %normalise.1.refs_1_.refs_2_ = bf16[1024,1024]{1,0:T(8,128)(2,1)S(1)} custom-call(bf16[512,1024]{1,0:T(8,128)(2,1)S(1)} %copy-done.2, bf16[512,1024]{1,0:T(8,128)(2,1)S(1)} %collective-permute-done.2.sibling_ref), custom_call_target="tpu_custom_call" | custom-call | flops 1000 | bytes 1000 | tf_op jit(solution)/shard_map/normalise/pallas_call | solution.py:206
  13.5 2.6 %score_0.1 = (f32[256,1024]{1,0:T(8,128)S(1)}, f32[2,128]{1,0:T(2,128)S(1)}, f32[8,128]{1,0:T(8,128)S(1)}) custom-call(bf16[256,1024]{1,0:T(8,128)(2,1)S(1)} %copy-done.3, bf16[1024,1024]{1,0:T(8,128)(2,1)S(1)} %normalise.1.refs_1_.refs_2_, s32[1,128,128]{2,1,0:T(8,128)S(1)} %get-tuple-element.24.refs_2_.refs_3_, ...), custom_call_target="tpu_custom_call" | custom-call | flops 1000 | bytes 1000 | tf_op jit(solution)/shard_map/score_0/pallas_call | solution.py:230
  16.4 1.5 %collective-permute-done.1.refs_0_ = bf16[256,1024]{1,0:T(8,128)(2,1)S(1)} collective-permute-done((bf16[256,1024]{1,0:T(8,128)(2,1)}, bf16[256,1024]{1,0:T(8,128)(2,1)S(1)}, u32[]{:S(2)}, u32[]{:S(2)}) %collective-permute-start.1) | collective-permute-done | bytes 524320 | tf_op jit(solution)/shard_map/ppermute | solution.py:182
  18.4 1.7 %collective-permute-start.4 = (bf16[128,1024]{1,0:T(8,128)(2,1)S(1)}, bf16[128,1024]{1,0:T(8,128)(2,1)S(1)}, u32[]{:S(2)}, u32[]{:S(2)}) collective-permute-start(bf16[128,1024]{1,0:T(8,128)(2,1)S(1)} %slice.30), channel_id=1, source_target_pairs={{0,4},{1,5},{2,6},{3,7},{4,0},{5,1},{6,2},{7,3},{8,12},{9,13},{10,... | collective-permute-start | bytes 786440 | tf_op jit(solution)/shard_map/ppermute | solution.py:182
  20.1 2.6 %score_2.1 = (f32[256,1024]{1,0:T(8,128)S(1)}, f32[2,128]{1,0:T(2,128)S(1)}, f32[8,128]{1,0:T(8,128)S(1)}) custom-call(bf16[256,1024]{1,0:T(8,128)(2,1)S(1)} %collective-permute-done.1.refs_0_, bf16[1024,1024]{1,0:T(8,128)(2,1)S(1)} %normalise.1.refs_1_.refs_2_, s32[1,128,128]{2,1,0:T(8,128)S(1)} %get-tuple-element.24.refs_2_.refs_3_, ...), custom_call_target="tpu_custom_call" | custom-call | flops 1073741824 | bytes 1048576 | tf_op jit(solution)/shard_map/score_2/pallas_call | solution.py:230
  22.7 2.7 %score_1.1 = (f32[256,1024]{1,0:T(8,128)S(1)}, f32[2,128]{1,0:T(2,128)S(1)}, f32[8,128]{1,0:T(8,128)S(1)}) custom-call(bf16[256,1024]{1,0:T(8,128)(2,1)S(1)} %collective-permute-done.refs_0_, bf16[1024,1024]{1,0:T(8,128)(2,1)S(1)} %normalise.1.refs_1_.refs_2_, s32[1,128,128]{2,1,0:T(8,128)S(1)} %get-tuple-element.24.refs_2_.refs_3_, ...), custom_call_target="tpu_custom_call" | custom-call | flops 1073741824 | bytes 1048576 | tf_op jit(solution)/shard_map/score_1/pallas_call | solution.py:230
  25.9 2.7 %score_3.1 = (f32[256,1024]{1,0:T(8,128)S(1)}, f32[8,128]{1,0:T(8,128)S(1)}, f32[8,128]{1,0:T(8,128)S(1)}) custom-call(bf16[128,1024]{1,0:T(8,128)(2,1)S(1)} %collective-permute-done.4.refs_0_, bf16[128,1024]{1,0:T(8,128)(2,1)S(1)} %collective-permute-done.5.refs_1_, bf16[1024,1024]{1,0:T(8,128)(2,1)S(1)} %normalise.1.refs_1_.refs_2_, ...), custom_call_target="tpu_custom_call" | custom-call | flops 1073741824 | bytes 1048576 | tf_op jit(solution)/shard_map/score_3/pallas_call | solution.py:230
  29.6 1.4 %collective-permute-start.6 = (f32[8,128]{1,0:T(8,128)S(1)}, f32[8,128]{1,0:T(8,128)S(1)}, u32[]{:S(2)}, u32[]{:S(2)}) collective-permute-start(f32[8,128]{1,0:T(8,128)S(1)} %get-tuple-element.41), channel_id=1, source_target_pairs={{0,2},{1,3},{2,0},{3,1},{4,6},{5,7},{6,4},{7,5},{8,10},{9,11},{10,... | collective-permute-start | bytes 12296 | tf_op jit(solution)/shard_map/ppermute | solution.py:182
  31.0 1.6 %collective-permute-start.9 = (f32[8,128]{1,0:T(8,128)S(1)}, f32[8,128]{1,0:T(8,128)S(1)}, u32[]{:S(2)}, u32[]{:S(2)}) collective-permute-start(f32[8,128]{1,0:T(8,128)S(1)} %maximum_add_fusion), channel_id=1, source_target_pairs={{0,8},{8,0},{16,24},{24,16},{1,9},{9,1},{17,25},{25,17},{2,10},{10... | collective-permute-start | bytes 12296 | tf_op jit(solution)/shard_map/ppermute | solution.py:182
  33.2 1.5 %collective-permute-start.7 = (f32[8,128]{1,0:T(8,128)S(1)}, f32[8,128]{1,0:T(8,128)S(1)}, u32[]{:S(2)}, u32[]{:S(2)}) collective-permute-start(f32[8,128]{1,0:T(8,128)S(1)} %add.15), channel_id=1, source_target_pairs={{0,4},{1,5},{2,6},{3,7},{4,0},{5,1},{6,2},{7,3},{8,12},{9,13},{10,... | collective-permute-start | bytes 12296 | tf_op jit(solution)/shard_map/ppermute | solution.py:182
  34.7 2.6 %collective-permute-start.10 = (f32[8,128]{1,0:T(8,128)S(1)}, f32[8,128]{1,0:T(8,128)S(1)}, u32[]{:S(2)}, u32[]{:S(2)}) collective-permute-start(f32[8,128]{1,0:T(8,128)S(1)} %add.18), channel_id=1, source_target_pairs={{0,16},{8,24},{16,0},{24,8},{1,17},{9,25},{17,1},{25,9},{2,18},{10... | collective-permute-start | bytes 12296 | tf_op jit(solution)/shard_map/ppermute | solution.py:182
  37.3 1.9 %collective-permute-done.10 = f32[8,128]{1,0:T(8,128)S(1)} collective-permute-done((f32[8,128]{1,0:T(8,128)S(1)}, f32[8,128]{1,0:T(8,128)S(1)}, u32[]{:S(2)}, u32[]{:S(2)}) %collective-permute-start.10) | collective-permute-done | bytes 4128 | tf_op jit(solution)/shard_map/ppermute | solution.py:182
  39.2 1.2 %copy-done.1 = f32[256,1024]{1,0:T(8,128)S(1)} copy-done((f32[256,1024]{1,0:T(8,128)S(1)}, f32[256,1024]{1,0:T(8,128)}, u32[]{:S(2)}) %copy-start.1) | copy-done | bytes 1048600
  40.4 2.4 %margins.1 = (f32[8,128]{1,0:T(8,128)S(1)}, f32[8,128]{1,0:T(8,128)S(1)}) custom-call(f32[256,1024]{1,0:T(8,128)S(1)} %get-tuple-element.29.refs_0_, f32[256,1024]{1,0:T(8,128)S(1)} %get-tuple-element.31.refs_1_, f32[256,1024]{1,0:T(8,128)S(1)} %get-tuple-element.33.refs_2_, f32[256,1024]{1,0:T(8,128)S(1)} %copy-done.1, f32[8,128]{1,0:T(8,128)S(1)} %add.16.refs_4_, ...), custom_call_target="tpu_custom_call" | custom-call | flops 10485760 | bytes 4194304 | tf_op jit(solution)/shard_map/margins/pallas_call | solution.py:272
  43.0 1.3 %collective-permute-start.11 = (f32[4,128]{1,0:T(4,128)S(1)}, f32[4,128]{1,0:T(4,128)S(1)}, u32[]{:S(2)}, u32[]{:S(2)}) collective-permute-start(f32[4,128]{1,0:T(4,128)S(1)} %slice.35), channel_id=1, source_target_pairs={{0,4},{1,5},{2,6},{3,7},{4,0},{5,1},{6,2},{7,3},{8,12},{9,13},{10,... | collective-permute-start | bytes 6152 | tf_op jit(solution)/shard_map/ppermute | solution.py:182
  44.3 1.3 %collective-permute-start.14 = (f32[4,128]{1,0:T(4,128)S(1)}, f32[4,128]{1,0:T(4,128)S(1)}, u32[]{:S(2)}, u32[]{:S(2)}) collective-permute-start(f32[4,128]{1,0:T(4,128)S(1)} %slice_maximum_fusion), channel_id=1, source_target_pairs={{0,8},{8,0},{16,24},{24,16},{1,9},{9,1},{17,25},{25,17},{2,10},{10... | collective-permute-start | bytes 6152 | tf_op jit(solution)/shard_map/ppermute | solution.py:182
  45.6 1.0 %collective-permute-done.11 = f32[4,128]{1,0:T(4,128)S(1)} collective-permute-done((f32[4,128]{1,0:T(4,128)S(1)}, f32[4,128]{1,0:T(4,128)S(1)}, u32[]{:S(2)}, u32[]{:S(2)}) %collective-permute-start.11) | collective-permute-done | bytes 2080 | tf_op jit(solution)/shard_map/ppermute | solution.py:182
  47.9 2.4 %collective-permute-start.15 = (f32[4,128]{1,0:T(4,128)S(1)}, f32[4,128]{1,0:T(4,128)S(1)}, u32[]{:S(2)}, u32[]{:S(2)}) collective-permute-start(f32[4,128]{1,0:T(4,128)S(1)} %max.18), channel_id=1, source_target_pairs={{0,16},{8,24},{16,0},{24,8},{1,17},{9,25},{17,1},{25,9},{2,18},{10... | collective-permute-start | bytes 6152 | tf_op jit(solution)/shard_map/ppermute | solution.py:182
  50.9 1.5 %collective-permute-done.15 = f32[4,128]{1,0:T(4,128)S(1)} collective-permute-done((f32[4,128]{1,0:T(4,128)S(1)}, f32[4,128]{1,0:T(4,128)S(1)}, u32[]{:S(2)}, u32[]{:S(2)}) %collective-permute-start.15) | collective-permute-done | bytes 2080 | tf_op jit(solution)/shard_map/ppermute | solution.py:182
  (47 shorter events, 8.3 us)
Async XLA Ops:
  0.6 9.7 %collective-permute-start.2 = (bf16[512,1024]{1,0:T(8,128)(2,1)}, bf16[512,1024]{1,0:T(8,128)(2,1)S(1)}, u32[]{:S(2)}, u32[]{:S(2)}) collective-permute-start(bf16[512,1024]{1,0:T(8,128)(2,1)} %own_ref.1), channel_id=1, source_target_pairs={{0,1},{1,0},{2,3},{3,2},{4,5},{5,4},{6,7},{7,6},{8,9},{9,8},{10,11... | collective-permute-start | bytes 3145736 | tf_op jit(solution)/shard_map/ppermute | solution.py:182
  1.1 15.3 %collective-permute-start = (bf16[256,1024]{1,0:T(8,128)(2,1)}, bf16[256,1024]{1,0:T(8,128)(2,1)S(1)}, u32[]{:S(2)}, u32[]{:S(2)}) collective-permute-start(bf16[256,1024]{1,0:T(8,128)(2,1)} %refs_0_.1), channel_id=1, source_target_pairs={{0,2},{1,3},{2,0},{3,1},{4,6},{5,7},{6,4},{7,5},{8,10},{9,11},{10,... | collective-permute-start | bytes 1572872 | tf_op jit(solution)/shard_map/ppermute | solution.py:182
  3.7 14.2 %collective-permute-start.1 = (bf16[256,1024]{1,0:T(8,128)(2,1)}, bf16[256,1024]{1,0:T(8,128)(2,1)S(1)}, u32[]{:S(2)}, u32[]{:S(2)}) collective-permute-start(bf16[256,1024]{1,0:T(8,128)(2,1)} %refs_0_.1), channel_id=1, source_target_pairs={{0,4},{1,5},{2,6},{3,7},{4,0},{5,1},{6,2},{7,3},{8,12},{9,13},{10,... | collective-permute-start | bytes 1572872 | tf_op jit(solution)/shard_map/ppermute | solution.py:182
  5.2 1.4 %collective-permute-start.3 = (s32[16,512]{1,0:T(8,128)}, s32[16,512]{1,0:T(8,128)S(1)}, u32[]{:S(2)}, u32[]{:S(2)}) collective-permute-start(s32[16,512]{1,0:T(8,128)} %bitcast.11), channel_id=1, source_target_pairs={{0,1},{1,0},{2,3},{3,2},{4,5},{5,4},{6,7},{7,6},{8,9},{9,8},{10,11... | collective-permute-start | bytes 98312 | tf_op jit(solution)/shard_map/ppermute | solution.py:182
  6.7 0.9 %copy-start.4 = (s32[2048,16]{0,1:T(8,128)S(1)}, s32[2048,16]{0,1:T(8,128)}, u32[]{:S(2)}) copy-start(s32[2048,16]{0,1:T(8,128)} %param.8) | copy-start | bytes 393220
  7.6 0.8 %copy-start.5 = (s32[512,16]{0,1:T(8,128)S(1)}, s32[512,16]{0,1:T(8,128)}, u32[]{:S(2)}) copy-start(s32[512,16]{0,1:T(8,128)} %param.9) | copy-start | bytes 98308
  8.3 0.7 %copy-start.6 = (s32[8,8]{1,0:T(8,128)S(1)}, s32[8,8]{1,0:T(8,128)}, u32[]{:S(2)}) copy-start(s32[8,8]{1,0:T(8,128)} %pairs_ref.1) | copy-start | bytes 772
  10.4 1.2 %copy-start.2 = (bf16[512,1024]{1,0:T(8,128)(2,1)S(1)}, bf16[512,1024]{1,0:T(8,128)(2,1)}, u32[]{:S(2)}) copy-start(bf16[512,1024]{1,0:T(8,128)(2,1)} %own_ref.1) | copy-start | bytes 3145732
  11.6 1.8 %copy-start.3 = (bf16[256,1024]{1,0:T(8,128)(2,1)S(1)}, bf16[256,1024]{1,0:T(8,128)(2,1)}, u32[]{:S(2)}) copy-start(bf16[256,1024]{1,0:T(8,128)(2,1)} %refs_0_.1) | copy-start | bytes 1572868
  18.0 7.6 %collective-permute-start.5 = (bf16[128,1024]{1,0:T(8,128)(2,1)S(1)}, bf16[128,1024]{1,0:T(8,128)(2,1)S(1)}, u32[]{:S(2)}, u32[]{:S(2)}) collective-permute-start(bf16[128,1024]{1,0:T(8,128)(2,1)S(1)} %slice.31), channel_id=1, source_target_pairs={{0,2},{1,3},{2,0},{3,1},{4,6},{5,7},{6,4},{7,5},{8,10},{9,11},{10,... | collective-permute-start | bytes 786440 | tf_op jit(solution)/shard_map/ppermute | solution.py:182
  18.4 7.5 %collective-permute-start.4 = (bf16[128,1024]{1,0:T(8,128)(2,1)S(1)}, bf16[128,1024]{1,0:T(8,128)(2,1)S(1)}, u32[]{:S(2)}, u32[]{:S(2)}) collective-permute-start(bf16[128,1024]{1,0:T(8,128)(2,1)S(1)} %slice.30), channel_id=1, source_target_pairs={{0,4},{1,5},{2,6},{3,7},{4,0},{5,1},{6,2},{7,3},{8,12},{9,13},{10,... | collective-permute-start | bytes 786440 | tf_op jit(solution)/shard_map/ppermute | solution.py:182
  28.6 1.0 %copy-start = (f32[256,1024]{1,0:T(8,128)}, f32[256,1024]{1,0:T(8,128)S(1)}, u32[]{:S(2)}) copy-start(f32[256,1024]{1,0:T(8,128)S(1)} %get-tuple-element.40.refs_3_) | copy-start | bytes 3145732
  29.6 1.4 %collective-permute-start.8 = (f32[8,128]{1,0:T(8,128)S(1)}, f32[8,128]{1,0:T(8,128)S(1)}, u32[]{:S(2)}, u32[]{:S(2)}) collective-permute-start(f32[8,128]{1,0:T(8,128)S(1)} %get-tuple-element.42), channel_id=1, source_target_pairs={{0,1},{1,0},{2,3},{3,2},{4,5},{5,4},{6,7},{7,6},{8,9},{9,8},{10,11... | collective-permute-start | bytes 12296 | tf_op jit(solution)/shard_map/ppermute | solution.py:182
  29.6 3.6 %collective-permute-start.6 = (f32[8,128]{1,0:T(8,128)S(1)}, f32[8,128]{1,0:T(8,128)S(1)}, u32[]{:S(2)}, u32[]{:S(2)}) collective-permute-start(f32[8,128]{1,0:T(8,128)S(1)} %get-tuple-element.41), channel_id=1, source_target_pairs={{0,2},{1,3},{2,0},{3,1},{4,6},{5,7},{6,4},{7,5},{8,10},{9,11},{10,... | collective-permute-start | bytes 12296 | tf_op jit(solution)/shard_map/ppermute | solution.py:182
  31.0 3.7 %collective-permute-start.9 = (f32[8,128]{1,0:T(8,128)S(1)}, f32[8,128]{1,0:T(8,128)S(1)}, u32[]{:S(2)}, u32[]{:S(2)}) collective-permute-start(f32[8,128]{1,0:T(8,128)S(1)} %maximum_add_fusion), channel_id=1, source_target_pairs={{0,8},{8,0},{16,24},{24,16},{1,9},{9,1},{17,25},{25,17},{2,10},{10... | collective-permute-start | bytes 12296 | tf_op jit(solution)/shard_map/ppermute | solution.py:182
  33.2 4.1 %collective-permute-start.7 = (f32[8,128]{1,0:T(8,128)S(1)}, f32[8,128]{1,0:T(8,128)S(1)}, u32[]{:S(2)}, u32[]{:S(2)}) collective-permute-start(f32[8,128]{1,0:T(8,128)S(1)} %add.15), channel_id=1, source_target_pairs={{0,4},{1,5},{2,6},{3,7},{4,0},{5,1},{6,2},{7,3},{8,12},{9,13},{10,... | collective-permute-start | bytes 12296 | tf_op jit(solution)/shard_map/ppermute | solution.py:182
  34.7 4.5 %collective-permute-start.10 = (f32[8,128]{1,0:T(8,128)S(1)}, f32[8,128]{1,0:T(8,128)S(1)}, u32[]{:S(2)}, u32[]{:S(2)}) collective-permute-start(f32[8,128]{1,0:T(8,128)S(1)} %add.18), channel_id=1, source_target_pairs={{0,16},{8,24},{16,0},{24,8},{1,17},{9,25},{17,1},{25,9},{2,18},{10... | collective-permute-start | bytes 12296 | tf_op jit(solution)/shard_map/ppermute | solution.py:182
  39.2 1.2 %copy-start.1 = (f32[256,1024]{1,0:T(8,128)S(1)}, f32[256,1024]{1,0:T(8,128)}, u32[]{:S(2)}) copy-start(f32[256,1024]{1,0:T(8,128)} %copy-done) | copy-start | bytes 3145732
  42.9 1.4 %collective-permute-start.13 = (f32[4,128]{1,0:T(4,128)S(1)}, f32[4,128]{1,0:T(4,128)S(1)}, u32[]{:S(2)}, u32[]{:S(2)}) collective-permute-start(f32[4,128]{1,0:T(4,128)S(1)} %slice.39), channel_id=1, source_target_pairs={{0,1},{1,0},{2,3},{3,2},{4,5},{5,4},{6,7},{7,6},{8,9},{9,8},{10,11... | collective-permute-start | bytes 6152 | tf_op jit(solution)/shard_map/ppermute | solution.py:182
  43.0 3.7 %collective-permute-start.11 = (f32[4,128]{1,0:T(4,128)S(1)}, f32[4,128]{1,0:T(4,128)S(1)}, u32[]{:S(2)}, u32[]{:S(2)}) collective-permute-start(f32[4,128]{1,0:T(4,128)S(1)} %slice.35), channel_id=1, source_target_pairs={{0,4},{1,5},{2,6},{3,7},{4,0},{5,1},{6,2},{7,3},{8,12},{9,13},{10,... | collective-permute-start | bytes 6152 | tf_op jit(solution)/shard_map/ppermute | solution.py:182
  44.3 3.6 %collective-permute-start.14 = (f32[4,128]{1,0:T(4,128)S(1)}, f32[4,128]{1,0:T(4,128)S(1)}, u32[]{:S(2)}, u32[]{:S(2)}) collective-permute-start(f32[4,128]{1,0:T(4,128)S(1)} %slice_maximum_fusion), channel_id=1, source_target_pairs={{0,8},{8,0},{16,24},{24,16},{1,9},{9,1},{17,25},{25,17},{2,10},{10... | collective-permute-start | bytes 6152 | tf_op jit(solution)/shard_map/ppermute | solution.py:182
  46.6 3.7 %collective-permute-start.12 = (f32[2,128]{1,0:T(2,128)S(1)}, f32[2,128]{1,0:T(2,128)S(1)}, u32[]{:S(2)}, u32[]{:S(2)}) collective-permute-start(f32[2,128]{1,0:T(2,128)S(1)} %slice.37), channel_id=1, source_target_pairs={{0,2},{1,3},{2,0},{3,1},{4,6},{5,7},{6,4},{7,5},{8,10},{9,11},{10,... | collective-permute-start | bytes 3080 | tf_op jit(solution)/shard_map/ppermute | solution.py:182
  47.9 4.5 %collective-permute-start.15 = (f32[4,128]{1,0:T(4,128)S(1)}, f32[4,128]{1,0:T(4,128)S(1)}, u32[]{:S(2)}, u32[]{:S(2)}) collective-permute-start(f32[4,128]{1,0:T(4,128)S(1)} %max.18), channel_id=1, source_target_pairs={{0,16},{8,24},{16,0},{24,8},{1,17},{9,25},{17,1},{25,9},{2,18},{10... | collective-permute-start | bytes 6152 | tf_op jit(solution)/shard_map/ppermute | solution.py:182

commit v3 on v2

--- a/solution.py
+++ b/solution.py
@@ -21,29 +21,31 @@
     return (wide * factor).astype(jnp.bfloat16)
 
 
-def params(flops, bytes_accessed, **more):
+def params(flops, bytes_accessed):
     return dict(
-        compiler_params=pltpu.CompilerParams(vmem_limit_bytes=16 * 2**20, **more),
+        compiler_params=pltpu.CompilerParams(vmem_limit_bytes=16 * 2**20),
         cost_estimate=pl.CostEstimate(flops=flops, bytes_accessed=bytes_accessed, transcendentals=0),
     )
 
 
-def normalise_kernel(own_ref, sibling_ref, unit_ref):
-    rows = own_ref.shape[0]
-    for i, ref in enumerate((own_ref, sibling_ref)):
-
-        def step(j, _, i=i, ref=ref):
-            at = pl.multiple_of(j * 64, 64)
-            unit_ref[pl.ds(i * rows + at, 64), :] = unit_rows(ref[pl.ds(at, 64), :])
-            return 0
-
-        lax.fori_loop(0, rows // 64, step, 0)
-
-
-def lists_kernel(slots, rows, pairs_ref, fwd_ref, bwd_own_ref, bwd_sibling_ref, fwd_at_ref, bwd_at_ref, listed_ref):
+def prepare_kernel(
+    slots, own_ref, sibling_ref, pairs_ref, fwd_ref, bwd_own_ref, bwd_sibling_ref, unit_ref, fwd_at_ref, bwd_at_ref, listed_ref
+):
     src_pos = lax.axis_index("src")
     tgt_pos = lax.axis_index("tgt")
     tgt_count = lax.axis_size("tgt")
+    rows = own_ref.shape[0]
+
+    def normalise(ref, base):
+        def step(i, _):
+            at = pl.multiple_of(i * BLOCK, BLOCK)
+            unit_ref[pl.ds(base + at, BLOCK), :] = unit_rows(ref[pl.ds(at, BLOCK), :])
+            return 0
+
+        lax.fori_loop(0, rows // BLOCK, step, 0)
+
+    normalise(own_ref, 0)
+    normalise(sibling_ref, rows)
     for group in range(fwd_at_ref.shape[0]):
         parts = []
         for g in range(8):
@@ -93,8 +95,7 @@
     columns = unit_ref.shape[0] // LANES
     lane_tile = lax.broadcasted_iota(jnp.int32, (8, LANES), 1) // 16
 
-    def gather(q, _):
-        at = pl.multiple_of(q * 8, 8)
+    def gather(at):
         near = fwd_at_ref[(2 * slot) // 8, pl.ds(at, 8), :]
         low, high = near & (LANES - 1), near >> 7
         got = jnp.zeros((8, LANES), jnp.float32)
@@ -114,9 +115,9 @@
                     piece = turned_ref[pl.ds((group * 8 + g) * LANES + at, 8), c * LANES : (c + 1) * LANES]
                     got = jnp.where(mine == 2 * slot + c, jnp.take_along_axis(piece, low, axis=1), got)
             bwd_got[group, pl.ds(at, 8), :] = got
-        return 0
-
-    lax.fori_loop(0, LANES // 8, gather, 0, unroll=2)
+
+    for q in range(LANES // 8):
+        gather(q * 8)
     first = (2 * slot) % 8 * 16
     fwd = fwd_got[...].T[first : first + 32].reshape(2, 16, LANES).sum(axis=1)
     bwd = [bwd_got[group].T.reshape(8, 16, LANES).sum(axis=1) for group in range(bwd_at_ref.shape[0])]
@@ -203,34 +204,27 @@
     bwd_lists = bwd_idx.T
     sibling_lists = swap(bwd_lists, "tgt", 1)
 
-    unit = pl.pallas_call(
-        normalise_kernel,
-        out_shape=jax.ShapeDtypeStruct((columns, width), jnp.bfloat16),
-        in_specs=[VMEM, VMEM],
-        out_specs=VMEM,
-        name="normalise",
-        **params(1000, 1000),
-    )(tgt_emb, sibling_emb)
     bwd_shape = jax.ShapeDtypeStruct((columns // (8 * LANES), LANES, LANES), jnp.int32)
-    fwd_at, bwd_at, listed = pl.pallas_call(
-        functools.partial(lists_kernel, slots, rows),
+    unit, fwd_at, bwd_at, listed = pl.pallas_call(
+        functools.partial(prepare_kernel, slots),
         out_shape=(
+            jax.ShapeDtypeStruct((columns, width), jnp.bfloat16),
             jax.ShapeDtypeStruct((-(-slots // 4), LANES, LANES), jnp.int32),
             bwd_shape,
             jax.ShapeDtypeStruct((slots * columns // BLOCK,), jnp.int32),
         ),
-        in_specs=[SMEM, VMEM, VMEM, VMEM],
-        out_specs=(VMEM, VMEM, SMEM),
-        name="lists",
+        in_specs=[VMEM, VMEM, SMEM, VMEM, VMEM, VMEM],
+        out_specs=(VMEM, VMEM, VMEM, SMEM),
+        name="prepare",
         **params(1000, 1000),
-    )(pair_list, fwd_idx.T, bwd_lists, sibling_lists)
+    )(tgt_emb, sibling_emb, pair_list, fwd_idx.T, bwd_lists, sibling_lists)
 
     def score(slot, blocks, before=()):
         args = [*blocks, unit, fwd_at, bwd_at, *before]
         return pl.pallas_call(
             functools.partial(score_kernel, slot, len(before) // 2, len(blocks)),
             out_shape=(
-                jax.ShapeDtypeStruct((BLOCK, columns), jnp.float32),
+                pltpu.VMEM((BLOCK, columns), jnp.float32),
                 jax.ShapeDtypeStruct((len(before) + 2, LANES), jnp.float32),
                 jax.ShapeDtypeStruct((columns // LANES, LANES), jnp.float32),
             ),

time: 53.4 us -> 52.6 us (0.985)
  Pallas kernels: 16.2 us -> 11.3 us
  waiting for transfers between devices: 9.22 us -> 11.4 us
  starting transfers between devices: 19.8 us -> 21.7 us
    pallas_call x4, Pallas kernels: 10.6 us -> 7.35 us  [score(): pl.pallas_call(functools.partial(score_kernel, slot, len(before) // 2, le...]
    ppermute x16, waiting for transfers between devices: 9.22 us -> 11.4 us  [swap(): return lax.ppermute(value, axis, [(i, i ^ mask) for i in range(count)])]
    ppermute x16, starting transfers between devices: 19.8 us -> 21.7 us  [swap(): return lax.ppermute(value, axis, [(i, i ^ mask) for i in range(count)])]
    pallas_call x2 -> x1, Pallas kernels: 3.2 us -> 2.12 us  [body(): pl.pallas_call(functools.partial(prepare_kernel, slots), out_shape=(jax.S...]
  transfers between devices with their start and end apart: 16 -> 16, of which waited for: 10 -> 9; matrix products, arithmetic and copies ran while one was open for 1% -> 1% of each run, Pallas kernels for 21% -> 15%
where the time goes in v3:
time: 52.6 us; the launch traced here: 52.2 us
  starting transfers between devices  21.7 us (41%)
  waiting for transfers between devices  11.4 us (22%)
  Pallas kernels  11.3 us (21%)
  local copies, waits for them, and re-layouts  5.85 us (11%)
  other arithmetic  1.19 us (2%)
  between operations  0.75 us (1%)
    ppermute x16, starting transfers between devices, swap(): return lax.ppermute(value, axis, [(i, i ^ mask) for i in range(count)])  21.7 us
    ppermute x16, waiting for transfers between devices, swap(): return lax.ppermute(value, axis, [(i, i ^ mask) for i in range(count)])  11.4 us
    pallas_call x4, Pallas kernels, score(): pl.pallas_call(functools.partial(score_kernel, slot, len(before) // 2, le...  7.35 us
    unnamed x14, local copies, waits for them, and re-layouts  5.79 us
    pallas_call x1, Pallas kernels, body(): pl.pallas_call(functools.partial(prepare_kernel, slots), out_shape=(jax.S...  2.12 us
    pallas_call x1, Pallas kernels, body(): pl.pallas_call(functools.partial(margin_kernel, slots, columns), out_shap...  1.88 us
    reshape x2, other arithmetic, body(): return (src_best.reshape(-1), tgt_best.reshape(-1))  1.15 us
  transfers between devices with their start and end apart: 16, of which 9 were waited for; matrix products, arithmetic and copies ran while one was open for 1% of the time, Pallas kernels for 15%

profile of v3, /device:TPU:0, one launch (start us, length us, event | category | flops | bytes accessed | tf_op | source)
XLA Modules:
  0.0 52.2 jit_solution(14270596691219098283)
XLA Ops:
  1.1 2.6 %collective-permute-start = (bf16[256,1024]{1,0:T(8,128)(2,1)}, bf16[256,1024]{1,0:T(8,128)(2,1)S(1)}, u32[]{:S(2)}, u32[]{:S(2)}) collective-permute-start(bf16[256,1024]{1,0:T(8,128)(2,1)} %refs_0_.1), channel_id=1, source_target_pairs={{0,2},{1,3},{2,0},{3,1},{4,6},{5,7},{6,4},{7,5},{8,10},{9,11},{10,... | collective-permute-start | bytes 1572872 | tf_op jit(solution)/shard_map/ppermute | solution.py:183
  3.7 1.5 %collective-permute-start.1 = (bf16[256,1024]{1,0:T(8,128)(2,1)}, bf16[256,1024]{1,0:T(8,128)(2,1)S(1)}, u32[]{:S(2)}, u32[]{:S(2)}) collective-permute-start(bf16[256,1024]{1,0:T(8,128)(2,1)} %refs_0_.1), channel_id=1, source_target_pairs={{0,4},{1,5},{2,6},{3,7},{4,0},{5,1},{6,2},{7,3},{8,12},{9,13},{10,... | collective-permute-start | bytes 1572872 | tf_op jit(solution)/shard_map/ppermute | solution.py:183
  5.2 1.4 %collective-permute-done.3.bwd_sibling_ref = s32[16,512]{1,0:T(8,128)S(1)} collective-permute-done((s32[16,512]{1,0:T(8,128)}, s32[16,512]{1,0:T(8,128)S(1)}, u32[]{:S(2)}, u32[]{:S(2)}) %collective-permute-start.3) | collective-permute-done | bytes 32800 | tf_op jit(solution)/shard_map/ppermute | solution.py:183
  6.7 1.2 %copy-done.2 = bf16[512,1024]{1,0:T(8,128)(2,1)S(1)} copy-done((bf16[512,1024]{1,0:T(8,128)(2,1)S(1)}, bf16[512,1024]{1,0:T(8,128)(2,1)}, u32[]{:S(2)}) %copy-start.2) | copy-done | bytes 1048600
  10.2 2.1 %prepare.1 = (bf16[1024,1024]{1,0:T(8,128)(2,1)S(1)}, s32[1,128,128]{2,1,0:T(8,128)S(1)}, s32[1,128,128]{2,1,0:T(8,128)S(1)}, s32[16]{0:T(128)S(1)}) custom-call(bf16[512,1024]{1,0:T(8,128)(2,1)S(1)} %copy-done.2, bf16[512,1024]{1,0:T(8,128)(2,1)S(1)} %collective-permute-done.2.sibling_ref, s32[8,8]{1,0:T(8,128)S(1)} %copy-done.6, s32[16,2048]{1,0:T(8,128)S(1)} %bitcast.10, ...), custom_call_target="tpu_custom_call" | custom-call | flops 1000 | bytes 1000 | tf_op jit(solution)/shard_map/prepare/pallas_call | solution.py:208
  12.4 1.8 %score_0.1 = (f32[256,1024]{1,0:T(8,128)S(1)}, f32[2,128]{1,0:T(2,128)S(1)}, f32[8,128]{1,0:T(8,128)S(1)}) custom-call(bf16[256,1024]{1,0:T(8,128)(2,1)S(1)} %copy-done.3, bf16[1024,1024]{1,0:T(8,128)(2,1)S(1)} %get-tuple-element.25.refs_1_.refs_2_, s32[1,128,128]{2,1,0:T(8,128)S(1)} %get-tuple-element.26.refs_2_.refs_3_, ...), custom_call_target="tpu_custom_call" | custom-call | flops 1000 | bytes 1000 | tf_op jit(solution)/shard_map/score_0/pallas_call | solution.py:224
  14.2 2.2 %collective-permute-done.refs_0_ = bf16[256,1024]{1,0:T(8,128)(2,1)S(1)} collective-permute-done((bf16[256,1024]{1,0:T(8,128)(2,1)}, bf16[256,1024]{1,0:T(8,128)(2,1)S(1)}, u32[]{:S(2)}, u32[]{:S(2)}) %collective-permute-start) | collective-permute-done | bytes 524320 | tf_op jit(solution)/shard_map/ppermute | solution.py:183
  16.4 1.5 %collective-permute-done.1.refs_0_ = bf16[256,1024]{1,0:T(8,128)(2,1)S(1)} collective-permute-done((bf16[256,1024]{1,0:T(8,128)(2,1)}, bf16[256,1024]{1,0:T(8,128)(2,1)S(1)}, u32[]{:S(2)}, u32[]{:S(2)}) %collective-permute-start.1) | collective-permute-done | bytes 524320 | tf_op jit(solution)/shard_map/ppermute | solution.py:183
  18.4 1.7 %collective-permute-start.4 = (bf16[128,1024]{1,0:T(8,128)(2,1)S(1)}, bf16[128,1024]{1,0:T(8,128)(2,1)S(1)}, u32[]{:S(2)}, u32[]{:S(2)}) collective-permute-start(bf16[128,1024]{1,0:T(8,128)(2,1)S(1)} %slice.30), channel_id=1, source_target_pairs={{0,4},{1,5},{2,6},{3,7},{4,0},{5,1},{6,2},{7,3},{8,12},{9,13},{10,... | collective-permute-start | bytes 786440 | tf_op jit(solution)/shard_map/ppermute | solution.py:183
  20.1 1.8 %score_2.1 = (f32[256,1024]{1,0:T(8,128)S(1)}, f32[2,128]{1,0:T(2,128)S(1)}, f32[8,128]{1,0:T(8,128)S(1)}) custom-call(bf16[256,1024]{1,0:T(8,128)(2,1)S(1)} %collective-permute-done.1.refs_0_, bf16[1024,1024]{1,0:T(8,128)(2,1)S(1)} %get-tuple-element.25.refs_1_.refs_2_, s32[1,128,128]{2,1,0:T(8,128)S(1)} %get-tuple-element.26.refs_2_.refs_3_, ...), custom_call_target="tpu_custom_call" | custom-call | flops 1073741824 | bytes 1048576 | tf_op jit(solution)/shard_map/score_2/pallas_call | solution.py:224
  21.9 1.8 %score_1.1 = (f32[256,1024]{1,0:T(8,128)S(1)}, f32[2,128]{1,0:T(2,128)S(1)}, f32[8,128]{1,0:T(8,128)S(1)}) custom-call(bf16[256,1024]{1,0:T(8,128)(2,1)S(1)} %collective-permute-done.refs_0_, bf16[1024,1024]{1,0:T(8,128)(2,1)S(1)} %get-tuple-element.25.refs_1_.refs_2_, s32[1,128,128]{2,1,0:T(8,128)S(1)} %get-tuple-element.26.refs_2_.refs_3_, ...), custom_call_target="tpu_custom_call" | custom-call | flops 1073741824 | bytes 1048576 | tf_op jit(solution)/shard_map/score_1/pallas_call | solution.py:224
  23.8 1.8 %collective-permute-done.5.refs_1_ = bf16[128,1024]{1,0:T(8,128)(2,1)S(1)} collective-permute-done((bf16[128,1024]{1,0:T(8,128)(2,1)S(1)}, bf16[128,1024]{1,0:T(8,128)(2,1)S(1)}, u32[]{:S(2)}, u32[]{:S(2)}) %collective-permute-start.5) | collective-permute-done | bytes 262176 | tf_op jit(solution)/shard_map/ppermute | solution.py:183
  25.9 1.8 %score_3.1 = (f32[256,1024]{1,0:T(8,128)S(1)}, f32[8,128]{1,0:T(8,128)S(1)}, f32[8,128]{1,0:T(8,128)S(1)}) custom-call(bf16[128,1024]{1,0:T(8,128)(2,1)S(1)} %collective-permute-done.4.refs_0_, bf16[128,1024]{1,0:T(8,128)(2,1)S(1)} %collective-permute-done.5.refs_1_, bf16[1024,1024]{1,0:T(8,128)(2,1)S(1)} %get-tuple-element.25.refs_1_.refs_2_, ...), custom_call_target="tpu_custom_call" | custom-call | flops 1073741824 | bytes 1048576 | tf_op jit(solution)/shard_map/score_3/pallas_call | solution.py:224
  28.8 1.4 %collective-permute-start.6 = (f32[8,128]{1,0:T(8,128)S(1)}, f32[8,128]{1,0:T(8,128)S(1)}, u32[]{:S(2)}, u32[]{:S(2)}) collective-permute-start(f32[8,128]{1,0:T(8,128)S(1)} %get-tuple-element.43), channel_id=1, source_target_pairs={{0,2},{1,3},{2,0},{3,1},{4,6},{5,7},{6,4},{7,5},{8,10},{9,11},{10,... | collective-permute-start | bytes 12296 | tf_op jit(solution)/shard_map/ppermute | solution.py:183
  30.2 1.6 %collective-permute-start.9 = (f32[8,128]{1,0:T(8,128)S(1)}, f32[8,128]{1,0:T(8,128)S(1)}, u32[]{:S(2)}, u32[]{:S(2)}) collective-permute-start(f32[8,128]{1,0:T(8,128)S(1)} %maximum_add_fusion), channel_id=1, source_target_pairs={{0,8},{8,0},{16,24},{24,16},{1,9},{9,1},{17,25},{25,17},{2,10},{10... | collective-permute-start | bytes 12296 | tf_op jit(solution)/shard_map/ppermute | solution.py:183
  32.4 1.5 %collective-permute-start.7 = (f32[8,128]{1,0:T(8,128)S(1)}, f32[8,128]{1,0:T(8,128)S(1)}, u32[]{:S(2)}, u32[]{:S(2)}) collective-permute-start(f32[8,128]{1,0:T(8,128)S(1)} %add.15), channel_id=1, source_target_pairs={{0,4},{1,5},{2,6},{3,7},{4,0},{5,1},{6,2},{7,3},{8,12},{9,13},{10,... | collective-permute-start | bytes 12296 | tf_op jit(solution)/shard_map/ppermute | solution.py:183
  33.9 2.6 %collective-permute-start.10 = (f32[8,128]{1,0:T(8,128)S(1)}, f32[8,128]{1,0:T(8,128)S(1)}, u32[]{:S(2)}, u32[]{:S(2)}) collective-permute-start(f32[8,128]{1,0:T(8,128)S(1)} %add.18), channel_id=1, source_target_pairs={{0,16},{8,24},{16,0},{24,8},{1,17},{9,25},{17,1},{25,9},{2,18},{10... | collective-permute-start | bytes 12296 | tf_op jit(solution)/shard_map/ppermute | solution.py:183
  36.5 1.9 %collective-permute-done.10 = f32[8,128]{1,0:T(8,128)S(1)} collective-permute-done((f32[8,128]{1,0:T(8,128)S(1)}, f32[8,128]{1,0:T(8,128)S(1)}, u32[]{:S(2)}, u32[]{:S(2)}) %collective-permute-start.10) | collective-permute-done | bytes 4128 | tf_op jit(solution)/shard_map/ppermute | solution.py:183
  38.4 1.2 %copy-done.1 = f32[256,1024]{1,0:T(8,128)S(1)} copy-done((f32[256,1024]{1,0:T(8,128)S(1)}, f32[256,1024]{1,0:T(8,128)}, u32[]{:S(2)}) %copy-start.1) | copy-done | bytes 1048600
  39.6 1.9 %margins.1 = (f32[8,128]{1,0:T(8,128)S(1)}, f32[8,128]{1,0:T(8,128)S(1)}) custom-call(f32[256,1024]{1,0:T(8,128)S(1)} %get-tuple-element.31.refs_0_, f32[256,1024]{1,0:T(8,128)S(1)} %get-tuple-element.33.refs_1_, f32[256,1024]{1,0:T(8,128)S(1)} %get-tuple-element.35.refs_2_, f32[256,1024]{1,0:T(8,128)S(1)} %copy-done.1, f32[8,128]{1,0:T(8,128)S(1)} %add.16.refs_4_, ...), custom_call_target="tpu_custom_call" | custom-call | flops 10485760 | bytes 4194304 | tf_op jit(solution)/shard_map/margins/pallas_call | solution.py:266
  41.6 2.0 %collective-permute-start.11 = (f32[4,128]{1,0:T(4,128)S(1)}, f32[4,128]{1,0:T(4,128)S(1)}, u32[]{:S(2)}, u32[]{:S(2)}) collective-permute-start(f32[4,128]{1,0:T(4,128)S(1)} %slice.35), channel_id=1, source_target_pairs={{0,4},{1,5},{2,6},{3,7},{4,0},{5,1},{6,2},{7,3},{8,12},{9,13},{10,... | collective-permute-start | bytes 6152 | tf_op jit(solution)/shard_map/ppermute | solution.py:183
  43.6 1.7 %collective-permute-start.14 = (f32[4,128]{1,0:T(4,128)S(1)}, f32[4,128]{1,0:T(4,128)S(1)}, u32[]{:S(2)}, u32[]{:S(2)}) collective-permute-start(f32[4,128]{1,0:T(4,128)S(1)} %slice_maximum_fusion), channel_id=1, source_target_pairs={{0,8},{8,0},{16,24},{24,16},{1,9},{9,1},{17,25},{25,17},{2,10},{10... | collective-permute-start | bytes 6152 | tf_op jit(solution)/shard_map/ppermute | solution.py:183
  45.3 1.4 %collective-permute-start.12 = (f32[2,128]{1,0:T(2,128)S(1)}, f32[2,128]{1,0:T(2,128)S(1)}, u32[]{:S(2)}, u32[]{:S(2)}) collective-permute-start(f32[2,128]{1,0:T(2,128)S(1)} %slice.37), channel_id=1, source_target_pairs={{0,2},{1,3},{2,0},{3,1},{4,6},{5,7},{6,4},{7,5},{8,10},{9,11},{10,... | collective-permute-start | bytes 3080 | tf_op jit(solution)/shard_map/ppermute | solution.py:183
  47.2 2.7 %collective-permute-start.15 = (f32[4,128]{1,0:T(4,128)S(1)}, f32[4,128]{1,0:T(4,128)S(1)}, u32[]{:S(2)}, u32[]{:S(2)}) collective-permute-start(f32[4,128]{1,0:T(4,128)S(1)} %max.18), channel_id=1, source_target_pairs={{0,16},{8,24},{16,0},{24,8},{1,17},{9,25},{17,1},{25,9},{2,18},{10... | collective-permute-start | bytes 6152 | tf_op jit(solution)/shard_map/ppermute | solution.py:183
  (46 shorter events, 8.2 us)
Async XLA Ops:
  0.6 6.0 %collective-permute-start.2 = (bf16[512,1024]{1,0:T(8,128)(2,1)}, bf16[512,1024]{1,0:T(8,128)(2,1)S(1)}, u32[]{:S(2)}, u32[]{:S(2)}) collective-permute-start(bf16[512,1024]{1,0:T(8,128)(2,1)} %own_ref.1), channel_id=1, source_target_pairs={{0,1},{1,0},{2,3},{3,2},{4,5},{5,4},{6,7},{7,6},{8,9},{9,8},{10,11... | collective-permute-start | bytes 3145736 | tf_op jit(solution)/shard_map/ppermute | solution.py:183
  1.1 15.3 %collective-permute-start = (bf16[256,1024]{1,0:T(8,128)(2,1)}, bf16[256,1024]{1,0:T(8,128)(2,1)S(1)}, u32[]{:S(2)}, u32[]{:S(2)}) collective-permute-start(bf16[256,1024]{1,0:T(8,128)(2,1)} %refs_0_.1), channel_id=1, source_target_pairs={{0,2},{1,3},{2,0},{3,1},{4,6},{5,7},{6,4},{7,5},{8,10},{9,11},{10,... | collective-permute-start | bytes 1572872 | tf_op jit(solution)/shard_map/ppermute | solution.py:183
  3.7 14.2 %collective-permute-start.1 = (bf16[256,1024]{1,0:T(8,128)(2,1)}, bf16[256,1024]{1,0:T(8,128)(2,1)S(1)}, u32[]{:S(2)}, u32[]{:S(2)}) collective-permute-start(bf16[256,1024]{1,0:T(8,128)(2,1)} %refs_0_.1), channel_id=1, source_target_pairs={{0,4},{1,5},{2,6},{3,7},{4,0},{5,1},{6,2},{7,3},{8,12},{9,13},{10,... | collective-permute-start | bytes 1572872 | tf_op jit(solution)/shard_map/ppermute | solution.py:183
  5.2 1.4 %collective-permute-start.3 = (s32[16,512]{1,0:T(8,128)}, s32[16,512]{1,0:T(8,128)S(1)}, u32[]{:S(2)}, u32[]{:S(2)}) collective-permute-start(s32[16,512]{1,0:T(8,128)} %bitcast.11), channel_id=1, source_target_pairs={{0,1},{1,0},{2,3},{3,2},{4,5},{5,4},{6,7},{7,6},{8,9},{9,8},{10,11... | collective-permute-start | bytes 98312 | tf_op jit(solution)/shard_map/ppermute | solution.py:183
  6.7 1.2 %copy-start.2 = (bf16[512,1024]{1,0:T(8,128)(2,1)S(1)}, bf16[512,1024]{1,0:T(8,128)(2,1)}, u32[]{:S(2)}) copy-start(bf16[512,1024]{1,0:T(8,128)(2,1)} %own_ref.1) | copy-start | bytes 3145732
  7.9 0.9 %copy-start.4 = (s32[2048,16]{0,1:T(8,128)S(1)}, s32[2048,16]{0,1:T(8,128)}, u32[]{:S(2)}) copy-start(s32[2048,16]{0,1:T(8,128)} %param.8) | copy-start | bytes 393220
  8.8 0.8 %copy-start.5 = (s32[512,16]{0,1:T(8,128)S(1)}, s32[512,16]{0,1:T(8,128)}, u32[]{:S(2)}) copy-start(s32[512,16]{0,1:T(8,128)} %param.9) | copy-start | bytes 98308
  9.5 0.7 %copy-start.6 = (s32[8,8]{1,0:T(8,128)S(1)}, s32[8,8]{1,0:T(8,128)}, u32[]{:S(2)}) copy-start(s32[8,8]{1,0:T(8,128)} %pairs_ref.1) | copy-start | bytes 772
  10.2 2.1 %copy-start.3 = (bf16[256,1024]{1,0:T(8,128)(2,1)S(1)}, bf16[256,1024]{1,0:T(8,128)(2,1)}, u32[]{:S(2)}) copy-start(bf16[256,1024]{1,0:T(8,128)(2,1)} %refs_0_.1) | copy-start | bytes 1572868
  18.0 7.6 %collective-permute-start.5 = (bf16[128,1024]{1,0:T(8,128)(2,1)S(1)}, bf16[128,1024]{1,0:T(8,128)(2,1)S(1)}, u32[]{:S(2)}, u32[]{:S(2)}) collective-permute-start(bf16[128,1024]{1,0:T(8,128)(2,1)S(1)} %slice.31), channel_id=1, source_target_pairs={{0,2},{1,3},{2,0},{3,1},{4,6},{5,7},{6,4},{7,5},{8,10},{9,11},{10,... | collective-permute-start | bytes 786440 | tf_op jit(solution)/shard_map/ppermute | solution.py:183
  18.4 7.5 %collective-permute-start.4 = (bf16[128,1024]{1,0:T(8,128)(2,1)S(1)}, bf16[128,1024]{1,0:T(8,128)(2,1)S(1)}, u32[]{:S(2)}, u32[]{:S(2)}) collective-permute-start(bf16[128,1024]{1,0:T(8,128)(2,1)S(1)} %slice.30), channel_id=1, source_target_pairs={{0,4},{1,5},{2,6},{3,7},{4,0},{5,1},{6,2},{7,3},{8,12},{9,13},{10,... | collective-permute-start | bytes 786440 | tf_op jit(solution)/shard_map/ppermute | solution.py:183
  27.8 1.0 %copy-start = (f32[256,1024]{1,0:T(8,128)}, f32[256,1024]{1,0:T(8,128)S(1)}, u32[]{:S(2)}) copy-start(f32[256,1024]{1,0:T(8,128)S(1)} %get-tuple-element.42.refs_3_) | copy-start | bytes 3145732
  28.8 1.4 %collective-permute-start.8 = (f32[8,128]{1,0:T(8,128)S(1)}, f32[8,128]{1,0:T(8,128)S(1)}, u32[]{:S(2)}, u32[]{:S(2)}) collective-permute-start(f32[8,128]{1,0:T(8,128)S(1)} %get-tuple-element.44), channel_id=1, source_target_pairs={{0,1},{1,0},{2,3},{3,2},{4,5},{5,4},{6,7},{7,6},{8,9},{9,8},{10,11... | collective-permute-start | bytes 12296 | tf_op jit(solution)/shard_map/ppermute | solution.py:183
  28.8 3.6 %collective-permute-start.6 = (f32[8,128]{1,0:T(8,128)S(1)}, f32[8,128]{1,0:T(8,128)S(1)}, u32[]{:S(2)}, u32[]{:S(2)}) collective-permute-start(f32[8,128]{1,0:T(8,128)S(1)} %get-tuple-element.43), channel_id=1, source_target_pairs={{0,2},{1,3},{2,0},{3,1},{4,6},{5,7},{6,4},{7,5},{8,10},{9,11},{10,... | collective-permute-start | bytes 12296 | tf_op jit(solution)/shard_map/ppermute | solution.py:183
  30.2 3.7 %collective-permute-start.9 = (f32[8,128]{1,0:T(8,128)S(1)}, f32[8,128]{1,0:T(8,128)S(1)}, u32[]{:S(2)}, u32[]{:S(2)}) collective-permute-start(f32[8,128]{1,0:T(8,128)S(1)} %maximum_add_fusion), channel_id=1, source_target_pairs={{0,8},{8,0},{16,24},{24,16},{1,9},{9,1},{17,25},{25,17},{2,10},{10... | collective-permute-start | bytes 12296 | tf_op jit(solution)/shard_map/ppermute | solution.py:183
  32.4 4.1 %collective-permute-start.7 = (f32[8,128]{1,0:T(8,128)S(1)}, f32[8,128]{1,0:T(8,128)S(1)}, u32[]{:S(2)}, u32[]{:S(2)}) collective-permute-start(f32[8,128]{1,0:T(8,128)S(1)} %add.15), channel_id=1, source_target_pairs={{0,4},{1,5},{2,6},{3,7},{4,0},{5,1},{6,2},{7,3},{8,12},{9,13},{10,... | collective-permute-start | bytes 12296 | tf_op jit(solution)/shard_map/ppermute | solution.py:183
  33.9 4.5 %collective-permute-start.10 = (f32[8,128]{1,0:T(8,128)S(1)}, f32[8,128]{1,0:T(8,128)S(1)}, u32[]{:S(2)}, u32[]{:S(2)}) collective-permute-start(f32[8,128]{1,0:T(8,128)S(1)} %add.18), channel_id=1, source_target_pairs={{0,16},{8,24},{16,0},{24,8},{1,17},{9,25},{17,1},{25,9},{2,18},{10... | collective-permute-start | bytes 12296 | tf_op jit(solution)/shard_map/ppermute | solution.py:183
  38.4 1.2 %copy-start.1 = (f32[256,1024]{1,0:T(8,128)S(1)}, f32[256,1024]{1,0:T(8,128)}, u32[]{:S(2)}) copy-start(f32[256,1024]{1,0:T(8,128)} %copy-done) | copy-start | bytes 3145732
  41.5 2.1 %collective-permute-start.13 = (f32[4,128]{1,0:T(4,128)S(1)}, f32[4,128]{1,0:T(4,128)S(1)}, u32[]{:S(2)}, u32[]{:S(2)}) collective-permute-start(f32[4,128]{1,0:T(4,128)S(1)} %slice.39), channel_id=1, source_target_pairs={{0,1},{1,0},{2,3},{3,2},{4,5},{5,4},{6,7},{7,6},{8,9},{9,8},{10,11... | collective-permute-start | bytes 6152 | tf_op jit(solution)/shard_map/ppermute | solution.py:183
  41.6 3.7 %collective-permute-start.11 = (f32[4,128]{1,0:T(4,128)S(1)}, f32[4,128]{1,0:T(4,128)S(1)}, u32[]{:S(2)}, u32[]{:S(2)}) collective-permute-start(f32[4,128]{1,0:T(4,128)S(1)} %slice.35), channel_id=1, source_target_pairs={{0,4},{1,5},{2,6},{3,7},{4,0},{5,1},{6,2},{7,3},{8,12},{9,13},{10,... | collective-permute-start | bytes 6152 | tf_op jit(solution)/shard_map/ppermute | solution.py:183
  43.6 3.6 %collective-permute-start.14 = (f32[4,128]{1,0:T(4,128)S(1)}, f32[4,128]{1,0:T(4,128)S(1)}, u32[]{:S(2)}, u32[]{:S(2)}) collective-permute-start(f32[4,128]{1,0:T(4,128)S(1)} %slice_maximum_fusion), channel_id=1, source_target_pairs={{0,8},{8,0},{16,24},{24,16},{1,9},{9,1},{17,25},{25,17},{2,10},{10... | collective-permute-start | bytes 6152 | tf_op jit(solution)/shard_map/ppermute | solution.py:183
  45.3 4.6 %collective-permute-start.12 = (f32[2,128]{1,0:T(2,128)S(1)}, f32[2,128]{1,0:T(2,128)S(1)}, u32[]{:S(2)}, u32[]{:S(2)}) collective-permute-start(f32[2,128]{1,0:T(2,128)S(1)} %slice.37), channel_id=1, source_target_pairs={{0,2},{1,3},{2,0},{3,1},{4,6},{5,7},{6,4},{7,5},{8,10},{9,11},{10,... | collective-permute-start | bytes 3080 | tf_op jit(solution)/shard_map/ppermute | solution.py:183
  47.2 4.5 %collective-permute-start.15 = (f32[4,128]{1,0:T(4,128)S(1)}, f32[4,128]{1,0:T(4,128)S(1)}, u32[]{:S(2)}, u32[]{:S(2)}) collective-permute-start(f32[4,128]{1,0:T(4,128)S(1)} %max.18), channel_id=1, source_target_pairs={{0,16},{8,24},{16,0},{24,8},{1,17},{9,25},{17,1},{25,9},{2,18},{10... | collective-permute-start | bytes 6152 | tf_op jit(solution)/shard_map/ppermute | solution.py:183

commit v4 on v3

v4 whole, which is shorter than its diff:
```python
import functools

import jax
import jax.numpy as jnp
from jax import lax
from jax.experimental import pallas as pl
from jax.experimental.pallas import tpu as pltpu
from jax.sharding import PartitionSpec as P

BLOCK = 256
LANES = 128
FIRST = 144
ROWS_CONTRACT = (((1,), (1,)), ((), ()))
VMEM = pl.BlockSpec(memory_space=pltpu.VMEM)
SMEM = pl.BlockSpec(memory_space=pltpu.SMEM)


def unit_rows(values):
    wide = values.astype(jnp.float32)
    factor = lax.rsqrt(jnp.sum(wide * wide, axis=1, keepdims=True) + 1e-06)
    return (wide * factor).astype(jnp.bfloat16)


def params(flops, bytes_accessed):
    return dict(
        compiler_params=pltpu.CompilerParams(vmem_limit_bytes=16 * 2**20),
        cost_estimate=pl.CostEstimate(flops=flops, bytes_accessed=bytes_accessed, transcendentals=0),
    )


def cut_kernel(emb_ref, second_ref, first_ref):
    second_ref[...] = emb_ref[: BLOCK - FIRST, :]
    first_ref[...] = emb_ref[BLOCK - FIRST :, :]


def normalise_kernel(emb_ref, unit_ref):
    def step(i, _):
        at = pl.multiple_of(i * BLOCK, BLOCK)
        unit_ref[pl.ds(at, BLOCK), :] = unit_rows(emb_ref[pl.ds(at, BLOCK), :])
        return 0

    lax.fori_loop(0, emb_ref.shape[0] // BLOCK, step, 0)


def prepare_kernel(
    slots, own_ref, pairs_ref, fwd_ref, bwd_own_ref, bwd_sibling_ref, unit_ref, fwd_at_ref, bwd_at_ref, listed_ref
):
    src_pos = lax.axis_index("src")
    tgt_pos = lax.axis_index("tgt")
    tgt_count = lax.axis_size("tgt")
    rows = own_ref.shape[0]
    normalise_kernel(own_ref, unit_ref)
    for group in range(fwd_at_ref.shape[0]):
        parts = []
        for g in range(8):
            slot, half = (group * 8 + g) // 2, g % 2
            first = lax.bitwise_xor(tgt_pos, 2 * slot) * BLOCK + half * LANES
            parts.append(fwd_ref[:, pl.ds(pl.multiple_of(first, LANES), LANES)])
        near = jnp.concatenate(parts, axis=0)
        chip = lax.bitwise_xor(near // rows, tgt_pos)
        at = jnp.where(chip < 2, chip * rows + near % rows, -1)
        fwd_at_ref[group] = at.T
    tiles = rows // LANES
    for group in range(bwd_at_ref.shape[0]):
        parts = []
        for g in range(8):
            tile = group * 8 + g
            ref = bwd_own_ref if tile < tiles else bwd_sibling_ref
            parts.append(ref[:, (tile % tiles) * LANES : (tile % tiles + 1) * LANES])
        near = jnp.concatenate(parts, axis=0)
        block = near // BLOCK - src_pos * tgt_count
        inside = (block >= 0) & (block < tgt_count)
        peer = lax.bitwise_xor(jnp.where(inside, block, 0), tgt_pos)
        inside = inside & (lax.bitwise_and(peer, 1) == 0)
        at = jnp.where(inside, (peer // 2) * BLOCK + near % BLOCK, -1)
        bwd_at_ref[group] = at.T
    blocks = 2 * rows // BLOCK
    for slot in range(slots):
        row = lax.bitwise_xor(tgt_pos, 2 * slot)
        named = [pairs_ref[row, k] for k in range(pairs_ref.shape[1])]
        for p in range(blocks):
            owner = lax.bitwise_xor(tgt_pos, p // (blocks // 2))
            block = owner * (blocks // 2) + p % (blocks // 2)
            hit = jnp.int32(0)
            for name in named:
                hit = hit | (name == block).astype(jnp.int32)
            listed_ref[slot * blocks + p] = hit


def gather_lanes(near, mine, first, pieces, got):
    for c, piece in enumerate(pieces):
        got = jnp.where(mine == first + c, jnp.take_along_axis(piece, near & (LANES - 1), axis=1), got)
    return got


def lane_tiles():
    return lax.broadcasted_iota(jnp.int32, (8, LANES), 1) // 16


def forward_part(slot, unit, own_ref, sibling_ref, fwd_at_ref, scores_ref, got_ref):
    rows = own_ref.shape[0]
    for i, ref in enumerate((own_ref, sibling_ref)):
        scores_ref[:, i * rows : (i + 1) * rows] = lax.dot_general(
            unit, ref[...], ROWS_CONTRACT, preferred_element_type=jnp.float32
        )
    lane_tile = lane_tiles()
    for at in range(0, LANES, 8):
        near = fwd_at_ref[(2 * slot) // 8, at : at + 8, :]
        got = jnp.zeros((8, LANES), jnp.float32)
        for half in range(2):
            mine = jnp.where(lane_tile == (2 * slot + half) % 8, near >> 7, -1)
            row = half * LANES + at
            pieces = [scores_ref[row : row + 8, c : c + LANES] for c in range(0, 2 * rows, LANES)]
            got = gather_lanes(near, mine, 0, pieces, got)
        got_ref[at : at + 8, :] = got
    first = (2 * slot) % 8 * 16
    return got_ref[...].T[first : first + 32].reshape(2, 16, LANES).sum(axis=1)


def backward_part(slot, unit, own_ref, sibling_ref, bwd_at_ref, turned_ref, got_ref):
    rows = own_ref.shape[0]
    for i, ref in enumerate((own_ref, sibling_ref)):
        turned_ref[i * rows : (i + 1) * rows, :] = lax.dot_general(
            ref[...], unit, ROWS_CONTRACT, preferred_element_type=jnp.float32
        )
    lane_tile = lane_tiles()
    sums = []
    for group in range(bwd_at_ref.shape[0]):
        for at in range(0, LANES, 8):
            near = bwd_at_ref[group, at : at + 8, :]
            got = jnp.zeros((8, LANES), jnp.float32)
            for g in range(8):
                mine = jnp.where(lane_tile == g, near >> 7, -1)
                row = (group * 8 + g) * LANES + at
                pieces = [turned_ref[row : row + 8, c : c + LANES] for c in range(0, BLOCK, LANES)]
                got = gather_lanes(near, mine, 2 * slot, pieces, got)
            got_ref[at : at + 8, :] = got
        sums.append(got_ref[...].T.reshape(8, 16, LANES).sum(axis=1))
    return sums[0] if len(sums) == 1 else jnp.concatenate(sums, axis=0)


def score_kernel(slot, parts, own_ref, sibling_ref, fwd_at_ref, bwd_at_ref, *refs):
    chunk_refs = refs[:parts]
    scores_ref, fwd_ref, bwd_ref, turned_ref, got_ref, back_ref = refs[parts:]
    unit = jnp.concatenate([unit_rows(ref[...]) for ref in chunk_refs], axis=0)
    fwd_ref[...] = forward_part(slot, unit, own_ref, sibling_ref, fwd_at_ref, scores_ref, got_ref)
    bwd_ref[...] = backward_part(slot, unit, own_ref, sibling_ref, bwd_at_ref, turned_ref, back_ref)


def last_score_kernel(slot, parts, own_ref, sibling_ref, fwd_at_ref, bwd_at_ref, *refs):
    chunk_refs, refs = refs[:parts], refs[parts:]
    fwd_before, bwd_before = refs[:slot], refs[slot : 2 * slot]
    scores_ref, fwd_ref, bwd_ref, turned_ref, got_ref, back_ref = refs[2 * slot :]
    unit = jnp.concatenate([unit_rows(ref[...]) for ref in chunk_refs], axis=0)
    for i, ref in enumerate(fwd_before):
        fwd_ref[2 * i : 2 * i + 2, :] = ref[...]
    fwd_ref[2 * slot :, :] = forward_part(slot, unit, own_ref, sibling_ref, fwd_at_ref, scores_ref, got_ref)
    bwd = backward_part(slot, unit, own_ref, sibling_ref, bwd_at_ref, turned_ref, back_ref)
    for ref in bwd_before:
        bwd = bwd + ref[...]
    bwd_ref[...] = bwd


def widen_kernel(fwd_ref, wide_ref):
    for g in range(fwd_ref.shape[0]):
        wide_ref[g * LANES : (g + 1) * LANES, :] = jnp.broadcast_to(fwd_ref[g : g + 1, :], (LANES, LANES)).T


def margin_kernel(slots, columns, *refs):
    score_refs = refs[:slots]
    wide_ref, bwd_ref, listed_ref, row_ref, tgt_ref, col_ref = refs[slots:]
    blocks = columns // BLOCK
    row_ref[...] = jnp.zeros_like(row_ref)
    col_ref[...] = jnp.zeros_like(col_ref)

    for slot in range(slots):
        scores_ref = score_refs[slot]

        def tile(p, _, slot=slot, scores_ref=scores_ref):
            @pl.when(listed_ref[slot * blocks + p] != 0)
            def _():
                columns_at = [pl.ds(pl.multiple_of(p * BLOCK + c * LANES, LANES), LANES) for c in range(2)]
                bwd = [jnp.broadcast_to(bwd_ref[pl.ds(2 * p + c, 1), :], (8, LANES)) for c in range(2)]
                peak = [jnp.zeros((8, LANES), jnp.float32)] * 2
                for at in range(0, BLOCK, 8):
                    rows = slice(slot * BLOCK + at, slot * BLOCK + at + 8)
                    fwd = wide_ref[rows, :]
                    best = row_ref[rows, :]
                    for c in range(2):
                        total = fwd + bwd[c]
                        inverse = pl.reciprocal(total, approx=True)
                        inverse = inverse * (2.0 - total * inverse)
                        ratio = scores_ref[at : at + 8, columns_at[c]] * inverse
                        best = jnp.maximum(best, ratio)
                        peak[c] = jnp.maximum(peak[c], ratio)
                    row_ref[rows, :] = best
                for c in range(2):
                    col_ref[:, columns_at[c]] = jnp.maximum(col_ref[:, columns_at[c]], peak[c])

            return 0

        lax.fori_loop(0, blocks, tile, 0)
    for c in range(columns // LANES):
        tgt_ref[c : c + 1, :] = 32.0 * jnp.max(col_ref[:, c * LANES : (c + 1) * LANES], axis=0, keepdims=True)


def row_kernel(row_ref, src_ref):
    for g in range(src_ref.shape[0]):
        src_ref[g : g + 1, :] = 32.0 * jnp.max(row_ref[g * LANES : (g + 1) * LANES, :].T, axis=0, keepdims=True)


def swap(value, axis, mask):
    count = lax.axis_size(axis)
    return lax.ppermute(value, axis, [(i, i ^ mask) for i in range(count)])


def turn_slots(value, bit):
    step = 2 * bit
    order = [i ^ 1 for i in range(value.shape[0] // step)]
    return jnp.concatenate([value[i * step : (i + 1) * step] for i in order], axis=0)


def body(src_emb, tgt_emb, pair_list, fwd_idx, bwd_idx):
    tgt_count = lax.axis_size("tgt")
    src_count = lax.axis_size("src")
    slots = tgt_count // 2
    rows, width = tgt_emb.shape
    columns = 2 * rows
    tgt_bits = [1 << b for b in range(1, tgt_count.bit_length() - 1)]
    src_bits = [1 << b for b in range(src_count.bit_length() - 1)]

    along_x = swap(src_emb, "tgt", 2)
    second, first = pl.pallas_call(
        cut_kernel,
        out_shape=(
            jax.ShapeDtypeStruct((BLOCK - FIRST, width), src_emb.dtype),
            jax.ShapeDtypeStruct((FIRST, width), src_emb.dtype),
        ),
        in_specs=[VMEM],
        out_specs=(VMEM, VMEM),
        name="cut",
        **params(1000, 1000),
    )(src_emb)
    y_first = swap(first, "tgt", 4)

    sibling_emb = swap(tgt_emb, "tgt", 1)
    bwd_lists = bwd_idx.T
    sibling_lists = swap(bwd_lists, "tgt", 1)

    bwd_shape = jax.ShapeDtypeStruct((columns // (8 * LANES), LANES, LANES), jnp.int32)
    unit_shape = jax.ShapeDtypeStruct((rows, width), jnp.bfloat16)
    sibling_unit = pl.pallas_call(
        normalise_kernel,
        out_shape=unit_shape,
        in_specs=[VMEM],
        out_specs=VMEM,
        name="normalise",
        **params(10**9, rows * width * 4),
    )(sibling_emb)
    own_unit, fwd_at, bwd_at, listed = pl.pallas_call(
        functools.partial(prepare_kernel, slots),
        out_shape=(
            unit_shape,
            jax.ShapeDtypeStruct((-(-slots // 4), LANES, LANES), jnp.int32),
            bwd_shape,
            jax.ShapeDtypeStruct((slots * columns // BLOCK,), jnp.int32),
        ),
        in_specs=[VMEM, SMEM, VMEM, VMEM, VMEM],
        out_specs=(VMEM, VMEM, VMEM, SMEM),
        name="prepare",
        **params(1000, 1000),
    )(tgt_emb, pair_list, fwd_idx.T, bwd_lists, sibling_lists)

    scores_shape = jax.ShapeDtypeStruct((BLOCK, columns), jnp.float32)
    bwd_sums = jax.ShapeDtypeStruct((columns // LANES, LANES), jnp.float32)
    turned = pltpu.VMEM((columns, BLOCK), jnp.float32)
    got = pltpu.VMEM((LANES, LANES), jnp.float32)

    def score(slot, parts):
        args = [own_unit, sibling_unit, fwd_at, bwd_at, *parts]
        return pl.pallas_call(
            functools.partial(score_kernel, slot, len(parts)),
            out_shape=(scores_shape, jax.ShapeDtypeStruct((2, LANES), jnp.float32), bwd_sums),
            in_specs=[VMEM] * len(args),
            out_specs=(VMEM, VMEM, VMEM),
            scratch_shapes=[turned, got, got],
            name=f"score_{slot}",
            **(params(4 * BLOCK * columns * width, BLOCK * columns * 4) if slot else params(1000, 1000)),
        )(*args)

    second, own_unit, sibling_unit = lax.optimization_barrier((second, own_unit, sibling_unit))
    y_second = swap(second, "tgt", 4)
    done = [score(0, (src_emb,))]
    y_first, *done[0] = lax.optimization_barrier((y_first, *done[0]))
    far_first = swap(y_first, "tgt", 2)
    along_x, *done[0] = lax.optimization_barrier((along_x, *done[0]))
    far_second = swap(along_x[: BLOCK - FIRST], "tgt", 4)
    blocks = [(src_emb,), (along_x,), (y_second, y_first), (far_second, far_first)]
    for bit in tgt_bits[2:]:
        blocks += [tuple(swap(part, "tgt", bit) for part in held) for held in blocks]
    for slot in range(1, slots - 1):
        done.append(score(slot, blocks[slot]))
    args = [own_unit, sibling_unit, fwd_at, bwd_at, *blocks[-1], *(d[1] for d in done), *(d[2] for d in done)]
    last_scores, fwd, bwd = pl.pallas_call(
        functools.partial(last_score_kernel, slots - 1, len(blocks[-1])),
        out_shape=(scores_shape, jax.ShapeDtypeStruct((2 * slots, LANES), jnp.float32), bwd_sums),
        in_specs=[VMEM] * len(args),
        out_specs=(VMEM, VMEM, VMEM),
        scratch_shapes=[turned, got, got],
        name=f"score_{slots - 1}",
        **params(4 * BLOCK * columns * width, BLOCK * columns * 4),
    )(*args)
    scores = [*(d[0] for d in done), last_scores]

    def turn_pair(value):
        half = value.shape[0] // 2
        return jnp.concatenate([value[half:], value[:half]], axis=0)

    for bit in src_bits:
        bwd = bwd + swap(bwd, "src", bit)
    bwd = bwd + turn_pair(swap(bwd, "tgt", 1))
    for bit in tgt_bits:
        fwd = fwd + turn_slots(swap(fwd, "tgt", bit), bit // 2)

    wide_shape = jax.ShapeDtypeStruct((slots * BLOCK, LANES), jnp.float32)
    wide = pl.pallas_call(
        widen_kernel, out_shape=wide_shape, in_specs=[VMEM], out_specs=VMEM, name="widen", **params(10**6, 10**6)
    )(fwd)
    row_peaks, tgt_best = pl.pallas_call(
        functools.partial(margin_kernel, slots, columns),
        out_shape=(wide_shape, bwd_sums),
        in_specs=[VMEM] * (slots + 2) + [SMEM],
        out_specs=(VMEM, VMEM),
        scratch_shapes=[pltpu.VMEM((8, columns), jnp.float32)],
        name="margins",
        **params(slots * BLOCK * columns * 10, slots * BLOCK * columns * 4),
    )(*scores, wide, bwd, listed)
    src_best = pl.pallas_call(
        row_kernel,
        out_shape=jax.ShapeDtypeStruct((2 * slots, LANES), jnp.float32),
        in_specs=[VMEM],
        out_specs=VMEM,
        name="row_best",
        **params(10**6, 10**6),
    )(row_peaks)

    for bit in src_bits:
        tgt_best = jnp.maximum(tgt_best, swap(tgt_best, "src", bit))
    half = columns // LANES // 2
    tgt_best = jnp.maximum(tgt_best[:half], swap(tgt_best[half:], "tgt", 1))
    for bit in reversed(tgt_bits):
        keep = src_best.shape[0] // 2
        src_best = jnp.maximum(src_best[:keep], swap(src_best[keep:], "tgt", bit))
    return src_best.reshape(-1), tgt_best.reshape(-1)


def solution(mesh):
    return jax.shard_map(
        body,
        mesh=mesh,
        in_specs=(
            P(("src", "tgt"), None),
            P("tgt", None),
            P("src", None),
            P("src", None),
            P("tgt", None),
        ),
        out_specs=(P(("src", "tgt")), P("tgt")),
        check_vma=False,
    )
```

time: 52.6 us -> 48.1 us (0.914)
  local copies, waits for them, and re-layouts: 5.85 us -> 2.37 us
  waiting for transfers between devices: 11.4 us -> 10.1 us
    unnamed x14 -> x12, local copies, waits for them, and re-layouts: 5.79 us -> 2.32 us
    ppermute x16 -> x17, waiting for transfers between devices: 11.4 us -> 10.1 us  [swap(): return lax.ppermute(value, axis, [(i, i ^ mask) for i in range(count)])]
    pallas_call x5 -> x9, Pallas kernels: 9.46 us -> 9.92 us  [the longest x3 5.52 us: score(): pl.pallas_call(functools.partial(score_kernel, slot, len(parts)), out_sha...]
    ppermute x16 -> x17, starting transfers between devices: 21.7 us -> 21.9 us  [swap(): return lax.ppermute(value, axis, [(i, i ^ mask) for i in range(count)])]
  transfers between devices with their start and end apart: 16 -> 17, of which waited for: 9 -> 10; matrix products, arithmetic and copies ran while one was open for 1% -> 1% of each run, Pallas kernels for 15% -> 17%
where the time goes in v4:
time: 48.1 us; the launch traced here: 47.8 us
  starting transfers between devices  21.9 us (46%)
  Pallas kernels  11.4 us (24%)
  waiting for transfers between devices  10.1 us (21%)
  local copies, waits for them, and re-layouts  2.37 us (5%)
  other arithmetic  1.2 us (2%)
  between operations  0.78 us (2%)
    ppermute x17, starting transfers between devices, swap(): return lax.ppermute(value, axis, [(i, i ^ mask) for i in range(count)])  21.9 us
    ppermute x17, waiting for transfers between devices, swap(): return lax.ppermute(value, axis, [(i, i ^ mask) for i in range(count)])  10.1 us
    pallas_call x3, Pallas kernels, score(): pl.pallas_call(functools.partial(score_kernel, slot, len(parts)), out_sha...  5.52 us
    unnamed x12, local copies, waits for them, and re-layouts  2.32 us
    pallas_call x1, Pallas kernels, body(): pl.pallas_call(functools.partial(last_score_kernel, slots - 1, len(blocks...  1.85 us
    pallas_call x1, Pallas kernels, body(): pl.pallas_call(functools.partial(prepare_kernel, slots), out_shape=(unit_...  1.74 us
    pallas_call x1, Pallas kernels, body(): pl.pallas_call(functools.partial(margin_kernel, slots, columns), out_shap...  1.51 us
    reshape x2, other arithmetic, body(): return (src_best.reshape(-1), tgt_best.reshape(-1))  1.15 us
  transfers between devices with their start and end apart: 17, of which 10 were waited for; matrix products, arithmetic and copies ran while one was open for 1% of the time, Pallas kernels for 17%

profile of v4, /device:TPU:0, one launch (start us, length us, event | category | flops | bytes accessed | tf_op | source)
XLA Modules:
  0.0 47.8 jit_solution(4683576750821463823)
XLA Ops:
  1.1 2.6 %collective-permute-start = (bf16[256,1024]{1,0:T(8,128)(2,1)}, bf16[256,1024]{1,0:T(8,128)(2,1)S(1)}, u32[]{:S(2)}, u32[]{:S(2)}) collective-permute-start(bf16[256,1024]{1,0:T(8,128)(2,1)} %refs_0_.1), channel_id=1, source_target_pairs={{0,2},{1,3},{2,0},{3,1},{4,6},{5,7},{6,4},{7,5},{8,10},{9,11},{10,... | collective-permute-start | bytes 1572872 | tf_op jit(solution)/shard_map/ppermute | solution.py:214
  3.7 1.1 %copy-done = bf16[256,1024]{1,0:T(8,128)(2,1)S(1)} copy-done((bf16[256,1024]{1,0:T(8,128)(2,1)S(1)}, bf16[256,1024]{1,0:T(8,128)(2,1)}, u32[]{:S(2)}) %copy-start) | copy-done | bytes 524312
  4.8 1.6 %collective-permute-start.1 = (bf16[144,1024]{1,0:T(8,128)(2,1)S(1)}, bf16[144,1024]{1,0:T(8,128)(2,1)S(1)}, u32[]{:S(2)}, u32[]{:S(2)}) collective-permute-start(bf16[144,1024]{1,0:T(8,128)(2,1)S(1)} %get-tuple-element.33), channel_id=1, source_target_pairs={{0,4},{1,5},{2,6},{3,7},{4,0},{5,1},{6,2},{7,3},{8,12},{9,13},{10,... | collective-permute-start | bytes 884744 | tf_op jit(solution)/shard_map/ppermute | solution.py:214
  6.4 1.2 %collective-permute-done.2.bwd_sibling_ref = s32[16,512]{1,0:T(8,128)S(1)} collective-permute-done((s32[16,512]{1,0:T(8,128)S(1)}, s32[16,512]{1,0:T(8,128)S(1)}, u32[]{:S(2)}, u32[]{:S(2)}) %collective-permute-start.2) | collective-permute-done | bytes 32800 | tf_op jit(solution)/shard_map/ppermute | solution.py:214
  7.6 1.2 %copy-done.2 = bf16[512,1024]{1,0:T(8,128)(2,1)S(1)} copy-done((bf16[512,1024]{1,0:T(8,128)(2,1)S(1)}, bf16[512,1024]{1,0:T(8,128)(2,1)}, u32[]{:S(2)}) %copy-start.2) | copy-done | bytes 1048600
  8.9 1.7 %prepare.1 = (bf16[512,1024]{1,0:T(8,128)(2,1)S(1)}, s32[1,128,128]{2,1,0:T(8,128)S(1)}, s32[1,128,128]{2,1,0:T(8,128)S(1)}, s32[16]{0:T(128)S(1)}) custom-call(bf16[512,1024]{1,0:T(8,128)(2,1)S(1)} %copy-done.2, s32[8,8]{1,0:T(8,128)S(1)} %copy-done.5, s32[16,2048]{1,0:T(8,128)S(1)} %bitcast.6, s32[16,512]{1,0:T(8,128)S(1)} %bitcast.8, ...), custom_call_target="tpu_custom_call" | custom-call | flops 1000 | bytes 1000 | tf_op jit(solution)/shard_map/prepare/pallas_call | solution.py:260
  11.7 1.8 %score_0.1 = (f32[256,1024]{1,0:T(8,128)S(1)}, f32[2,128]{1,0:T(2,128)S(1)}, f32[8,128]{1,0:T(8,128)S(1)}) custom-call(bf16[512,1024]{1,0:T(8,128)(2,1)S(1)} %get-tuple-element.36.own_ref, bf16[512,1024]{1,0:T(8,128)(2,1)S(1)} %normalise.1.sibling_ref, s32[1,128,128]{2,1,0:T(8,128)S(1)} %get-tuple-element.38.fwd_at_ref, ...), custom_call_target="tpu_custom_call" | custom-call | flops 1000 | bytes 1000 | tf_op jit(solution)/shard_map/score_0/pallas_call | solution.py:281
  14.3 2.1 %collective-permute-done.refs_0_ = bf16[256,1024]{1,0:T(8,128)(2,1)S(1)} collective-permute-done((bf16[256,1024]{1,0:T(8,128)(2,1)}, bf16[256,1024]{1,0:T(8,128)(2,1)S(1)}, u32[]{:S(2)}, u32[]{:S(2)}) %collective-permute-start) | collective-permute-done | bytes 524320 | tf_op jit(solution)/shard_map/ppermute | solution.py:214
  16.5 2.3 %collective-permute-start.5 = (bf16[112,1024]{1,0:T(8,128)(2,1)S(1)}, bf16[112,1024]{1,0:T(8,128)(2,1)S(1)}, u32[]{:S(2)}, u32[]{:S(2)}) collective-permute-start(bf16[112,1024]{1,0:T(8,128)(2,1)S(1)} %slice.45), channel_id=1, source_target_pairs={{0,4},{1,5},{2,6},{3,7},{4,0},{5,1},{6,2},{7,3},{8,12},{9,13},{10,... | collective-permute-start | bytes 688136 | tf_op jit(solution)/shard_map/ppermute | solution.py:214
  18.8 1.8 %score_1.1 = (f32[256,1024]{1,0:T(8,128)S(1)}, f32[2,128]{1,0:T(2,128)S(1)}, f32[8,128]{1,0:T(8,128)S(1)}) custom-call(bf16[512,1024]{1,0:T(8,128)(2,1)S(1)} %get-tuple-element.36.own_ref, bf16[512,1024]{1,0:T(8,128)(2,1)S(1)} %normalise.1.sibling_ref, s32[1,128,128]{2,1,0:T(8,128)S(1)} %get-tuple-element.38.fwd_at_ref, ...), custom_call_target="tpu_custom_call" | custom-call | flops 1073741824 | bytes 1048576 | tf_op jit(solution)/shard_map/score_1/pallas_call | solution.py:281
  20.6 1.8 %score_2.1 = (f32[256,1024]{1,0:T(8,128)S(1)}, f32[2,128]{1,0:T(2,128)S(1)}, f32[8,128]{1,0:T(8,128)S(1)}) custom-call(bf16[512,1024]{1,0:T(8,128)(2,1)S(1)} %get-tuple-element.36.own_ref, bf16[512,1024]{1,0:T(8,128)(2,1)S(1)} %normalise.1.sibling_ref, s32[1,128,128]{2,1,0:T(8,128)S(1)} %get-tuple-element.38.fwd_at_ref, ...), custom_call_target="tpu_custom_call" | custom-call | flops 1073741824 | bytes 1048576 | tf_op jit(solution)/shard_map/score_2/pallas_call | solution.py:281
  22.5 1.4 %collective-permute-done.5.refs_0_ = bf16[112,1024]{1,0:T(8,128)(2,1)S(1)} collective-permute-done((bf16[112,1024]{1,0:T(8,128)(2,1)S(1)}, bf16[112,1024]{1,0:T(8,128)(2,1)S(1)}, u32[]{:S(2)}, u32[]{:S(2)}) %collective-permute-start.5) | collective-permute-done | bytes 229408 | tf_op jit(solution)/shard_map/ppermute | solution.py:214
  23.9 1.8 %score_3.1 = (f32[256,1024]{1,0:T(8,128)S(1)}, f32[8,128]{1,0:T(8,128)S(1)}, f32[8,128]{1,0:T(8,128)S(1)}) custom-call(bf16[512,1024]{1,0:T(8,128)(2,1)S(1)} %get-tuple-element.36.own_ref, bf16[512,1024]{1,0:T(8,128)(2,1)S(1)} %normalise.1.sibling_ref, s32[1,128,128]{2,1,0:T(8,128)S(1)} %get-tuple-element.38.fwd_at_ref, ...), custom_call_target="tpu_custom_call" | custom-call | flops 1073741824 | bytes 1048576 | tf_op jit(solution)/shard_map/score_3/pallas_call | solution.py:304
  25.7 1.7 %collective-permute-start.9 = (f32[8,128]{1,0:T(8,128)S(1)}, f32[8,128]{1,0:T(8,128)S(1)}, u32[]{:S(2)}, u32[]{:S(2)}) collective-permute-start(f32[8,128]{1,0:T(8,128)S(1)} %get-tuple-element.60), channel_id=1, source_target_pairs={{0,8},{8,0},{16,24},{24,16},{1,9},{9,1},{17,25},{25,17},{2,10},{10... | collective-permute-start | bytes 12296 | tf_op jit(solution)/shard_map/ppermute | solution.py:214
  27.5 1.5 %collective-permute-start.7 = (f32[8,128]{1,0:T(8,128)S(1)}, f32[8,128]{1,0:T(8,128)S(1)}, u32[]{:S(2)}, u32[]{:S(2)}) collective-permute-start(f32[8,128]{1,0:T(8,128)S(1)} %get-tuple-element.59), channel_id=1, source_target_pairs={{0,2},{1,3},{2,0},{3,1},{4,6},{5,7},{6,4},{7,5},{8,10},{9,11},{10,... | collective-permute-start | bytes 12296 | tf_op jit(solution)/shard_map/ppermute | solution.py:214
  29.4 2.7 %collective-permute-start.10 = (f32[8,128]{1,0:T(8,128)S(1)}, f32[8,128]{1,0:T(8,128)S(1)}, u32[]{:S(2)}, u32[]{:S(2)}) collective-permute-start(f32[8,128]{1,0:T(8,128)S(1)} %add.17), channel_id=1, source_target_pairs={{0,16},{8,24},{16,0},{24,8},{1,17},{9,25},{17,1},{25,9},{2,18},{10... | collective-permute-start | bytes 12296 | tf_op jit(solution)/shard_map/ppermute | solution.py:214
  32.1 1.6 %collective-permute-start.8 = (f32[8,128]{1,0:T(8,128)S(1)}, f32[8,128]{1,0:T(8,128)S(1)}, u32[]{:S(2)}, u32[]{:S(2)}) collective-permute-start(f32[8,128]{1,0:T(8,128)S(1)} %maximum_add_fusion), channel_id=1, source_target_pairs={{0,4},{1,5},{2,6},{3,7},{4,0},{5,1},{6,2},{7,3},{8,12},{9,13},{10,... | collective-permute-start | bytes 12296 | tf_op jit(solution)/shard_map/ppermute | solution.py:214
  33.9 1.8 %collective-permute-done.8 = f32[8,128]{1,0:T(8,128)S(1)} collective-permute-done((f32[8,128]{1,0:T(8,128)S(1)}, f32[8,128]{1,0:T(8,128)S(1)}, u32[]{:S(2)}, u32[]{:S(2)}) %collective-permute-start.8) | collective-permute-done | bytes 4128 | tf_op jit(solution)/shard_map/ppermute | solution.py:214
  36.0 1.5 %margins.1 = (f32[1024,128]{1,0:T(8,128)S(1)}, f32[8,128]{1,0:T(8,128)S(1)}) custom-call(f32[256,1024]{1,0:T(8,128)S(1)} %get-tuple-element.46.refs_0_, f32[256,1024]{1,0:T(8,128)S(1)} %get-tuple-element.48.refs_1_, f32[256,1024]{1,0:T(8,128)S(1)} %get-tuple-element.51.refs_2_, f32[256,1024]{1,0:T(8,128)S(1)} %get-tuple-element.58.refs_3_, ...), custom_call_target="tpu_custom_call" | custom-call | flops 10485760 | bytes 4194304 | tf_op jit(solution)/shard_map/margins/pallas_call | solution.py:329
  37.5 1.4 %collective-permute-start.14 = (f32[8,128]{1,0:T(8,128)S(1)}, f32[8,128]{1,0:T(8,128)S(1)}, u32[]{:S(2)}, u32[]{:S(2)}) collective-permute-start(f32[8,128]{1,0:T(8,128)S(1)} %get-tuple-element.63), channel_id=1, source_target_pairs={{0,8},{8,0},{16,24},{24,16},{1,9},{9,1},{17,25},{25,17},{2,10},{10... | collective-permute-start | bytes 12296 | tf_op jit(solution)/shard_map/ppermute | solution.py:214
  39.2 2.0 %collective-permute-start.12 = (f32[4,128]{1,0:T(4,128)S(1)}, f32[4,128]{1,0:T(4,128)S(1)}, u32[]{:S(2)}, u32[]{:S(2)}) collective-permute-start(f32[4,128]{1,0:T(4,128)S(1)} %slice.55), channel_id=1, source_target_pairs={{0,4},{1,5},{2,6},{3,7},{4,0},{5,1},{6,2},{7,3},{8,12},{9,13},{10,... | collective-permute-start | bytes 6152 | tf_op jit(solution)/shard_map/ppermute | solution.py:214
  41.2 1.7 %collective-permute-start.15 = (f32[8,128]{1,0:T(8,128)S(1)}, f32[8,128]{1,0:T(8,128)S(1)}, u32[]{:S(2)}, u32[]{:S(2)}) collective-permute-start(f32[8,128]{1,0:T(8,128)S(1)} %max.17), channel_id=1, source_target_pairs={{0,16},{8,24},{16,0},{24,8},{1,17},{9,25},{17,1},{25,9},{2,18},{10... | collective-permute-start | bytes 12296 | tf_op jit(solution)/shard_map/ppermute | solution.py:214
  43.0 1.4 %collective-permute-start.13 = (f32[2,128]{1,0:T(2,128)S(1)}, f32[2,128]{1,0:T(2,128)S(1)}, u32[]{:S(2)}, u32[]{:S(2)}) collective-permute-start(f32[2,128]{1,0:T(2,128)S(1)} %slice.57), channel_id=1, source_target_pairs={{0,2},{1,3},{2,0},{3,1},{4,6},{5,7},{6,4},{7,5},{8,10},{9,11},{10,... | collective-permute-start | bytes 3080 | tf_op jit(solution)/shard_map/ppermute | solution.py:214
  44.4 1.4 %collective-permute-done.15 = f32[8,128]{1,0:T(8,128)S(1)} collective-permute-done((f32[8,128]{1,0:T(8,128)S(1)}, f32[8,128]{1,0:T(8,128)S(1)}, u32[]{:S(2)}, u32[]{:S(2)}) %collective-permute-start.15) | collective-permute-done | bytes 4128 | tf_op jit(solution)/shard_map/ppermute | solution.py:214
  (49 shorter events, 5.7 us)
Async XLA Ops:
  0.6 10.0 %collective-permute-start.3 = (bf16[512,1024]{1,0:T(8,128)(2,1)}, bf16[512,1024]{1,0:T(8,128)(2,1)S(1)}, u32[]{:S(2)}, u32[]{:S(2)}) collective-permute-start(bf16[512,1024]{1,0:T(8,128)(2,1)} %own_ref.1), channel_id=1, source_target_pairs={{0,1},{1,0},{2,3},{3,2},{4,5},{5,4},{6,7},{7,6},{8,9},{9,8},{10,11... | collective-permute-start | bytes 3145736 | tf_op jit(solution)/shard_map/ppermute | solution.py:214
  1.1 15.3 %collective-permute-start = (bf16[256,1024]{1,0:T(8,128)(2,1)}, bf16[256,1024]{1,0:T(8,128)(2,1)S(1)}, u32[]{:S(2)}, u32[]{:S(2)}) collective-permute-start(bf16[256,1024]{1,0:T(8,128)(2,1)} %refs_0_.1), channel_id=1, source_target_pairs={{0,2},{1,3},{2,0},{3,1},{4,6},{5,7},{6,4},{7,5},{8,10},{9,11},{10,... | collective-permute-start | bytes 1572872 | tf_op jit(solution)/shard_map/ppermute | solution.py:214
  3.7 1.1 %copy-start = (bf16[256,1024]{1,0:T(8,128)(2,1)S(1)}, bf16[256,1024]{1,0:T(8,128)(2,1)}, u32[]{:S(2)}) copy-start(bf16[256,1024]{1,0:T(8,128)(2,1)} %refs_0_.1) | copy-start | bytes 1572868
  4.8 1.6 %copy-start.4 = (s32[512,16]{0,1:T(8,128)S(1)}, s32[512,16]{0,1:T(8,128)}, u32[]{:S(2)}) copy-start(s32[512,16]{0,1:T(8,128)} %param.9) | copy-start | bytes 98308
  4.8 2.9 %copy-start.3 = (s32[2048,16]{0,1:T(8,128)S(1)}, s32[2048,16]{0,1:T(8,128)}, u32[]{:S(2)}) copy-start(s32[2048,16]{0,1:T(8,128)} %param.8) | copy-start | bytes 393220
  4.8 2.8 %copy-start.5 = (s32[8,8]{1,0:T(8,128)S(1)}, s32[8,8]{1,0:T(8,128)}, u32[]{:S(2)}) copy-start(s32[8,8]{1,0:T(8,128)} %pairs_ref.1) | copy-start | bytes 772
  4.8 9.2 %collective-permute-start.1 = (bf16[144,1024]{1,0:T(8,128)(2,1)S(1)}, bf16[144,1024]{1,0:T(8,128)(2,1)S(1)}, u32[]{:S(2)}, u32[]{:S(2)}) collective-permute-start(bf16[144,1024]{1,0:T(8,128)(2,1)S(1)} %get-tuple-element.33), channel_id=1, source_target_pairs={{0,4},{1,5},{2,6},{3,7},{4,0},{5,1},{6,2},{7,3},{8,12},{9,13},{10,... | collective-permute-start | bytes 884744 | tf_op jit(solution)/shard_map/ppermute | solution.py:214
  6.4 1.2 %collective-permute-start.2 = (s32[16,512]{1,0:T(8,128)S(1)}, s32[16,512]{1,0:T(8,128)S(1)}, u32[]{:S(2)}, u32[]{:S(2)}) collective-permute-start(s32[16,512]{1,0:T(8,128)S(1)} %bitcast.7), channel_id=1, source_target_pairs={{0,1},{1,0},{2,3},{3,2},{4,5},{5,4},{6,7},{7,6},{8,9},{9,8},{10,11... | collective-permute-start | bytes 98312 | tf_op jit(solution)/shard_map/ppermute | solution.py:214
  7.6 1.2 %copy-start.2 = (bf16[512,1024]{1,0:T(8,128)(2,1)S(1)}, bf16[512,1024]{1,0:T(8,128)(2,1)}, u32[]{:S(2)}) copy-start(bf16[512,1024]{1,0:T(8,128)(2,1)} %own_ref.1) | copy-start | bytes 3145732
  10.6 1.1 %copy-start.1 = (bf16[256,1024]{1,0:T(8,128)(2,1)S(1)}, bf16[256,1024]{1,0:T(8,128)(2,1)}, u32[]{:S(2)}) copy-start(bf16[256,1024]{1,0:T(8,128)(2,1)} %refs_0_.1) | copy-start | bytes 1572868
  11.0 9.6 %collective-permute-start.4 = (bf16[112,1024]{1,0:T(8,128)(2,1)S(1)}, bf16[112,1024]{1,0:T(8,128)(2,1)S(1)}, u32[]{:S(2)}, u32[]{:S(2)}) collective-permute-start(bf16[112,1024]{1,0:T(8,128)(2,1)S(1)} %get-tuple-element.49), channel_id=1, source_target_pairs={{0,4},{1,5},{2,6},{3,7},{4,0},{5,1},{6,2},{7,3},{8,12},{9,13},{10,... | collective-permute-start | bytes 688136 | tf_op jit(solution)/shard_map/ppermute | solution.py:214
  14.1 9.8 %collective-permute-start.6 = (bf16[144,1024]{1,0:T(8,128)(2,1)S(1)}, bf16[144,1024]{1,0:T(8,128)(2,1)S(1)}, u32[]{:S(2)}, u32[]{:S(2)}) collective-permute-start(bf16[144,1024]{1,0:T(8,128)(2,1)S(1)} %collective-permute-done.1.refs_1_), channel_id=1, source_target_pairs={{0,2},{1,3},{2,0},{3,1},{4,6},{5,7},{6,4},{7,5},{8,10},{9,11},{10,... | collective-permute-start | bytes 884744 | tf_op jit(solution)/shard_map/ppermute | solution.py:214
  16.5 7.4 %collective-permute-start.5 = (bf16[112,1024]{1,0:T(8,128)(2,1)S(1)}, bf16[112,1024]{1,0:T(8,128)(2,1)S(1)}, u32[]{:S(2)}, u32[]{:S(2)}) collective-permute-start(bf16[112,1024]{1,0:T(8,128)(2,1)S(1)} %slice.45), channel_id=1, source_target_pairs={{0,4},{1,5},{2,6},{3,7},{4,0},{5,1},{6,2},{7,3},{8,12},{9,13},{10,... | collective-permute-start | bytes 688136 | tf_op jit(solution)/shard_map/ppermute | solution.py:214
  25.7 3.7 %collective-permute-start.9 = (f32[8,128]{1,0:T(8,128)S(1)}, f32[8,128]{1,0:T(8,128)S(1)}, u32[]{:S(2)}, u32[]{:S(2)}) collective-permute-start(f32[8,128]{1,0:T(8,128)S(1)} %get-tuple-element.60), channel_id=1, source_target_pairs={{0,8},{8,0},{16,24},{24,16},{1,9},{9,1},{17,25},{25,17},{2,10},{10... | collective-permute-start | bytes 12296 | tf_op jit(solution)/shard_map/ppermute | solution.py:214
  27.5 4.6 %collective-permute-start.7 = (f32[8,128]{1,0:T(8,128)S(1)}, f32[8,128]{1,0:T(8,128)S(1)}, u32[]{:S(2)}, u32[]{:S(2)}) collective-permute-start(f32[8,128]{1,0:T(8,128)S(1)} %get-tuple-element.59), channel_id=1, source_target_pairs={{0,2},{1,3},{2,0},{3,1},{4,6},{5,7},{6,4},{7,5},{8,10},{9,11},{10,... | collective-permute-start | bytes 12296 | tf_op jit(solution)/shard_map/ppermute | solution.py:214
  29.4 4.5 %collective-permute-start.10 = (f32[8,128]{1,0:T(8,128)S(1)}, f32[8,128]{1,0:T(8,128)S(1)}, u32[]{:S(2)}, u32[]{:S(2)}) collective-permute-start(f32[8,128]{1,0:T(8,128)S(1)} %add.17), channel_id=1, source_target_pairs={{0,16},{8,24},{16,0},{24,8},{1,17},{9,25},{17,1},{25,9},{2,18},{10... | collective-permute-start | bytes 12296 | tf_op jit(solution)/shard_map/ppermute | solution.py:214
  32.1 3.7 %collective-permute-start.8 = (f32[8,128]{1,0:T(8,128)S(1)}, f32[8,128]{1,0:T(8,128)S(1)}, u32[]{:S(2)}, u32[]{:S(2)}) collective-permute-start(f32[8,128]{1,0:T(8,128)S(1)} %maximum_add_fusion), channel_id=1, source_target_pairs={{0,4},{1,5},{2,6},{3,7},{4,0},{5,1},{6,2},{7,3},{8,12},{9,13},{10,... | collective-permute-start | bytes 12296 | tf_op jit(solution)/shard_map/ppermute | solution.py:214
  33.9 2.1 %collective-permute-start.11 = (f32[8,128]{1,0:T(8,128)S(1)}, f32[8,128]{1,0:T(8,128)S(1)}, u32[]{:S(2)}, u32[]{:S(2)}) collective-permute-start(f32[8,128]{1,0:T(8,128)S(1)} %add.18), channel_id=1, source_target_pairs={{0,1},{1,0},{2,3},{3,2},{4,5},{5,4},{6,7},{7,6},{8,9},{9,8},{10,11... | collective-permute-start | bytes 12296 | tf_op jit(solution)/shard_map/ppermute | solution.py:214
  37.5 3.7 %collective-permute-start.14 = (f32[8,128]{1,0:T(8,128)S(1)}, f32[8,128]{1,0:T(8,128)S(1)}, u32[]{:S(2)}, u32[]{:S(2)}) collective-permute-start(f32[8,128]{1,0:T(8,128)S(1)} %get-tuple-element.63), channel_id=1, source_target_pairs={{0,8},{8,0},{16,24},{24,16},{1,9},{9,1},{17,25},{25,17},{2,10},{10... | collective-permute-start | bytes 12296 | tf_op jit(solution)/shard_map/ppermute | solution.py:214
  39.2 3.8 %collective-permute-start.12 = (f32[4,128]{1,0:T(4,128)S(1)}, f32[4,128]{1,0:T(4,128)S(1)}, u32[]{:S(2)}, u32[]{:S(2)}) collective-permute-start(f32[4,128]{1,0:T(4,128)S(1)} %slice.55), channel_id=1, source_target_pairs={{0,4},{1,5},{2,6},{3,7},{4,0},{5,1},{6,2},{7,3},{8,12},{9,13},{10,... | collective-permute-start | bytes 6152 | tf_op jit(solution)/shard_map/ppermute | solution.py:214
  41.2 4.5 %collective-permute-start.15 = (f32[8,128]{1,0:T(8,128)S(1)}, f32[8,128]{1,0:T(8,128)S(1)}, u32[]{:S(2)}, u32[]{:S(2)}) collective-permute-start(f32[8,128]{1,0:T(8,128)S(1)} %max.17), channel_id=1, source_target_pairs={{0,16},{8,24},{16,0},{24,8},{1,17},{9,25},{17,1},{25,9},{2,18},{10... | collective-permute-start | bytes 12296 | tf_op jit(solution)/shard_map/ppermute | solution.py:214
  43.0 3.6 %collective-permute-start.13 = (f32[2,128]{1,0:T(2,128)S(1)}, f32[2,128]{1,0:T(2,128)S(1)}, u32[]{:S(2)}, u32[]{:S(2)}) collective-permute-start(f32[2,128]{1,0:T(2,128)S(1)} %slice.57), channel_id=1, source_target_pairs={{0,2},{1,3},{2,0},{3,1},{4,6},{5,7},{6,4},{7,5},{8,10},{9,11},{10,... | collective-permute-start | bytes 3080 | tf_op jit(solution)/shard_map/ppermute | solution.py:214
  45.7 1.4 %collective-permute-start.16 = (f32[4,128]{1,0:T(4,128)S(1)}, f32[4,128]{1,0:T(4,128)S(1)}, u32[]{:S(2)}, u32[]{:S(2)}) collective-permute-start(f32[4,128]{1,0:T(4,128)S(1)} %slice.59), channel_id=1, source_target_pairs={{0,1},{1,0},{2,3},{3,2},{4,5},{5,4},{6,7},{7,6},{8,9},{9,8},{10,11... | collective-permute-start | bytes 6152 | tf_op jit(solution)/shard_map/ppermute | solution.py:214

commit v5 on v4

--- a/solution.py
+++ b/solution.py
@@ -9,7 +9,7 @@
 
 BLOCK = 256
 LANES = 128
-FIRST = 144
+FIRST = 160
 ROWS_CONTRACT = (((1,), (1,)), ((), ()))
 VMEM = pl.BlockSpec(memory_space=pltpu.VMEM)
 SMEM = pl.BlockSpec(memory_space=pltpu.SMEM)
@@ -150,7 +150,7 @@
 def last_score_kernel(slot, parts, own_ref, sibling_ref, fwd_at_ref, bwd_at_ref, *refs):
     chunk_refs, refs = refs[:parts], refs[parts:]
     fwd_before, bwd_before = refs[:slot], refs[slot : 2 * slot]
-    scores_ref, fwd_ref, bwd_ref, turned_ref, got_ref, back_ref = refs[2 * slot :]
+    scores_ref, fwd_ref, bwd_ref, send_ref, turned_ref, got_ref, back_ref = refs[2 * slot :]
     unit = jnp.concatenate([unit_rows(ref[...]) for ref in chunk_refs], axis=0)
     for i, ref in enumerate(fwd_before):
         fwd_ref[2 * i : 2 * i + 2, :] = ref[...]
@@ -159,16 +159,61 @@
     for ref in bwd_before:
         bwd = bwd + ref[...]
     bwd_ref[...] = bwd
-
-
-def widen_kernel(fwd_ref, wide_ref):
-    for g in range(fwd_ref.shape[0]):
-        wide_ref[g * LANES : (g + 1) * LANES, :] = jnp.broadcast_to(fwd_ref[g : g + 1, :], (LANES, LANES)).T
+    send_ref[...] = choose(fwd_ref[...], bwd, send_ref.shape[0])
+
+
+def fit(value, rows):
+    if value.shape[0] < rows:
+        value = jnp.concatenate([value, jnp.zeros((rows - value.shape[0], LANES), value.dtype)], axis=0)
+    return value[:rows]
+
+
+def choose(on_odd, on_even, rows):
+    odd = lax.broadcasted_iota(jnp.int32, (rows, LANES), 0) * 0 + lax.axis_index("tgt") % 2 == 1
+    return jnp.where(odd, fit(on_odd, rows), fit(on_even, rows))
+
+
+def turn_pair(value):
+    half = value.shape[0] // 2
+    return jnp.concatenate([value[half:], value[:half]], axis=0)
+
+
+def masks(slots):
+    return [2, 1, *range(3, slots)]
+
+
+def pair_kernel(combine, by_src_ref, by_tgt_ref, got_ref, state_ref):
+    high, wide = by_src_ref.shape[0], by_tgt_ref.shape[0]
+    by_src = jnp.concatenate([by_src_ref[...], got_ref[:high, :]], axis=0)
+    by_tgt = combine(by_tgt_ref[...], turn_pair(got_ref[:wide, :]))
+    state_ref[...] = choose(by_tgt, by_src, state_ref.shape[0])
+
+
+def collect_kernel(combine, slots, wide, last, state_ref, *refs):
+    got_refs, (total_ref, send_ref) = refs[:-2], refs[-2:]
+    by_tgt = state_ref[:wide, :]
+    by_src = [state_ref[2 * i : 2 * i + 2, :] for i in range(2 * slots)]
+    for k, ref in enumerate(got_refs):
+        by_tgt = combine(by_tgt, ref[:wide, :])
+        if k + 1 < slots:
+            order = [2 * (i ^ masks(slots)[k]) for i in range(2 * slots)]
+            by_src = [combine(one, ref[i : i + 2, :]) for one, i in zip(by_src, order, strict=True)]
+    by_src = jnp.concatenate(by_src, axis=0)
+    total_ref[...] = choose(by_tgt, by_src, total_ref.shape[0])
+    send_ref[...] = choose(by_tgt[wide // 2 :] if last else by_tgt, by_src[2 * slots :], send_ref.shape[0])
+
+
+def widen_kernel(wide, total_ref, got_ref, wide_ref, bwd_ref):
+    high = wide_ref.shape[0] // LANES
+    fwd = choose(got_ref[:high, :], total_ref[:high, :], high)
+    bwd_ref[...] = choose(total_ref[:wide, :], turn_pair(got_ref[:wide, :]), wide)
+    for g in range(high):
+        wide_ref[g * LANES : (g + 1) * LANES, :] = jnp.broadcast_to(fwd[g : g + 1, :], (LANES, LANES)).T
 
 
 def margin_kernel(slots, columns, *refs):
     score_refs = refs[:slots]
-    wide_ref, bwd_ref, listed_ref, row_ref, tgt_ref, col_ref = refs[slots:]
+    wide_ref, bwd_ref, listed_ref, src_ref, tgt_ref, send_ref, row_ref, col_ref = refs[slots:]
     blocks = columns // BLOCK
     row_ref[...] = jnp.zeros_like(row_ref)
     col_ref[...] = jnp.zeros_like(col_ref)
@@ -202,11 +247,15 @@
         lax.fori_loop(0, blocks, tile, 0)
     for c in range(columns // LANES):
         tgt_ref[c : c + 1, :] = 32.0 * jnp.max(col_ref[:, c * LANES : (c + 1) * LANES], axis=0, keepdims=True)
-
-
-def row_kernel(row_ref, src_ref):
     for g in range(src_ref.shape[0]):
         src_ref[g : g + 1, :] = 32.0 * jnp.max(row_ref[g * LANES : (g + 1) * LANES, :].T, axis=0, keepdims=True)
+    send_ref[...] = choose(src_ref[...], tgt_ref[...], send_ref.shape[0])
+
+
+def last_kernel(total_ref, got_ref, src_ref, tgt_ref):
+    src, tgt = src_ref.shape[0], tgt_ref.shape[0]
+    src_ref[...] = choose(got_ref[:src, :], total_ref[:src, :], src)
+    tgt_ref[...] = choose(total_ref[:tgt, :], got_ref[:tgt, :], tgt)
 
 
 def swap(value, axis, mask):
@@ -214,20 +263,45 @@
     return lax.ppermute(value, axis, [(i, i ^ mask) for i in range(count)])
 
 
-def turn_slots(value, bit):
-    step = 2 * bit
-    order = [i ^ 1 for i in range(value.shape[0] // step)]
-    return jnp.concatenate([value[i * step : (i + 1) * step] for i in order], axis=0)
+def small_call(kernel, name, shapes, *args):
+    return pl.pallas_call(
+        kernel,
+        out_shape=tuple(jax.ShapeDtypeStruct((rows, LANES), jnp.float32) for rows in shapes),
+        in_specs=[VMEM] * len(args),
+        out_specs=(VMEM,) * len(shapes),
+        name=name,
+        **params(10**6, 10**6),
+    )(*args)
+
+
+def reduce_all(combine, by_src, by_tgt, send, name, last):
+    tgt_count, src_count = lax.axis_size("tgt"), lax.axis_size("src")
+    high, wide = by_src.shape[0], by_tgt.shape[0]
+    got = swap(send, "tgt", 1)
+    rows = max(2 * high, wide)
+    (state,) = small_call(functools.partial(pair_kernel, combine), name + "_pair", (rows,), by_src, by_tgt, got)
+    parts = []
+    for i in range(1, max(tgt_count // 2, src_count)):
+        pairs = []
+        for device in range(src_count * tgt_count):
+            if device % 2 == 0 and i < tgt_count // 2:
+                pairs.append((device, device ^ (2 * masks(tgt_count // 2)[i - 1])))
+            if device % 2 == 1 and i < src_count:
+                pairs.append((device, device ^ (i * tgt_count)))
+        parts.append(lax.ppermute(state, ("src", "tgt"), pairs))
+    back = max(2, wide // 2) if last else max(high, wide)
+    total, send = small_call(
+        functools.partial(collect_kernel, combine, high // 2, wide, last), name + "_collect", (rows, back), state, *parts
+    )
+    return total, swap(send, "tgt", 1)
 
 
 def body(src_emb, tgt_emb, pair_list, fwd_idx, bwd_idx):
     tgt_count = lax.axis_size("tgt")
-    src_count = lax.axis_size("src")
     slots = tgt_count // 2
     rows, width = tgt_emb.shape
     columns = 2 * rows
     tgt_bits = [1 << b for b in range(1, tgt_count.bit_length() - 1)]
-    src_bits = [1 << b for b in range(src_count.bit_length() - 1)]
 
     along_x = swap(src_emb, "tgt", 2)
     second, first = pl.pallas_call(
@@ -288,7 +362,7 @@
             **(params(4 * BLOCK * columns * width, BLOCK * columns * 4) if slot else params(1000, 1000)),
         )(*args)
 
-    second, own_unit, sibling_unit = lax.optimization_barrier((second, own_unit, sibling_unit))
+    own_unit, sibling_unit = lax.optimization_barrier((own_unit, sibling_unit))
     y_second = swap(second, "tgt", 4)
     done = [score(0, (src_emb,))]
     y_first, *done[0] = lax.optimization_barrier((y_first, *done[0]))
@@ -298,59 +372,40 @@
     blocks = [(src_emb,), (along_x,), (y_second, y_first), (far_second, far_first)]
     for bit in tgt_bits[2:]:
         blocks += [tuple(swap(part, "tgt", bit) for part in held) for held in blocks]
-    for slot in range(1, slots - 1):
+    along_y = score(2, blocks[2])
+    along_x, *along_y = lax.optimization_barrier((along_x, *along_y))
+    done += [score(1, (along_x,)), along_y]
+    for slot in range(3, slots - 1):
         done.append(score(slot, blocks[slot]))
     args = [own_unit, sibling_unit, fwd_at, bwd_at, *blocks[-1], *(d[1] for d in done), *(d[2] for d in done)]
-    last_scores, fwd, bwd = pl.pallas_call(
+    fwd_sums = jax.ShapeDtypeStruct((2 * slots, LANES), jnp.float32)
+    sent = jax.ShapeDtypeStruct((max(2 * slots, columns // LANES), LANES), jnp.float32)
+    last_scores, fwd, bwd, send = pl.pallas_call(
         functools.partial(last_score_kernel, slots - 1, len(blocks[-1])),
-        out_shape=(scores_shape, jax.ShapeDtypeStruct((2 * slots, LANES), jnp.float32), bwd_sums),
+        out_shape=(scores_shape, fwd_sums, bwd_sums, sent),
         in_specs=[VMEM] * len(args),
-        out_specs=(VMEM, VMEM, VMEM),
+        out_specs=(VMEM,) * 4,
         scratch_shapes=[turned, got, got],
         name=f"score_{slots - 1}",
         **params(4 * BLOCK * columns * width, BLOCK * columns * 4),
     )(*args)
     scores = [*(d[0] for d in done), last_scores]
 
-    def turn_pair(value):
-        half = value.shape[0] // 2
-        return jnp.concatenate([value[half:], value[:half]], axis=0)
-
-    for bit in src_bits:
-        bwd = bwd + swap(bwd, "src", bit)
-    bwd = bwd + turn_pair(swap(bwd, "tgt", 1))
-    for bit in tgt_bits:
-        fwd = fwd + turn_slots(swap(fwd, "tgt", bit), bit // 2)
-
-    wide_shape = jax.ShapeDtypeStruct((slots * BLOCK, LANES), jnp.float32)
-    wide = pl.pallas_call(
-        widen_kernel, out_shape=wide_shape, in_specs=[VMEM], out_specs=VMEM, name="widen", **params(10**6, 10**6)
-    )(fwd)
-    row_peaks, tgt_best = pl.pallas_call(
+    total, got = reduce_all(jnp.add, fwd, bwd, send, "mean", False)
+    wide, bwd = small_call(
+        functools.partial(widen_kernel, columns // LANES), "widen", (slots * BLOCK, columns // LANES), total, got
+    )
+    src_best, tgt_best, send = pl.pallas_call(
         functools.partial(margin_kernel, slots, columns),
-        out_shape=(wide_shape, bwd_sums),
+        out_shape=(fwd_sums, bwd_sums, sent),
         in_specs=[VMEM] * (slots + 2) + [SMEM],
-        out_specs=(VMEM, VMEM),
-        scratch_shapes=[pltpu.VMEM((8, columns), jnp.float32)],
+        out_specs=(VMEM,) * 3,
+        scratch_shapes=[pltpu.VMEM((slots * BLOCK, LANES), jnp.float32), pltpu.VMEM((8, columns), jnp.float32)],
         name="margins",
         **params(slots * BLOCK * columns * 10, slots * BLOCK * columns * 4),
     )(*scores, wide, bwd, listed)
-    src_best = pl.pallas_call(
-        row_kernel,
-        out_shape=jax.ShapeDtypeStruct((2 * slots, LANES), jnp.float32),
-        in_specs=[VMEM],
-        out_specs=VMEM,
-        name="row_best",
-        **params(10**6, 10**6),
-    )(row_peaks)
-
-    for bit in src_bits:
-        tgt_best = jnp.maximum(tgt_best, swap(tgt_best, "src", bit))
-    half = columns // LANES // 2
-    tgt_best = jnp.maximum(tgt_best[:half], swap(tgt_best[half:], "tgt", 1))
-    for bit in reversed(tgt_bits):
-        keep = src_best.shape[0] // 2
-        src_best = jnp.maximum(src_best[:keep], swap(src_best[keep:], "tgt", bit))
+    total, got = reduce_all(jnp.maximum, src_best, tgt_best, send, "best", True)
+    src_best, tgt_best = small_call(last_kernel, "last", (BLOCK // LANES, rows // LANES), total, got)
     return src_best.reshape(-1), tgt_best.reshape(-1)
 
 

time: 48.1 us -> 46.6 us (0.969)
  starting transfers between devices: 21.9 us -> 15.5 us
  waiting for transfers between devices: 10.1 us -> 15 us
  other arithmetic: 1.2 us -> 0 us
  Pallas kernels: 11.4 us -> 12.1 us
  local copies, waits for them, and re-layouts: 2.37 us -> 2.97 us
    ppermute x17 -> x11, starting transfers between devices: 21.9 us -> 8.47 us  [swap(): return lax.ppermute(value, axis, [(i, i ^ mask) for i in range(count)])]
    ppermute x0 -> x6, starting transfers between devices: none -> 6.98 us  [reduce_all(): parts.append(lax.ppermute(state, ('src', 'tgt'), pairs))]
    ppermute x0 -> x6, waiting for transfers between devices: none -> 6.21 us  [reduce_all(): parts.append(lax.ppermute(state, ('src', 'tgt'), pairs))]
    ppermute x17 -> x11, waiting for transfers between devices: 10.1 us -> 8.77 us  [swap(): return lax.ppermute(value, axis, [(i, i ^ mask) for i in range(count)])]
    reshape x2 -> x0, other arithmetic: 1.15 us -> none  [body(): return (src_best.reshape(-1), tgt_best.reshape(-1))]
    unnamed x12, local copies, waits for them, and re-layouts: 2.32 us -> 2.95 us
  transfers between devices with their start and end apart: 17 -> 17, of which waited for: 10 -> 16; matrix products, arithmetic and copies ran while one was open for 1% -> 0% of each run, Pallas kernels for 17% -> 17%
where the time goes in v5:
time: 46.6 us; the launch traced here: 46.2 us
  starting transfers between devices  15.5 us (33%)
  waiting for transfers between devices  15 us (32%)
  Pallas kernels  12.1 us (26%)
  local copies, waits for them, and re-layouts  2.97 us (6%)
  between operations  0.75 us (2%)
    ppermute x11, waiting for transfers between devices, swap(): return lax.ppermute(value, axis, [(i, i ^ mask) for i in range(count)])  8.77 us
    ppermute x11, starting transfers between devices, swap(): return lax.ppermute(value, axis, [(i, i ^ mask) for i in range(count)])  8.47 us
    ppermute x6, starting transfers between devices, reduce_all(): parts.append(lax.ppermute(state, ('src', 'tgt'), pairs))  6.98 us
    ppermute x6, waiting for transfers between devices, reduce_all(): parts.append(lax.ppermute(state, ('src', 'tgt'), pairs))  6.21 us
    pallas_call x3, Pallas kernels, score(): pl.pallas_call(functools.partial(score_kernel, slot, len(parts)), out_sha...  5.57 us
    unnamed x12, local copies, waits for them, and re-layouts  2.95 us
    pallas_call x1, Pallas kernels, body(): pl.pallas_call(functools.partial(last_score_kernel, slots - 1, len(blocks...  1.86 us
    pallas_call x1, Pallas kernels, body(): pl.pallas_call(functools.partial(prepare_kernel, slots), out_shape=(unit_...  1.74 us
  transfers between devices with their start and end apart: 17, of which 16 were waited for; matrix products, arithmetic and copies ran while one was open for 0% of the time, Pallas kernels for 17%

profile of v5, /device:TPU:0, one launch (start us, length us, event | category | flops | bytes accessed | tf_op | source)
XLA Modules:
  0.0 46.2 jit_solution(15768829528322004960)
XLA Ops:
  1.1 2.6 %collective-permute-start = (bf16[256,1024]{1,0:T(8,128)(2,1)}, bf16[256,1024]{1,0:T(8,128)(2,1)S(1)}, u32[]{:S(2)}, u32[]{:S(2)}) collective-permute-start(bf16[256,1024]{1,0:T(8,128)(2,1)} %refs_0_.1), channel_id=1, source_target_pairs={{0,2},{1,3},{2,0},{3,1},{4,6},{5,7},{6,4},{7,5},{8,10},{9,11},{10,... | collective-permute-start | bytes 1572872 | tf_op jit(solution)/shard_map/ppermute | solution.py:263
  3.7 1.1 %copy-done = bf16[256,1024]{1,0:T(8,128)(2,1)S(1)} copy-done((bf16[256,1024]{1,0:T(8,128)(2,1)S(1)}, bf16[256,1024]{1,0:T(8,128)(2,1)}, u32[]{:S(2)}) %copy-start) | copy-done | bytes 524312
  4.8 1.6 %collective-permute-start.1 = (bf16[160,1024]{1,0:T(8,128)(2,1)S(1)}, bf16[160,1024]{1,0:T(8,128)(2,1)S(1)}, u32[]{:S(2)}, u32[]{:S(2)}) collective-permute-start(bf16[160,1024]{1,0:T(8,128)(2,1)S(1)} %get-tuple-element.46), channel_id=1, source_target_pairs={{0,4},{1,5},{2,6},{3,7},{4,0},{5,1},{6,2},{7,3},{8,12},{9,13},{10,... | collective-permute-start | bytes 983048 | tf_op jit(solution)/shard_map/ppermute | solution.py:263
  6.4 0.8 %collective-permute-start.4 = (bf16[96,1024]{1,0:T(8,128)(2,1)S(1)}, bf16[96,1024]{1,0:T(8,128)(2,1)S(1)}, u32[]{:S(2)}, u32[]{:S(2)}) collective-permute-start(bf16[96,1024]{1,0:T(8,128)(2,1)S(1)} %get-tuple-element.60), channel_id=1, source_target_pairs={{0,4},{1,5},{2,6},{3,7},{4,0},{5,1},{6,2},{7,3},{8,12},{9,13},{10,... | collective-permute-start | bytes 589832 | tf_op jit(solution)/shard_map/ppermute | solution.py:263
  7.6 1.2 %copy-done.2 = bf16[512,1024]{1,0:T(8,128)(2,1)S(1)} copy-done((bf16[512,1024]{1,0:T(8,128)(2,1)S(1)}, bf16[512,1024]{1,0:T(8,128)(2,1)}, u32[]{:S(2)}) %copy-start.2) | copy-done | bytes 1048600
  8.9 1.7 %prepare.1 = (bf16[512,1024]{1,0:T(8,128)(2,1)S(1)}, s32[1,128,128]{2,1,0:T(8,128)S(1)}, s32[1,128,128]{2,1,0:T(8,128)S(1)}, s32[16]{0:T(128)S(1)}) custom-call(bf16[512,1024]{1,0:T(8,128)(2,1)S(1)} %copy-done.2, s32[8,8]{1,0:T(8,128)S(1)} %copy-done.5, s32[16,2048]{1,0:T(8,128)S(1)} %bitcast.4, s32[16,512]{1,0:T(8,128)S(1)} %bitcast.6, ...), custom_call_target="tpu_custom_call" | custom-call | flops 1000 | bytes 1000 | tf_op jit(solution)/shard_map/prepare/pallas_call | solution.py:334
  11.7 1.9 %score_0.1 = (f32[256,1024]{1,0:T(8,128)S(1)}, f32[2,128]{1,0:T(2,128)S(1)}, f32[8,128]{1,0:T(8,128)S(1)}) custom-call(bf16[512,1024]{1,0:T(8,128)(2,1)S(1)} %get-tuple-element.48.own_ref, bf16[512,1024]{1,0:T(8,128)(2,1)S(1)} %normalise.1.sibling_ref, s32[1,128,128]{2,1,0:T(8,128)S(1)} %get-tuple-element.50.fwd_at_ref, ...), custom_call_target="tpu_custom_call" | custom-call | flops 1000 | bytes 1000 | tf_op jit(solution)/shard_map/score_0/pallas_call | solution.py:355
  13.5 1.9 %collective-permute-done.1.refs_1_ = bf16[160,1024]{1,0:T(8,128)(2,1)S(1)} collective-permute-done((bf16[160,1024]{1,0:T(8,128)(2,1)S(1)}, bf16[160,1024]{1,0:T(8,128)(2,1)S(1)}, u32[]{:S(2)}, u32[]{:S(2)}) %collective-permute-start.1) | collective-permute-done | bytes 327712 | tf_op jit(solution)/shard_map/ppermute | solution.py:263
  15.5 1.0 %collective-permute-done.refs_0_ = bf16[256,1024]{1,0:T(8,128)(2,1)S(1)} collective-permute-done((bf16[256,1024]{1,0:T(8,128)(2,1)}, bf16[256,1024]{1,0:T(8,128)(2,1)S(1)}, u32[]{:S(2)}, u32[]{:S(2)}) %collective-permute-start) | collective-permute-done | bytes 524320 | tf_op jit(solution)/shard_map/ppermute | solution.py:263
  16.5 1.9 %collective-permute-start.5 = (bf16[96,1024]{1,0:T(8,128)(2,1)S(1)}, bf16[96,1024]{1,0:T(8,128)(2,1)S(1)}, u32[]{:S(2)}, u32[]{:S(2)}) collective-permute-start(bf16[96,1024]{1,0:T(8,128)(2,1)S(1)} %slice.3), channel_id=1, source_target_pairs={{0,4},{1,5},{2,6},{3,7},{4,0},{5,1},{6,2},{7,3},{8,12},{9,13},{10,... | collective-permute-start | bytes 589832 | tf_op jit(solution)/shard_map/ppermute | solution.py:263
  18.9 1.9 %score_2.1 = (f32[256,1024]{1,0:T(8,128)S(1)}, f32[2,128]{1,0:T(2,128)S(1)}, f32[8,128]{1,0:T(8,128)S(1)}) custom-call(bf16[512,1024]{1,0:T(8,128)(2,1)S(1)} %get-tuple-element.48.own_ref, bf16[512,1024]{1,0:T(8,128)(2,1)S(1)} %normalise.1.sibling_ref, s32[1,128,128]{2,1,0:T(8,128)S(1)} %get-tuple-element.50.fwd_at_ref, ...), custom_call_target="tpu_custom_call" | custom-call | flops 1073741824 | bytes 1048576 | tf_op jit(solution)/shard_map/score_2/pallas_call | solution.py:355
  20.8 1.9 %score_1.1 = (f32[256,1024]{1,0:T(8,128)S(1)}, f32[2,128]{1,0:T(2,128)S(1)}, f32[8,128]{1,0:T(8,128)S(1)}) custom-call(bf16[512,1024]{1,0:T(8,128)(2,1)S(1)} %get-tuple-element.48.own_ref, bf16[512,1024]{1,0:T(8,128)(2,1)S(1)} %normalise.1.sibling_ref, s32[1,128,128]{2,1,0:T(8,128)S(1)} %get-tuple-element.50.fwd_at_ref, ...), custom_call_target="tpu_custom_call" | custom-call | flops 1073741824 | bytes 1048576 | tf_op jit(solution)/shard_map/score_1/pallas_call | solution.py:355
  23.6 1.9 %score_3.1 = (f32[256,1024]{1,0:T(8,128)S(1)}, f32[8,128]{1,0:T(8,128)S(1)}, f32[8,128]{1,0:T(8,128)S(1)}, f32[8,128]{1,0:T(8,128)S(1)}) custom-call(bf16[512,1024]{1,0:T(8,128)(2,1)S(1)} %get-tuple-element.48.own_ref, bf16[512,1024]{1,0:T(8,128)(2,1)S(1)} %normalise.1.sibling_ref, s32[1,128,128]{2,1,0:T(8,128)S(1)} %get-tuple-element.50.fwd_at_ref, ...), custom_call_target="tpu_custom_call" | custom-call | flops 1073741824 | bytes 1048576 | tf_op jit(solution)/shard_map/score_3/pallas_call | solution.py:383
  25.6 1.2 %collective-permute-done.7.got_ref = f32[8,128]{1,0:T(8,128)S(1)} collective-permute-done((f32[8,128]{1,0:T(8,128)S(1)}, f32[8,128]{1,0:T(8,128)S(1)}, u32[]{:S(2)}, u32[]{:S(2)}) %collective-permute-start.7) | collective-permute-done | bytes 4128 | tf_op jit(solution)/shard_map/ppermute | solution.py:263
  26.7 2.5 %collective-permute-start.10 = (f32[16,128]{1,0:T(8,128)S(1)}, f32[16,128]{1,0:T(8,128)S(1)}, u32[]{:S(2)}, u32[]{:S(2)}) collective-permute-start(f32[16,128]{1,0:T(8,128)S(1)} %mean_pair.1.state_ref), channel_id=1, source_target_pairs={{0,6},{1,25},{2,4},{3,27},{4,2},{5,29},{6,0},{7,31},{8,14},{9,17},... | collective-permute-start | bytes 24584 | tf_op jit(solution)/shard_map/ppermute | solution.py:291
  30.2 1.1 %collective-permute-done.10.refs_2_ = f32[16,128]{1,0:T(8,128)S(1)} collective-permute-done((f32[16,128]{1,0:T(8,128)S(1)}, f32[16,128]{1,0:T(8,128)S(1)}, u32[]{:S(2)}, u32[]{:S(2)}) %collective-permute-start.10) | collective-permute-done | bytes 8224 | tf_op jit(solution)/shard_map/ppermute | solution.py:291
  31.3 1.6 %collective-permute-done.9.refs_1_ = f32[16,128]{1,0:T(8,128)S(1)} collective-permute-done((f32[16,128]{1,0:T(8,128)S(1)}, f32[16,128]{1,0:T(8,128)S(1)}, u32[]{:S(2)}, u32[]{:S(2)}) %collective-permute-start.9) | collective-permute-done | bytes 8224 | tf_op jit(solution)/shard_map/ppermute | solution.py:291
  33.8 0.9 %collective-permute-done.11.got_ref = f32[8,128]{1,0:T(8,128)S(1)} collective-permute-done((f32[8,128]{1,0:T(8,128)S(1)}, f32[8,128]{1,0:T(8,128)S(1)}, u32[]{:S(2)}, u32[]{:S(2)}) %collective-permute-start.11) | collective-permute-done | bytes 4128 | tf_op jit(solution)/shard_map/ppermute | solution.py:263
  34.9 1.7 %margins.1 = (f32[8,128]{1,0:T(8,128)S(1)}, f32[8,128]{1,0:T(8,128)S(1)}, f32[8,128]{1,0:T(8,128)S(1)}) custom-call(f32[256,1024]{1,0:T(8,128)S(1)} %get-tuple-element.58.refs_0_, f32[256,1024]{1,0:T(8,128)S(1)} %get-tuple-element.66.refs_1_, f32[256,1024]{1,0:T(8,128)S(1)} %get-tuple-element.67.refs_2_, f32[256,1024]{1,0:T(8,128)S(1)} %get-tuple-element.74.refs_3_, ...), custom_call_target="tpu_custom_call" | custom-call | flops 10485760 | bytes 4194304 | tf_op jit(solution)/shard_map/margins/pallas_call | solution.py:398
  36.8 1.0 %collective-permute-done.12.got_ref = f32[8,128]{1,0:T(8,128)S(1)} collective-permute-done((f32[8,128]{1,0:T(8,128)S(1)}, f32[8,128]{1,0:T(8,128)S(1)}, u32[]{:S(2)}, u32[]{:S(2)}) %collective-permute-start.12) | collective-permute-done | bytes 4128 | tf_op jit(solution)/shard_map/ppermute | solution.py:263
  37.8 2.7 %collective-permute-start.15 = (f32[16,128]{1,0:T(8,128)S(1)}, f32[16,128]{1,0:T(8,128)S(1)}, u32[]{:S(2)}, u32[]{:S(2)}) collective-permute-start(f32[16,128]{1,0:T(8,128)S(1)} %best_pair.1.state_ref), channel_id=1, source_target_pairs={{0,6},{1,25},{2,4},{3,27},{4,2},{5,29},{6,0},{7,31},{8,14},{9,17},... | collective-permute-start | bytes 24584 | tf_op jit(solution)/shard_map/ppermute | solution.py:291
  41.3 1.1 %collective-permute-done.15.refs_2_ = f32[16,128]{1,0:T(8,128)S(1)} collective-permute-done((f32[16,128]{1,0:T(8,128)S(1)}, f32[16,128]{1,0:T(8,128)S(1)}, u32[]{:S(2)}, u32[]{:S(2)}) %collective-permute-start.15) | collective-permute-done | bytes 8224 | tf_op jit(solution)/shard_map/ppermute | solution.py:291
  42.4 1.8 %collective-permute-done.14.refs_1_ = f32[16,128]{1,0:T(8,128)S(1)} collective-permute-done((f32[16,128]{1,0:T(8,128)S(1)}, f32[16,128]{1,0:T(8,128)S(1)}, u32[]{:S(2)}, u32[]{:S(2)}) %collective-permute-start.14) | collective-permute-done | bytes 8224 | tf_op jit(solution)/shard_map/ppermute | solution.py:291
  44.8 0.8 %collective-permute-done.16.got_ref = f32[4,128]{1,0:T(4,128)S(1)} collective-permute-done((f32[4,128]{1,0:T(4,128)S(1)}, f32[4,128]{1,0:T(4,128)S(1)}, u32[]{:S(2)}, u32[]{:S(2)}) %collective-permute-start.16) | collective-permute-done | bytes 2080 | tf_op jit(solution)/shard_map/ppermute | solution.py:263
  (37 shorter events, 8.0 us)
Async XLA Ops:
  0.6 10.0 %collective-permute-start.3 = (bf16[512,1024]{1,0:T(8,128)(2,1)}, bf16[512,1024]{1,0:T(8,128)(2,1)S(1)}, u32[]{:S(2)}, u32[]{:S(2)}) collective-permute-start(bf16[512,1024]{1,0:T(8,128)(2,1)} %own_ref.1), channel_id=1, source_target_pairs={{0,1},{1,0},{2,3},{3,2},{4,5},{5,4},{6,7},{7,6},{8,9},{9,8},{10,11... | collective-permute-start | bytes 3145736 | tf_op jit(solution)/shard_map/ppermute | solution.py:263
  1.1 15.3 %collective-permute-start = (bf16[256,1024]{1,0:T(8,128)(2,1)}, bf16[256,1024]{1,0:T(8,128)(2,1)S(1)}, u32[]{:S(2)}, u32[]{:S(2)}) collective-permute-start(bf16[256,1024]{1,0:T(8,128)(2,1)} %refs_0_.1), channel_id=1, source_target_pairs={{0,2},{1,3},{2,0},{3,1},{4,6},{5,7},{6,4},{7,5},{8,10},{9,11},{10,... | collective-permute-start | bytes 1572872 | tf_op jit(solution)/shard_map/ppermute | solution.py:263
  3.7 1.1 %copy-start = (bf16[256,1024]{1,0:T(8,128)(2,1)S(1)}, bf16[256,1024]{1,0:T(8,128)(2,1)}, u32[]{:S(2)}) copy-start(bf16[256,1024]{1,0:T(8,128)(2,1)} %refs_0_.1) | copy-start | bytes 1572868
  4.8 1.6 %copy-start.4 = (s32[512,16]{0,1:T(8,128)S(1)}, s32[512,16]{0,1:T(8,128)}, u32[]{:S(2)}) copy-start(s32[512,16]{0,1:T(8,128)} %param.9) | copy-start | bytes 98308
  4.8 2.9 %copy-start.3 = (s32[2048,16]{0,1:T(8,128)S(1)}, s32[2048,16]{0,1:T(8,128)}, u32[]{:S(2)}) copy-start(s32[2048,16]{0,1:T(8,128)} %param.8) | copy-start | bytes 393220
  4.8 2.8 %copy-start.5 = (s32[8,8]{1,0:T(8,128)S(1)}, s32[8,8]{1,0:T(8,128)}, u32[]{:S(2)}) copy-start(s32[8,8]{1,0:T(8,128)} %pairs_ref.1) | copy-start | bytes 772
  4.8 10.6 %collective-permute-start.1 = (bf16[160,1024]{1,0:T(8,128)(2,1)S(1)}, bf16[160,1024]{1,0:T(8,128)(2,1)S(1)}, u32[]{:S(2)}, u32[]{:S(2)}) collective-permute-start(bf16[160,1024]{1,0:T(8,128)(2,1)S(1)} %get-tuple-element.46), channel_id=1, source_target_pairs={{0,4},{1,5},{2,6},{3,7},{4,0},{5,1},{6,2},{7,3},{8,12},{9,13},{10,... | collective-permute-start | bytes 983048 | tf_op jit(solution)/shard_map/ppermute | solution.py:263
  6.4 1.2 %collective-permute-start.2 = (s32[16,512]{1,0:T(8,128)S(1)}, s32[16,512]{1,0:T(8,128)S(1)}, u32[]{:S(2)}, u32[]{:S(2)}) collective-permute-start(s32[16,512]{1,0:T(8,128)S(1)} %bitcast.5), channel_id=1, source_target_pairs={{0,1},{1,0},{2,3},{3,2},{4,5},{5,4},{6,7},{7,6},{8,9},{9,8},{10,11... | collective-permute-start | bytes 98312 | tf_op jit(solution)/shard_map/ppermute | solution.py:263
  6.4 12.5 %collective-permute-start.4 = (bf16[96,1024]{1,0:T(8,128)(2,1)S(1)}, bf16[96,1024]{1,0:T(8,128)(2,1)S(1)}, u32[]{:S(2)}, u32[]{:S(2)}) collective-permute-start(bf16[96,1024]{1,0:T(8,128)(2,1)S(1)} %get-tuple-element.60), channel_id=1, source_target_pairs={{0,4},{1,5},{2,6},{3,7},{4,0},{5,1},{6,2},{7,3},{8,12},{9,13},{10,... | collective-permute-start | bytes 589832 | tf_op jit(solution)/shard_map/ppermute | solution.py:263
  7.6 1.2 %copy-start.2 = (bf16[512,1024]{1,0:T(8,128)(2,1)S(1)}, bf16[512,1024]{1,0:T(8,128)(2,1)}, u32[]{:S(2)}) copy-start(bf16[512,1024]{1,0:T(8,128)(2,1)} %own_ref.1) | copy-start | bytes 3145732
  10.6 1.0 %copy-start.1 = (bf16[256,1024]{1,0:T(8,128)(2,1)S(1)}, bf16[256,1024]{1,0:T(8,128)(2,1)}, u32[]{:S(2)}) copy-start(bf16[256,1024]{1,0:T(8,128)(2,1)} %refs_0_.1) | copy-start | bytes 1572868
  15.5 8.2 %collective-permute-start.6 = (bf16[160,1024]{1,0:T(8,128)(2,1)S(1)}, bf16[160,1024]{1,0:T(8,128)(2,1)S(1)}, u32[]{:S(2)}, u32[]{:S(2)}) collective-permute-start(bf16[160,1024]{1,0:T(8,128)(2,1)S(1)} %collective-permute-done.1.refs_1_), channel_id=1, source_target_pairs={{0,2},{1,3},{2,0},{3,1},{4,6},{5,7},{6,4},{7,5},{8,10},{9,11},{10,... | collective-permute-start | bytes 983048 | tf_op jit(solution)/shard_map/ppermute | solution.py:263
  16.5 6.7 %collective-permute-start.5 = (bf16[96,1024]{1,0:T(8,128)(2,1)S(1)}, bf16[96,1024]{1,0:T(8,128)(2,1)S(1)}, u32[]{:S(2)}, u32[]{:S(2)}) collective-permute-start(bf16[96,1024]{1,0:T(8,128)(2,1)S(1)} %slice.3), channel_id=1, source_target_pairs={{0,4},{1,5},{2,6},{3,7},{4,0},{5,1},{6,2},{7,3},{8,12},{9,13},{10,... | collective-permute-start | bytes 589832 | tf_op jit(solution)/shard_map/ppermute | solution.py:263
  25.5 1.2 %collective-permute-start.7 = (f32[8,128]{1,0:T(8,128)S(1)}, f32[8,128]{1,0:T(8,128)S(1)}, u32[]{:S(2)}, u32[]{:S(2)}) collective-permute-start(f32[8,128]{1,0:T(8,128)S(1)} %get-tuple-element.77), channel_id=1, source_target_pairs={{0,1},{1,0},{2,3},{3,2},{4,5},{5,4},{6,7},{7,6},{8,9},{9,8},{10,11... | collective-permute-start | bytes 12296 | tf_op jit(solution)/shard_map/ppermute | solution.py:263
  26.7 4.5 %collective-permute-start.10 = (f32[16,128]{1,0:T(8,128)S(1)}, f32[16,128]{1,0:T(8,128)S(1)}, u32[]{:S(2)}, u32[]{:S(2)}) collective-permute-start(f32[16,128]{1,0:T(8,128)S(1)} %mean_pair.1.state_ref), channel_id=1, source_target_pairs={{0,6},{1,25},{2,4},{3,27},{4,2},{5,29},{6,0},{7,31},{8,14},{9,17},... | collective-permute-start | bytes 24584 | tf_op jit(solution)/shard_map/ppermute | solution.py:291
  29.3 3.7 %collective-permute-start.9 = (f32[16,128]{1,0:T(8,128)S(1)}, f32[16,128]{1,0:T(8,128)S(1)}, u32[]{:S(2)}, u32[]{:S(2)}) collective-permute-start(f32[16,128]{1,0:T(8,128)S(1)} %mean_pair.1.state_ref), channel_id=1, source_target_pairs={{0,2},{1,17},{2,0},{3,19},{4,6},{5,21},{6,4},{7,23},{8,10},{9,25},... | collective-permute-start | bytes 24584 | tf_op jit(solution)/shard_map/ppermute | solution.py:291
  29.8 3.7 %collective-permute-start.8 = (f32[16,128]{1,0:T(8,128)S(1)}, f32[16,128]{1,0:T(8,128)S(1)}, u32[]{:S(2)}, u32[]{:S(2)}) collective-permute-start(f32[16,128]{1,0:T(8,128)S(1)} %mean_pair.1.state_ref), channel_id=1, source_target_pairs={{0,4},{1,9},{2,6},{3,11},{4,0},{5,13},{6,2},{7,15},{8,12},{9,1},{1... | collective-permute-start | bytes 24584 | tf_op jit(solution)/shard_map/ppermute | solution.py:291
  33.5 1.2 %collective-permute-start.11 = (f32[8,128]{1,0:T(8,128)S(1)}, f32[8,128]{1,0:T(8,128)S(1)}, u32[]{:S(2)}, u32[]{:S(2)}) collective-permute-start(f32[8,128]{1,0:T(8,128)S(1)} %get-tuple-element.79), channel_id=1, source_target_pairs={{0,1},{1,0},{2,3},{3,2},{4,5},{5,4},{6,7},{7,6},{8,9},{9,8},{10,11... | collective-permute-start | bytes 12296 | tf_op jit(solution)/shard_map/ppermute | solution.py:263
  36.6 1.2 %collective-permute-start.12 = (f32[8,128]{1,0:T(8,128)S(1)}, f32[8,128]{1,0:T(8,128)S(1)}, u32[]{:S(2)}, u32[]{:S(2)}) collective-permute-start(f32[8,128]{1,0:T(8,128)S(1)} %get-tuple-element.85), channel_id=1, source_target_pairs={{0,1},{1,0},{2,3},{3,2},{4,5},{5,4},{6,7},{7,6},{8,9},{9,8},{10,11... | collective-permute-start | bytes 12296 | tf_op jit(solution)/shard_map/ppermute | solution.py:263
  37.8 4.5 %collective-permute-start.15 = (f32[16,128]{1,0:T(8,128)S(1)}, f32[16,128]{1,0:T(8,128)S(1)}, u32[]{:S(2)}, u32[]{:S(2)}) collective-permute-start(f32[16,128]{1,0:T(8,128)S(1)} %best_pair.1.state_ref), channel_id=1, source_target_pairs={{0,6},{1,25},{2,4},{3,27},{4,2},{5,29},{6,0},{7,31},{8,14},{9,17},... | collective-permute-start | bytes 24584 | tf_op jit(solution)/shard_map/ppermute | solution.py:291
  40.5 3.7 %collective-permute-start.14 = (f32[16,128]{1,0:T(8,128)S(1)}, f32[16,128]{1,0:T(8,128)S(1)}, u32[]{:S(2)}, u32[]{:S(2)}) collective-permute-start(f32[16,128]{1,0:T(8,128)S(1)} %best_pair.1.state_ref), channel_id=1, source_target_pairs={{0,2},{1,17},{2,0},{3,19},{4,6},{5,21},{6,4},{7,23},{8,10},{9,25},... | collective-permute-start | bytes 24584 | tf_op jit(solution)/shard_map/ppermute | solution.py:291
  40.6 3.7 %collective-permute-start.13 = (f32[16,128]{1,0:T(8,128)S(1)}, f32[16,128]{1,0:T(8,128)S(1)}, u32[]{:S(2)}, u32[]{:S(2)}) collective-permute-start(f32[16,128]{1,0:T(8,128)S(1)} %best_pair.1.state_ref), channel_id=1, source_target_pairs={{0,4},{1,9},{2,6},{3,11},{4,0},{5,13},{6,2},{7,15},{8,12},{9,1},{1... | collective-permute-start | bytes 24584 | tf_op jit(solution)/shard_map/ppermute | solution.py:291
  44.3 1.3 %collective-permute-start.16 = (f32[4,128]{1,0:T(4,128)S(1)}, f32[4,128]{1,0:T(4,128)S(1)}, u32[]{:S(2)}, u32[]{:S(2)}) collective-permute-start(f32[4,128]{1,0:T(4,128)S(1)} %get-tuple-element.87), channel_id=1, source_target_pairs={{0,1},{1,0},{2,3},{3,2},{4,5},{5,4},{6,7},{7,6},{8,9},{9,8},{10,11... | collective-permute-start | bytes 6152 | tf_op jit(solution)/shard_map/ppermute | solution.py:263

commit v6 on v5

--- a/solution.py
+++ b/solution.py
@@ -97,12 +97,17 @@
     return lax.broadcasted_iota(jnp.int32, (8, LANES), 1) // 16
 
 
-def forward_part(slot, unit, own_ref, sibling_ref, fwd_at_ref, scores_ref, got_ref):
+def score_rows(unit, own_ref, sibling_ref, scores_ref):
     rows = own_ref.shape[0]
     for i, ref in enumerate((own_ref, sibling_ref)):
         scores_ref[:, i * rows : (i + 1) * rows] = lax.dot_general(
             unit, ref[...], ROWS_CONTRACT, preferred_element_type=jnp.float32
         )
+
+
+def forward_part(slot, unit, own_ref, sibling_ref, fwd_at_ref, scores_ref, got_ref):
+    rows = own_ref.shape[0]
+    score_rows(unit, own_ref, sibling_ref, scores_ref)
     lane_tile = lane_tiles()
     for at in range(0, LANES, 8):
         near = fwd_at_ref[(2 * slot) // 8, at : at + 8, :]
@@ -147,19 +152,43 @@
     bwd_ref[...] = backward_part(slot, unit, own_ref, sibling_ref, bwd_at_ref, turned_ref, back_ref)
 
 
-def last_score_kernel(slot, parts, own_ref, sibling_ref, fwd_at_ref, bwd_at_ref, *refs):
+def last_first_kernel(slot, parts, own_ref, sibling_ref, fwd_at_ref, bwd_at_ref, *refs):
     chunk_refs, refs = refs[:parts], refs[parts:]
     fwd_before, bwd_before = refs[:slot], refs[slot : 2 * slot]
-    scores_ref, fwd_ref, bwd_ref, send_ref, turned_ref, got_ref, back_ref = refs[2 * slot :]
-    unit = jnp.concatenate([unit_rows(ref[...]) for ref in chunk_refs], axis=0)
-    for i, ref in enumerate(fwd_before):
-        fwd_ref[2 * i : 2 * i + 2, :] = ref[...]
-    fwd_ref[2 * slot :, :] = forward_part(slot, unit, own_ref, sibling_ref, fwd_at_ref, scores_ref, got_ref)
-    bwd = backward_part(slot, unit, own_ref, sibling_ref, bwd_at_ref, turned_ref, back_ref)
+    unit_ref, scores_ref, send_ref, keep_ref, turned_ref, got_ref = refs[2 * slot :]
+    unit_ref[...] = jnp.concatenate([unit_rows(ref[...]) for ref in chunk_refs], axis=0)
+    odd = lax.axis_index("tgt") % 2 == 1
+    rows = send_ref.shape[0]
+
+    @pl.when(odd)
+    def _():
+        fwd = forward_part(slot, unit_ref[...], own_ref, sibling_ref, fwd_at_ref, scores_ref, got_ref)
+        send_ref[...] = fit(jnp.concatenate([*(ref[...] for ref in fwd_before), fwd], axis=0), rows)
+
+    bwd = backward_part(slot, unit_ref[...], own_ref, sibling_ref, bwd_at_ref, turned_ref, got_ref)
     for ref in bwd_before:
         bwd = bwd + ref[...]
-    bwd_ref[...] = bwd
-    send_ref[...] = choose(fwd_ref[...], bwd, send_ref.shape[0])
+    keep_ref[...] = fit(bwd, rows)
+
+    @pl.when(jnp.logical_not(odd))
+    def _():
+        send_ref[...] = fit(bwd, rows)
+
+
+def last_second_kernel(slot, own_ref, sibling_ref, fwd_at_ref, unit_ref, first_scores_ref, *refs):
+    fwd_before, (scores_ref, keep_ref, got_ref) = refs[:slot], refs[slot:]
+    rows = keep_ref.shape[0]
+    odd = lax.axis_index("tgt") % 2 == 1
+
+    @pl.when(odd)
+    def _():
+        scores_ref[...] = first_scores_ref[...]
+        keep_ref[...] = jnp.zeros_like(keep_ref)
+
+    @pl.when(jnp.logical_not(odd))
+    def _():
+        fwd = forward_part(slot, unit_ref[...], own_ref, sibling_ref, fwd_at_ref, scores_ref, got_ref)
+        keep_ref[...] = fit(jnp.concatenate([*(ref[...] for ref in fwd_before), fwd], axis=0), rows)
 
 
 def fit(value, rows):
@@ -186,6 +215,12 @@
     high, wide = by_src_ref.shape[0], by_tgt_ref.shape[0]
     by_src = jnp.concatenate([by_src_ref[...], got_ref[:high, :]], axis=0)
     by_tgt = combine(by_tgt_ref[...], turn_pair(got_ref[:wide, :]))
+    state_ref[...] = choose(by_tgt, by_src, state_ref.shape[0])
+
+
+def pair_kept_kernel(high, wide, by_tgt_ref, by_src_ref, got_ref, state_ref):
+    by_src = jnp.concatenate([by_src_ref[:high, :], got_ref[:high, :]], axis=0)
+    by_tgt = by_tgt_ref[:wide, :] + turn_pair(got_ref[:wide, :])
     state_ref[...] = choose(by_tgt, by_src, state_ref.shape[0])
 
 
@@ -274,12 +309,8 @@
     )(*args)
 
 
-def reduce_all(combine, by_src, by_tgt, send, name, last):
+def reduce_all(combine, high, wide, state, name, last):
     tgt_count, src_count = lax.axis_size("tgt"), lax.axis_size("src")
-    high, wide = by_src.shape[0], by_tgt.shape[0]
-    got = swap(send, "tgt", 1)
-    rows = max(2 * high, wide)
-    (state,) = small_call(functools.partial(pair_kernel, combine), name + "_pair", (rows,), by_src, by_tgt, got)
     parts = []
     for i in range(1, max(tgt_count // 2, src_count)):
         pairs = []
@@ -291,7 +322,7 @@
         parts.append(lax.ppermute(state, ("src", "tgt"), pairs))
     back = max(2, wide // 2) if last else max(high, wide)
     total, send = small_call(
-        functools.partial(collect_kernel, combine, high // 2, wide, last), name + "_collect", (rows, back), state, *parts
+        functools.partial(collect_kernel, combine, high // 2, wide, last), name, (state.shape[0], back), state, *parts
     )
     return total, swap(send, "tgt", 1)
 
@@ -377,35 +408,54 @@
     done += [score(1, (along_x,)), along_y]
     for slot in range(3, slots - 1):
         done.append(score(slot, blocks[slot]))
-    args = [own_unit, sibling_unit, fwd_at, bwd_at, *blocks[-1], *(d[1] for d in done), *(d[2] for d in done)]
-    fwd_sums = jax.ShapeDtypeStruct((2 * slots, LANES), jnp.float32)
-    sent = jax.ShapeDtypeStruct((max(2 * slots, columns // LANES), LANES), jnp.float32)
-    last_scores, fwd, bwd, send = pl.pallas_call(
-        functools.partial(last_score_kernel, slots - 1, len(blocks[-1])),
-        out_shape=(scores_shape, fwd_sums, bwd_sums, sent),
+    high, wide = 2 * slots, columns // LANES
+    sent = jax.ShapeDtypeStruct((max(high, wide), LANES), jnp.float32)
+    before = [*(d[1] for d in done), *(d[2] for d in done)]
+    args = [own_unit, sibling_unit, fwd_at, bwd_at, *blocks[-1], *before]
+    last_unit, last_scores, send, keep_tgt = pl.pallas_call(
+        functools.partial(last_first_kernel, slots - 1, len(blocks[-1])),
+        out_shape=(jax.ShapeDtypeStruct((BLOCK, width), jnp.bfloat16), scores_shape, sent, sent),
         in_specs=[VMEM] * len(args),
         out_specs=(VMEM,) * 4,
-        scratch_shapes=[turned, got, got],
-        name=f"score_{slots - 1}",
-        **params(4 * BLOCK * columns * width, BLOCK * columns * 4),
+        scratch_shapes=[turned, got],
+        name="last_first",
+        **params(2 * BLOCK * columns * width, BLOCK * columns * 4),
+    )(*args)
+    got_sums = swap(send, "tgt", 1)
+    args = [own_unit, sibling_unit, fwd_at, last_unit, last_scores, *(d[1] for d in done)]
+    last_scores, keep_src = pl.pallas_call(
+        functools.partial(last_second_kernel, slots - 1),
+        out_shape=(scores_shape, sent),
+        in_specs=[VMEM] * len(args),
+        out_specs=(VMEM, VMEM),
+        input_output_aliases={4: 0},
+        scratch_shapes=[got],
+        name="last_second",
+        **params(2 * BLOCK * columns * width, BLOCK * columns * 4),
     )(*args)
     scores = [*(d[0] for d in done), last_scores]
 
-    total, got = reduce_all(jnp.add, fwd, bwd, send, "mean", False)
-    wide, bwd = small_call(
-        functools.partial(widen_kernel, columns // LANES), "widen", (slots * BLOCK, columns // LANES), total, got
+    state_rows = max(2 * high, wide)
+    (state,) = small_call(
+        functools.partial(pair_kept_kernel, high, wide), "mean_pair", (state_rows,), keep_tgt, keep_src, got_sums
     )
+    total, got_sums = reduce_all(jnp.add, high, wide, state, "mean_collect", False)
+    wide_fwd, bwd = small_call(functools.partial(widen_kernel, wide), "widen", (slots * BLOCK, wide), total, got_sums)
     src_best, tgt_best, send = pl.pallas_call(
         functools.partial(margin_kernel, slots, columns),
-        out_shape=(fwd_sums, bwd_sums, sent),
+        out_shape=(jax.ShapeDtypeStruct((high, LANES), jnp.float32), bwd_sums, sent),
         in_specs=[VMEM] * (slots + 2) + [SMEM],
         out_specs=(VMEM,) * 3,
         scratch_shapes=[pltpu.VMEM((slots * BLOCK, LANES), jnp.float32), pltpu.VMEM((8, columns), jnp.float32)],
         name="margins",
         **params(slots * BLOCK * columns * 10, slots * BLOCK * columns * 4),
-    )(*scores, wide, bwd, listed)
-    total, got = reduce_all(jnp.maximum, src_best, tgt_best, send, "best", True)
-    src_best, tgt_best = small_call(last_kernel, "last", (BLOCK // LANES, rows // LANES), total, got)
+    )(*scores, wide_fwd, bwd, listed)
+    got_best = swap(send, "tgt", 1)
+    (state,) = small_call(
+        functools.partial(pair_kernel, jnp.maximum), "best_pair", (state_rows,), src_best, tgt_best, got_best
+    )
+    total, got_best = reduce_all(jnp.maximum, high, wide, state, "best_collect", True)
+    src_best, tgt_best = small_call(last_kernel, "last", (BLOCK // LANES, rows // LANES), total, got_best)
     return src_best.reshape(-1), tgt_best.reshape(-1)
 
 

time: 46.6 us -> 46.1 us (0.989)
  waiting for transfers between devices: 15 us -> 14 us
    ppermute x11, waiting for transfers between devices: 8.77 us -> 7.62 us  [swap(): return lax.ppermute(value, axis, [(i, i ^ mask) for i in range(count)])]
    pallas_call x1 -> x2, Pallas kernels: 1.86 us -> 2.4 us  [the longest x1 1.38 us: body(): pl.pallas_call(functools.partial(last_first_kernel, slots - 1, len(blocks...]
  transfers between devices with their start and end apart: 17 -> 17, of which waited for: 16 -> 16; matrix products, arithmetic and copies ran while one was open for 0% -> 0% of each run, Pallas kernels for 17% -> 19%
where the time goes in v6:
time: 46.1 us; the launch traced here: 45.7 us
  starting transfers between devices  15.8 us (34%)
  waiting for transfers between devices  14 us (30%)
  Pallas kernels  12.2 us (26%)
  local copies, waits for them, and re-layouts  2.97 us (6%)
  between operations  0.76 us (2%)
    ppermute x11, starting transfers between devices, swap(): return lax.ppermute(value, axis, [(i, i ^ mask) for i in range(count)])  8.71 us
    ppermute x11, waiting for transfers between devices, swap(): return lax.ppermute(value, axis, [(i, i ^ mask) for i in range(count)])  7.62 us
    ppermute x6, starting transfers between devices, reduce_all(): parts.append(lax.ppermute(state, ('src', 'tgt'), pairs))  7.07 us
    ppermute x6, waiting for transfers between devices, reduce_all(): parts.append(lax.ppermute(state, ('src', 'tgt'), pairs))  6.36 us
    pallas_call x3, Pallas kernels, score(): pl.pallas_call(functools.partial(score_kernel, slot, len(parts)), out_sha...  5.53 us
    unnamed x12, local copies, waits for them, and re-layouts  2.95 us
    pallas_call x1, Pallas kernels, body(): pl.pallas_call(functools.partial(prepare_kernel, slots), out_shape=(unit_...  1.74 us
    pallas_call x1, Pallas kernels, body(): pl.pallas_call(functools.partial(last_first_kernel, slots - 1, len(blocks...  1.38 us
  transfers between devices with their start and end apart: 17, of which 16 were waited for; matrix products, arithmetic and copies ran while one was open for 0% of the time, Pallas kernels for 19%

profile of v6, /device:TPU:0, one launch (start us, length us, event | category | flops | bytes accessed | tf_op | source)
XLA Modules:
  0.0 45.7 jit_solution(11749747902841722945)
XLA Ops:
  1.1 2.6 %collective-permute-start = (bf16[256,1024]{1,0:T(8,128)(2,1)}, bf16[256,1024]{1,0:T(8,128)(2,1)S(1)}, u32[]{:S(2)}, u32[]{:S(2)}) collective-permute-start(bf16[256,1024]{1,0:T(8,128)(2,1)} %refs_0_.1), channel_id=1, source_target_pairs={{0,2},{1,3},{2,0},{3,1},{4,6},{5,7},{6,4},{7,5},{8,10},{9,11},{10,... | collective-permute-start | bytes 1572872 | tf_op jit(solution)/shard_map/ppermute | solution.py:298
  3.7 1.1 %copy-done = bf16[256,1024]{1,0:T(8,128)(2,1)S(1)} copy-done((bf16[256,1024]{1,0:T(8,128)(2,1)S(1)}, bf16[256,1024]{1,0:T(8,128)(2,1)}, u32[]{:S(2)}) %copy-start) | copy-done | bytes 524312
  4.8 1.6 %collective-permute-start.1 = (bf16[160,1024]{1,0:T(8,128)(2,1)S(1)}, bf16[160,1024]{1,0:T(8,128)(2,1)S(1)}, u32[]{:S(2)}, u32[]{:S(2)}) collective-permute-start(bf16[160,1024]{1,0:T(8,128)(2,1)S(1)} %get-tuple-element.48), channel_id=1, source_target_pairs={{0,4},{1,5},{2,6},{3,7},{4,0},{5,1},{6,2},{7,3},{8,12},{9,13},{10,... | collective-permute-start | bytes 983048 | tf_op jit(solution)/shard_map/ppermute | solution.py:298
  6.4 0.8 %collective-permute-start.4 = (bf16[96,1024]{1,0:T(8,128)(2,1)S(1)}, bf16[96,1024]{1,0:T(8,128)(2,1)S(1)}, u32[]{:S(2)}, u32[]{:S(2)}) collective-permute-start(bf16[96,1024]{1,0:T(8,128)(2,1)S(1)} %get-tuple-element.62), channel_id=1, source_target_pairs={{0,4},{1,5},{2,6},{3,7},{4,0},{5,1},{6,2},{7,3},{8,12},{9,13},{10,... | collective-permute-start | bytes 589832 | tf_op jit(solution)/shard_map/ppermute | solution.py:298
  7.6 1.2 %copy-done.2 = bf16[512,1024]{1,0:T(8,128)(2,1)S(1)} copy-done((bf16[512,1024]{1,0:T(8,128)(2,1)S(1)}, bf16[512,1024]{1,0:T(8,128)(2,1)}, u32[]{:S(2)}) %copy-start.2) | copy-done | bytes 1048600
  8.9 1.7 %prepare.1 = (bf16[512,1024]{1,0:T(8,128)(2,1)S(1)}, s32[1,128,128]{2,1,0:T(8,128)S(1)}, s32[1,128,128]{2,1,0:T(8,128)S(1)}, s32[16]{0:T(128)S(1)}) custom-call(bf16[512,1024]{1,0:T(8,128)(2,1)S(1)} %copy-done.2, s32[8,8]{1,0:T(8,128)S(1)} %copy-done.5, s32[16,2048]{1,0:T(8,128)S(1)} %bitcast.4, s32[16,512]{1,0:T(8,128)S(1)} %bitcast.6, ...), custom_call_target="tpu_custom_call" | custom-call | flops 1000 | bytes 1000 | tf_op jit(solution)/shard_map/prepare/pallas_call | solution.py:365
  11.7 1.8 %score_0.1 = (f32[256,1024]{1,0:T(8,128)S(1)}, f32[2,128]{1,0:T(2,128)S(1)}, f32[8,128]{1,0:T(8,128)S(1)}) custom-call(bf16[512,1024]{1,0:T(8,128)(2,1)S(1)} %get-tuple-element.50.own_ref, bf16[512,1024]{1,0:T(8,128)(2,1)S(1)} %normalise.1.sibling_ref, s32[1,128,128]{2,1,0:T(8,128)S(1)} %get-tuple-element.52.fwd_at_ref, ...), custom_call_target="tpu_custom_call" | custom-call | flops 1000 | bytes 1000 | tf_op jit(solution)/shard_map/score_0/pallas_call | solution.py:386
  13.5 2.0 %collective-permute-done.1.refs_1_ = bf16[160,1024]{1,0:T(8,128)(2,1)S(1)} collective-permute-done((bf16[160,1024]{1,0:T(8,128)(2,1)S(1)}, bf16[160,1024]{1,0:T(8,128)(2,1)S(1)}, u32[]{:S(2)}, u32[]{:S(2)}) %collective-permute-start.1) | collective-permute-done | bytes 327712 | tf_op jit(solution)/shard_map/ppermute | solution.py:298
  15.5 1.0 %collective-permute-done.refs_0_ = bf16[256,1024]{1,0:T(8,128)(2,1)S(1)} collective-permute-done((bf16[256,1024]{1,0:T(8,128)(2,1)}, bf16[256,1024]{1,0:T(8,128)(2,1)S(1)}, u32[]{:S(2)}, u32[]{:S(2)}) %collective-permute-start) | collective-permute-done | bytes 524320 | tf_op jit(solution)/shard_map/ppermute | solution.py:298
  16.5 1.9 %collective-permute-start.5 = (bf16[96,1024]{1,0:T(8,128)(2,1)S(1)}, bf16[96,1024]{1,0:T(8,128)(2,1)S(1)}, u32[]{:S(2)}, u32[]{:S(2)}) collective-permute-start(bf16[96,1024]{1,0:T(8,128)(2,1)S(1)} %slice.3), channel_id=1, source_target_pairs={{0,4},{1,5},{2,6},{3,7},{4,0},{5,1},{6,2},{7,3},{8,12},{9,13},{10,... | collective-permute-start | bytes 589832 | tf_op jit(solution)/shard_map/ppermute | solution.py:298
  18.9 1.8 %score_2.1 = (f32[256,1024]{1,0:T(8,128)S(1)}, f32[2,128]{1,0:T(2,128)S(1)}, f32[8,128]{1,0:T(8,128)S(1)}) custom-call(bf16[512,1024]{1,0:T(8,128)(2,1)S(1)} %get-tuple-element.50.own_ref, bf16[512,1024]{1,0:T(8,128)(2,1)S(1)} %normalise.1.sibling_ref, s32[1,128,128]{2,1,0:T(8,128)S(1)} %get-tuple-element.52.fwd_at_ref, ...), custom_call_target="tpu_custom_call" | custom-call | flops 1073741824 | bytes 1048576 | tf_op jit(solution)/shard_map/score_2/pallas_call | solution.py:386
  20.7 1.8 %score_1.1 = (f32[256,1024]{1,0:T(8,128)S(1)}, f32[2,128]{1,0:T(2,128)S(1)}, f32[8,128]{1,0:T(8,128)S(1)}) custom-call(bf16[512,1024]{1,0:T(8,128)(2,1)S(1)} %get-tuple-element.50.own_ref, bf16[512,1024]{1,0:T(8,128)(2,1)S(1)} %normalise.1.sibling_ref, s32[1,128,128]{2,1,0:T(8,128)S(1)} %get-tuple-element.52.fwd_at_ref, ...), custom_call_target="tpu_custom_call" | custom-call | flops 1073741824 | bytes 1048576 | tf_op jit(solution)/shard_map/score_1/pallas_call | solution.py:386
  23.6 1.4 %last_first.1 = (bf16[256,1024]{1,0:T(8,128)(2,1)S(1)}, f32[256,1024]{1,0:T(8,128)S(1)}, f32[8,128]{1,0:T(8,128)S(1)}, f32[8,128]{1,0:T(8,128)S(1)}) custom-call(bf16[512,1024]{1,0:T(8,128)(2,1)S(1)} %get-tuple-element.50.own_ref, bf16[512,1024]{1,0:T(8,128)(2,1)S(1)} %normalise.1.sibling_ref, s32[1,128,128]{2,1,0:T(8,128)S(1)} %get-tuple-element.52.fwd_at_ref, ...), custom_call_target="tpu_custom_call" | custom-call | flops 536870912 | bytes 1048576 | tf_op jit(solution)/shard_map/last_first/pallas_call | solution.py:415
  25.1 1.0 %last_second.1 = (f32[256,1024]{1,0:T(8,128)S(1)}, f32[8,128]{1,0:T(8,128)S(1)}) custom-call(bf16[512,1024]{1,0:T(8,128)(2,1)S(1)} %get-tuple-element.50.own_ref, bf16[512,1024]{1,0:T(8,128)(2,1)S(1)} %normalise.1.sibling_ref, s32[1,128,128]{2,1,0:T(8,128)S(1)} %get-tuple-element.52.fwd_at_ref, ...), custom_call_target="tpu_custom_call", output_to_operand_aliasing={{0}: (4, {})} | custom-call | flops 536870912 | bytes 1048576 | tf_op jit(solution)/shard_map/last_second/pallas_call | solution.py:426
  26.3 2.5 %collective-permute-start.10 = (f32[16,128]{1,0:T(8,128)S(1)}, f32[16,128]{1,0:T(8,128)S(1)}, u32[]{:S(2)}, u32[]{:S(2)}) collective-permute-start(f32[16,128]{1,0:T(8,128)S(1)} %mean_pair.1.state_ref), channel_id=1, source_target_pairs={{0,6},{1,25},{2,4},{3,27},{4,2},{5,29},{6,0},{7,31},{8,14},{9,17},... | collective-permute-start | bytes 24584 | tf_op jit(solution)/shard_map/ppermute | solution.py:322
  29.8 1.1 %collective-permute-done.10.refs_2_ = f32[16,128]{1,0:T(8,128)S(1)} collective-permute-done((f32[16,128]{1,0:T(8,128)S(1)}, f32[16,128]{1,0:T(8,128)S(1)}, u32[]{:S(2)}, u32[]{:S(2)}) %collective-permute-start.10) | collective-permute-done | bytes 8224 | tf_op jit(solution)/shard_map/ppermute | solution.py:322
  30.8 1.6 %collective-permute-done.9.refs_1_ = f32[16,128]{1,0:T(8,128)S(1)} collective-permute-done((f32[16,128]{1,0:T(8,128)S(1)}, f32[16,128]{1,0:T(8,128)S(1)}, u32[]{:S(2)}, u32[]{:S(2)}) %collective-permute-start.9) | collective-permute-done | bytes 8224 | tf_op jit(solution)/shard_map/ppermute | solution.py:322
  33.3 0.9 %collective-permute-done.11.got_ref = f32[8,128]{1,0:T(8,128)S(1)} collective-permute-done((f32[8,128]{1,0:T(8,128)S(1)}, f32[8,128]{1,0:T(8,128)S(1)}, u32[]{:S(2)}, u32[]{:S(2)}) %collective-permute-start.11) | collective-permute-done | bytes 4128 | tf_op jit(solution)/shard_map/ppermute | solution.py:298
  34.4 1.3 %margins.1 = (f32[8,128]{1,0:T(8,128)S(1)}, f32[8,128]{1,0:T(8,128)S(1)}, f32[8,128]{1,0:T(8,128)S(1)}) custom-call(f32[256,1024]{1,0:T(8,128)S(1)} %get-tuple-element.60.refs_0_, f32[256,1024]{1,0:T(8,128)S(1)} %get-tuple-element.68.refs_1_, f32[256,1024]{1,0:T(8,128)S(1)} %get-tuple-element.69.refs_2_, f32[256,1024]{1,0:T(8,128)S(1)} %get-tuple-element.78.refs_3_, ...), custom_call_target="tpu_custom_call" | custom-call | flops 10485760 | bytes 4194304 | tf_op jit(solution)/shard_map/margins/pallas_call | solution.py:444
  36.3 0.8 %collective-permute-done.12.got_ref = f32[8,128]{1,0:T(8,128)S(1)} collective-permute-done((f32[8,128]{1,0:T(8,128)S(1)}, f32[8,128]{1,0:T(8,128)S(1)}, u32[]{:S(2)}, u32[]{:S(2)}) %collective-permute-start.12) | collective-permute-done | bytes 4128 | tf_op jit(solution)/shard_map/ppermute | solution.py:298
  37.1 2.6 %collective-permute-start.15 = (f32[16,128]{1,0:T(8,128)S(1)}, f32[16,128]{1,0:T(8,128)S(1)}, u32[]{:S(2)}, u32[]{:S(2)}) collective-permute-start(f32[16,128]{1,0:T(8,128)S(1)} %best_pair.1.state_ref), channel_id=1, source_target_pairs={{0,6},{1,25},{2,4},{3,27},{4,2},{5,29},{6,0},{7,31},{8,14},{9,17},... | collective-permute-start | bytes 24584 | tf_op jit(solution)/shard_map/ppermute | solution.py:322
  40.7 1.0 %collective-permute-done.15.refs_2_ = f32[16,128]{1,0:T(8,128)S(1)} collective-permute-done((f32[16,128]{1,0:T(8,128)S(1)}, f32[16,128]{1,0:T(8,128)S(1)}, u32[]{:S(2)}, u32[]{:S(2)}) %collective-permute-start.15) | collective-permute-done | bytes 8224 | tf_op jit(solution)/shard_map/ppermute | solution.py:322
  41.6 1.7 %collective-permute-done.14.refs_1_ = f32[16,128]{1,0:T(8,128)S(1)} collective-permute-done((f32[16,128]{1,0:T(8,128)S(1)}, f32[16,128]{1,0:T(8,128)S(1)}, u32[]{:S(2)}, u32[]{:S(2)}) %collective-permute-start.14) | collective-permute-done | bytes 8224 | tf_op jit(solution)/shard_map/ppermute | solution.py:322
  44.3 0.8 %collective-permute-done.16.got_ref = f32[4,128]{1,0:T(4,128)S(1)} collective-permute-done((f32[4,128]{1,0:T(4,128)S(1)}, f32[4,128]{1,0:T(4,128)S(1)}, u32[]{:S(2)}, u32[]{:S(2)}) %collective-permute-start.16) | collective-permute-done | bytes 2080 | tf_op jit(solution)/shard_map/ppermute | solution.py:298
  (38 shorter events, 8.9 us)
Async XLA Ops:
  0.6 10.0 %collective-permute-start.3 = (bf16[512,1024]{1,0:T(8,128)(2,1)}, bf16[512,1024]{1,0:T(8,128)(2,1)S(1)}, u32[]{:S(2)}, u32[]{:S(2)}) collective-permute-start(bf16[512,1024]{1,0:T(8,128)(2,1)} %own_ref.1), channel_id=1, source_target_pairs={{0,1},{1,0},{2,3},{3,2},{4,5},{5,4},{6,7},{7,6},{8,9},{9,8},{10,11... | collective-permute-start | bytes 3145736 | tf_op jit(solution)/shard_map/ppermute | solution.py:298
  1.1 15.3 %collective-permute-start = (bf16[256,1024]{1,0:T(8,128)(2,1)}, bf16[256,1024]{1,0:T(8,128)(2,1)S(1)}, u32[]{:S(2)}, u32[]{:S(2)}) collective-permute-start(bf16[256,1024]{1,0:T(8,128)(2,1)} %refs_0_.1), channel_id=1, source_target_pairs={{0,2},{1,3},{2,0},{3,1},{4,6},{5,7},{6,4},{7,5},{8,10},{9,11},{10,... | collective-permute-start | bytes 1572872 | tf_op jit(solution)/shard_map/ppermute | solution.py:298
  3.7 1.1 %copy-start = (bf16[256,1024]{1,0:T(8,128)(2,1)S(1)}, bf16[256,1024]{1,0:T(8,128)(2,1)}, u32[]{:S(2)}) copy-start(bf16[256,1024]{1,0:T(8,128)(2,1)} %refs_0_.1) | copy-start | bytes 1572868
  4.8 1.6 %copy-start.4 = (s32[512,16]{0,1:T(8,128)S(1)}, s32[512,16]{0,1:T(8,128)}, u32[]{:S(2)}) copy-start(s32[512,16]{0,1:T(8,128)} %param.9) | copy-start | bytes 98308
  4.8 2.9 %copy-start.3 = (s32[2048,16]{0,1:T(8,128)S(1)}, s32[2048,16]{0,1:T(8,128)}, u32[]{:S(2)}) copy-start(s32[2048,16]{0,1:T(8,128)} %param.8) | copy-start | bytes 393220
  4.8 2.8 %copy-start.5 = (s32[8,8]{1,0:T(8,128)S(1)}, s32[8,8]{1,0:T(8,128)}, u32[]{:S(2)}) copy-start(s32[8,8]{1,0:T(8,128)} %pairs_ref.1) | copy-start | bytes 772
  4.8 10.6 %collective-permute-start.1 = (bf16[160,1024]{1,0:T(8,128)(2,1)S(1)}, bf16[160,1024]{1,0:T(8,128)(2,1)S(1)}, u32[]{:S(2)}, u32[]{:S(2)}) collective-permute-start(bf16[160,1024]{1,0:T(8,128)(2,1)S(1)} %get-tuple-element.48), channel_id=1, source_target_pairs={{0,4},{1,5},{2,6},{3,7},{4,0},{5,1},{6,2},{7,3},{8,12},{9,13},{10,... | collective-permute-start | bytes 983048 | tf_op jit(solution)/shard_map/ppermute | solution.py:298
  6.4 1.2 %collective-permute-start.2 = (s32[16,512]{1,0:T(8,128)S(1)}, s32[16,512]{1,0:T(8,128)S(1)}, u32[]{:S(2)}, u32[]{:S(2)}) collective-permute-start(s32[16,512]{1,0:T(8,128)S(1)} %bitcast.5), channel_id=1, source_target_pairs={{0,1},{1,0},{2,3},{3,2},{4,5},{5,4},{6,7},{7,6},{8,9},{9,8},{10,11... | collective-permute-start | bytes 98312 | tf_op jit(solution)/shard_map/ppermute | solution.py:298
  6.4 12.5 %collective-permute-start.4 = (bf16[96,1024]{1,0:T(8,128)(2,1)S(1)}, bf16[96,1024]{1,0:T(8,128)(2,1)S(1)}, u32[]{:S(2)}, u32[]{:S(2)}) collective-permute-start(bf16[96,1024]{1,0:T(8,128)(2,1)S(1)} %get-tuple-element.62), channel_id=1, source_target_pairs={{0,4},{1,5},{2,6},{3,7},{4,0},{5,1},{6,2},{7,3},{8,12},{9,13},{10,... | collective-permute-start | bytes 589832 | tf_op jit(solution)/shard_map/ppermute | solution.py:298
  7.6 1.2 %copy-start.2 = (bf16[512,1024]{1,0:T(8,128)(2,1)S(1)}, bf16[512,1024]{1,0:T(8,128)(2,1)}, u32[]{:S(2)}) copy-start(bf16[512,1024]{1,0:T(8,128)(2,1)} %own_ref.1) | copy-start | bytes 3145732
  10.6 1.0 %copy-start.1 = (bf16[256,1024]{1,0:T(8,128)(2,1)S(1)}, bf16[256,1024]{1,0:T(8,128)(2,1)}, u32[]{:S(2)}) copy-start(bf16[256,1024]{1,0:T(8,128)(2,1)} %refs_0_.1) | copy-start | bytes 1572868
  15.5 8.2 %collective-permute-start.6 = (bf16[160,1024]{1,0:T(8,128)(2,1)S(1)}, bf16[160,1024]{1,0:T(8,128)(2,1)S(1)}, u32[]{:S(2)}, u32[]{:S(2)}) collective-permute-start(bf16[160,1024]{1,0:T(8,128)(2,1)S(1)} %collective-permute-done.1.refs_1_), channel_id=1, source_target_pairs={{0,2},{1,3},{2,0},{3,1},{4,6},{5,7},{6,4},{7,5},{8,10},{9,11},{10,... | collective-permute-start | bytes 983048 | tf_op jit(solution)/shard_map/ppermute | solution.py:298
  16.5 6.7 %collective-permute-start.5 = (bf16[96,1024]{1,0:T(8,128)(2,1)S(1)}, bf16[96,1024]{1,0:T(8,128)(2,1)S(1)}, u32[]{:S(2)}, u32[]{:S(2)}) collective-permute-start(bf16[96,1024]{1,0:T(8,128)(2,1)S(1)} %slice.3), channel_id=1, source_target_pairs={{0,4},{1,5},{2,6},{3,7},{4,0},{5,1},{6,2},{7,3},{8,12},{9,13},{10,... | collective-permute-start | bytes 589832 | tf_op jit(solution)/shard_map/ppermute | solution.py:298
  25.0 1.2 %collective-permute-start.7 = (f32[8,128]{1,0:T(8,128)S(1)}, f32[8,128]{1,0:T(8,128)S(1)}, u32[]{:S(2)}, u32[]{:S(2)}) collective-permute-start(f32[8,128]{1,0:T(8,128)S(1)} %get-tuple-element.81), channel_id=1, source_target_pairs={{0,1},{1,0},{2,3},{3,2},{4,5},{5,4},{6,7},{7,6},{8,9},{9,8},{10,11... | collective-permute-start | bytes 12296 | tf_op jit(solution)/shard_map/ppermute | solution.py:298
  26.3 4.5 %collective-permute-start.10 = (f32[16,128]{1,0:T(8,128)S(1)}, f32[16,128]{1,0:T(8,128)S(1)}, u32[]{:S(2)}, u32[]{:S(2)}) collective-permute-start(f32[16,128]{1,0:T(8,128)S(1)} %mean_pair.1.state_ref), channel_id=1, source_target_pairs={{0,6},{1,25},{2,4},{3,27},{4,2},{5,29},{6,0},{7,31},{8,14},{9,17},... | collective-permute-start | bytes 24584 | tf_op jit(solution)/shard_map/ppermute | solution.py:322
  28.8 3.7 %collective-permute-start.9 = (f32[16,128]{1,0:T(8,128)S(1)}, f32[16,128]{1,0:T(8,128)S(1)}, u32[]{:S(2)}, u32[]{:S(2)}) collective-permute-start(f32[16,128]{1,0:T(8,128)S(1)} %mean_pair.1.state_ref), channel_id=1, source_target_pairs={{0,2},{1,17},{2,0},{3,19},{4,6},{5,21},{6,4},{7,23},{8,10},{9,25},... | collective-permute-start | bytes 24584 | tf_op jit(solution)/shard_map/ppermute | solution.py:322
  29.3 3.7 %collective-permute-start.8 = (f32[16,128]{1,0:T(8,128)S(1)}, f32[16,128]{1,0:T(8,128)S(1)}, u32[]{:S(2)}, u32[]{:S(2)}) collective-permute-start(f32[16,128]{1,0:T(8,128)S(1)} %mean_pair.1.state_ref), channel_id=1, source_target_pairs={{0,4},{1,9},{2,6},{3,11},{4,0},{5,13},{6,2},{7,15},{8,12},{9,1},{1... | collective-permute-start | bytes 24584 | tf_op jit(solution)/shard_map/ppermute | solution.py:322
  33.0 1.2 %collective-permute-start.11 = (f32[8,128]{1,0:T(8,128)S(1)}, f32[8,128]{1,0:T(8,128)S(1)}, u32[]{:S(2)}, u32[]{:S(2)}) collective-permute-start(f32[8,128]{1,0:T(8,128)S(1)} %get-tuple-element.83), channel_id=1, source_target_pairs={{0,1},{1,0},{2,3},{3,2},{4,5},{5,4},{6,7},{7,6},{8,9},{9,8},{10,11... | collective-permute-start | bytes 12296 | tf_op jit(solution)/shard_map/ppermute | solution.py:298
  35.8 1.3 %collective-permute-start.12 = (f32[8,128]{1,0:T(8,128)S(1)}, f32[8,128]{1,0:T(8,128)S(1)}, u32[]{:S(2)}, u32[]{:S(2)}) collective-permute-start(f32[8,128]{1,0:T(8,128)S(1)} %get-tuple-element.89), channel_id=1, source_target_pairs={{0,1},{1,0},{2,3},{3,2},{4,5},{5,4},{6,7},{7,6},{8,9},{9,8},{10,11... | collective-permute-start | bytes 12296 | tf_op jit(solution)/shard_map/ppermute | solution.py:298
  37.1 4.5 %collective-permute-start.15 = (f32[16,128]{1,0:T(8,128)S(1)}, f32[16,128]{1,0:T(8,128)S(1)}, u32[]{:S(2)}, u32[]{:S(2)}) collective-permute-start(f32[16,128]{1,0:T(8,128)S(1)} %best_pair.1.state_ref), channel_id=1, source_target_pairs={{0,6},{1,25},{2,4},{3,27},{4,2},{5,29},{6,0},{7,31},{8,14},{9,17},... | collective-permute-start | bytes 24584 | tf_op jit(solution)/shard_map/ppermute | solution.py:322
  39.7 3.7 %collective-permute-start.14 = (f32[16,128]{1,0:T(8,128)S(1)}, f32[16,128]{1,0:T(8,128)S(1)}, u32[]{:S(2)}, u32[]{:S(2)}) collective-permute-start(f32[16,128]{1,0:T(8,128)S(1)} %best_pair.1.state_ref), channel_id=1, source_target_pairs={{0,2},{1,17},{2,0},{3,19},{4,6},{5,21},{6,4},{7,23},{8,10},{9,25},... | collective-permute-start | bytes 24584 | tf_op jit(solution)/shard_map/ppermute | solution.py:322
  40.1 3.7 %collective-permute-start.13 = (f32[16,128]{1,0:T(8,128)S(1)}, f32[16,128]{1,0:T(8,128)S(1)}, u32[]{:S(2)}, u32[]{:S(2)}) collective-permute-start(f32[16,128]{1,0:T(8,128)S(1)} %best_pair.1.state_ref), channel_id=1, source_target_pairs={{0,4},{1,9},{2,6},{3,11},{4,0},{5,13},{6,2},{7,15},{8,12},{9,1},{1... | collective-permute-start | bytes 24584 | tf_op jit(solution)/shard_map/ppermute | solution.py:322
  43.8 1.3 %collective-permute-start.16 = (f32[4,128]{1,0:T(4,128)S(1)}, f32[4,128]{1,0:T(4,128)S(1)}, u32[]{:S(2)}, u32[]{:S(2)}) collective-permute-start(f32[4,128]{1,0:T(4,128)S(1)} %get-tuple-element.91), channel_id=1, source_target_pairs={{0,1},{1,0},{2,3},{3,2},{4,5},{5,4},{6,7},{7,6},{8,9},{9,8},{10,11... | collective-permute-start | bytes 6152 | tf_op jit(solution)/shard_map/ppermute | solution.py:298

commit v7 on v6

--- a/solution.py
+++ b/solution.py
@@ -238,12 +238,31 @@
     send_ref[...] = choose(by_tgt[wide // 2 :] if last else by_tgt, by_src[2 * slots :], send_ref.shape[0])
 
 
-def widen_kernel(wide, total_ref, got_ref, wide_ref, bwd_ref):
-    high = wide_ref.shape[0] // LANES
-    fwd = choose(got_ref[:high, :], total_ref[:high, :], high)
+def widen(fwd, wide_ref):
+    for g in range(fwd.shape[0]):
+        wide_ref[g * LANES : (g + 1) * LANES, :] = jnp.broadcast_to(fwd[g : g + 1, :], (LANES, LANES)).T
+
+
+def widen_own_kernel(total_ref, wide_ref):
+    @pl.when(lax.axis_index("tgt") % 2 == 0)
+    def _():
+        widen(total_ref[: wide_ref.shape[0] // LANES, :], wide_ref)
+
+    @pl.when(lax.axis_index("tgt") % 2 == 1)
+    def _():
+        wide_ref[...] = jnp.zeros_like(wide_ref)
+
+
+def widen_kernel(wide, total_ref, got_ref, own_wide_ref, wide_ref, bwd_ref):
     bwd_ref[...] = choose(total_ref[:wide, :], turn_pair(got_ref[:wide, :]), wide)
-    for g in range(high):
-        wide_ref[g * LANES : (g + 1) * LANES, :] = jnp.broadcast_to(fwd[g : g + 1, :], (LANES, LANES)).T
+
+    @pl.when(lax.axis_index("tgt") % 2 == 1)
+    def _():
+        widen(got_ref[: wide_ref.shape[0] // LANES, :], wide_ref)
+
+    @pl.when(lax.axis_index("tgt") % 2 == 0)
+    def _():
+        wide_ref[...] = own_wide_ref[...]
 
 
 def margin_kernel(slots, columns, *refs):
@@ -440,7 +459,10 @@
         functools.partial(pair_kept_kernel, high, wide), "mean_pair", (state_rows,), keep_tgt, keep_src, got_sums
     )
     total, got_sums = reduce_all(jnp.add, high, wide, state, "mean_collect", False)
-    wide_fwd, bwd = small_call(functools.partial(widen_kernel, wide), "widen", (slots * BLOCK, wide), total, got_sums)
+    (own_wide,) = small_call(widen_own_kernel, "widen_own", (slots * BLOCK,), total)
+    wide_fwd, bwd = small_call(
+        functools.partial(widen_kernel, wide), "widen", (slots * BLOCK, wide), total, got_sums, own_wide
+    )
     src_best, tgt_best, send = pl.pallas_call(
         functools.partial(margin_kernel, slots, columns),
         out_shape=(jax.ShapeDtypeStruct((high, LANES), jnp.float32), bwd_sums, sent),

time: 46.1 us -> 46.1 us (level)
  Pallas kernels: 12.2 us -> 13 us
  waiting for transfers between devices: 14 us -> 13.4 us
    pallas_call x1, Pallas kernels: 1.33 us -> 2.04 us  [body(): pl.pallas_call(functools.partial(margin_kernel, slots, columns), out_shap...]
where the time goes in v7:
time: 46.1 us; the launch traced here: 46 us
  starting transfers between devices  15.9 us (34%)
  waiting for transfers between devices  13.4 us (29%)
  Pallas kernels  13 us (28%)
  local copies, waits for them, and re-layouts  2.97 us (6%)
  between operations  0.76 us (2%)
    ppermute x11, starting transfers between devices, swap(): return lax.ppermute(value, axis, [(i, i ^ mask) for i in range(count)])  8.95 us
    ppermute x11, waiting for transfers between devices, swap(): return lax.ppermute(value, axis, [(i, i ^ mask) for i in range(count)])  7.42 us
    ppermute x6, starting transfers between devices, reduce_all(): parts.append(lax.ppermute(state, ('src', 'tgt'), pairs))  6.98 us
    ppermute x6, waiting for transfers between devices, reduce_all(): parts.append(lax.ppermute(state, ('src', 'tgt'), pairs))  5.98 us
    pallas_call x3, Pallas kernels, score(): pl.pallas_call(functools.partial(score_kernel, slot, len(parts)), out_sha...  5.53 us
    unnamed x12, local copies, waits for them, and re-layouts  2.95 us
    pallas_call x1, Pallas kernels, body(): pl.pallas_call(functools.partial(margin_kernel, slots, columns), out_shap...  2.04 us
    pallas_call x1, Pallas kernels, body(): pl.pallas_call(functools.partial(prepare_kernel, slots), out_shape=(unit_...  1.74 us
  transfers between devices with their start and end apart: 17, of which 16 were waited for; matrix products, arithmetic and copies ran while one was open for 0% of the time, Pallas kernels for 19%

profile of v7, /device:TPU:0, one launch (start us, length us, event | category | flops | bytes accessed | tf_op | source)
XLA Modules:
  0.0 46.0 jit_solution(2748541528245573448)
XLA Ops:
  1.1 2.6 %collective-permute-start = (bf16[256,1024]{1,0:T(8,128)(2,1)}, bf16[256,1024]{1,0:T(8,128)(2,1)S(1)}, u32[]{:S(2)}, u32[]{:S(2)}) collective-permute-start(bf16[256,1024]{1,0:T(8,128)(2,1)} %refs_0_.1), channel_id=1, source_target_pairs={{0,2},{1,3},{2,0},{3,1},{4,6},{5,7},{6,4},{7,5},{8,10},{9,11},{10,... | collective-permute-start | bytes 1572872 | tf_op jit(solution)/shard_map/ppermute | solution.py:317
  3.7 1.1 %copy-done = bf16[256,1024]{1,0:T(8,128)(2,1)S(1)} copy-done((bf16[256,1024]{1,0:T(8,128)(2,1)S(1)}, bf16[256,1024]{1,0:T(8,128)(2,1)}, u32[]{:S(2)}) %copy-start) | copy-done | bytes 524312
  4.8 1.6 %collective-permute-start.1 = (bf16[160,1024]{1,0:T(8,128)(2,1)S(1)}, bf16[160,1024]{1,0:T(8,128)(2,1)S(1)}, u32[]{:S(2)}, u32[]{:S(2)}) collective-permute-start(bf16[160,1024]{1,0:T(8,128)(2,1)S(1)} %get-tuple-element.48), channel_id=1, source_target_pairs={{0,4},{1,5},{2,6},{3,7},{4,0},{5,1},{6,2},{7,3},{8,12},{9,13},{10,... | collective-permute-start | bytes 983048 | tf_op jit(solution)/shard_map/ppermute | solution.py:317
  6.4 0.8 %collective-permute-start.4 = (bf16[96,1024]{1,0:T(8,128)(2,1)S(1)}, bf16[96,1024]{1,0:T(8,128)(2,1)S(1)}, u32[]{:S(2)}, u32[]{:S(2)}) collective-permute-start(bf16[96,1024]{1,0:T(8,128)(2,1)S(1)} %get-tuple-element.62), channel_id=1, source_target_pairs={{0,4},{1,5},{2,6},{3,7},{4,0},{5,1},{6,2},{7,3},{8,12},{9,13},{10,... | collective-permute-start | bytes 589832 | tf_op jit(solution)/shard_map/ppermute | solution.py:317
  7.6 1.2 %copy-done.2 = bf16[512,1024]{1,0:T(8,128)(2,1)S(1)} copy-done((bf16[512,1024]{1,0:T(8,128)(2,1)S(1)}, bf16[512,1024]{1,0:T(8,128)(2,1)}, u32[]{:S(2)}) %copy-start.2) | copy-done | bytes 1048600
  8.9 1.7 %prepare.1 = (bf16[512,1024]{1,0:T(8,128)(2,1)S(1)}, s32[1,128,128]{2,1,0:T(8,128)S(1)}, s32[1,128,128]{2,1,0:T(8,128)S(1)}, s32[16]{0:T(128)S(1)}) custom-call(bf16[512,1024]{1,0:T(8,128)(2,1)S(1)} %copy-done.2, s32[8,8]{1,0:T(8,128)S(1)} %copy-done.5, s32[16,2048]{1,0:T(8,128)S(1)} %bitcast.4, s32[16,512]{1,0:T(8,128)S(1)} %bitcast.6, ...), custom_call_target="tpu_custom_call" | custom-call | flops 1000 | bytes 1000 | tf_op jit(solution)/shard_map/prepare/pallas_call | solution.py:384
  11.7 1.8 %score_0.1 = (f32[256,1024]{1,0:T(8,128)S(1)}, f32[2,128]{1,0:T(2,128)S(1)}, f32[8,128]{1,0:T(8,128)S(1)}) custom-call(bf16[512,1024]{1,0:T(8,128)(2,1)S(1)} %get-tuple-element.50.own_ref, bf16[512,1024]{1,0:T(8,128)(2,1)S(1)} %normalise.1.sibling_ref, s32[1,128,128]{2,1,0:T(8,128)S(1)} %get-tuple-element.52.fwd_at_ref, ...), custom_call_target="tpu_custom_call" | custom-call | flops 1000 | bytes 1000 | tf_op jit(solution)/shard_map/score_0/pallas_call | solution.py:405
  13.5 2.0 %collective-permute-done.1.refs_1_ = bf16[160,1024]{1,0:T(8,128)(2,1)S(1)} collective-permute-done((bf16[160,1024]{1,0:T(8,128)(2,1)S(1)}, bf16[160,1024]{1,0:T(8,128)(2,1)S(1)}, u32[]{:S(2)}, u32[]{:S(2)}) %collective-permute-start.1) | collective-permute-done | bytes 327712 | tf_op jit(solution)/shard_map/ppermute | solution.py:317
  15.5 1.0 %collective-permute-done.refs_0_ = bf16[256,1024]{1,0:T(8,128)(2,1)S(1)} collective-permute-done((bf16[256,1024]{1,0:T(8,128)(2,1)}, bf16[256,1024]{1,0:T(8,128)(2,1)S(1)}, u32[]{:S(2)}, u32[]{:S(2)}) %collective-permute-start) | collective-permute-done | bytes 524320 | tf_op jit(solution)/shard_map/ppermute | solution.py:317
  16.5 1.9 %collective-permute-start.5 = (bf16[96,1024]{1,0:T(8,128)(2,1)S(1)}, bf16[96,1024]{1,0:T(8,128)(2,1)S(1)}, u32[]{:S(2)}, u32[]{:S(2)}) collective-permute-start(bf16[96,1024]{1,0:T(8,128)(2,1)S(1)} %slice.3), channel_id=1, source_target_pairs={{0,4},{1,5},{2,6},{3,7},{4,0},{5,1},{6,2},{7,3},{8,12},{9,13},{10,... | collective-permute-start | bytes 589832 | tf_op jit(solution)/shard_map/ppermute | solution.py:317
  18.9 1.8 %score_2.1 = (f32[256,1024]{1,0:T(8,128)S(1)}, f32[2,128]{1,0:T(2,128)S(1)}, f32[8,128]{1,0:T(8,128)S(1)}) custom-call(bf16[512,1024]{1,0:T(8,128)(2,1)S(1)} %get-tuple-element.50.own_ref, bf16[512,1024]{1,0:T(8,128)(2,1)S(1)} %normalise.1.sibling_ref, s32[1,128,128]{2,1,0:T(8,128)S(1)} %get-tuple-element.52.fwd_at_ref, ...), custom_call_target="tpu_custom_call" | custom-call | flops 1073741824 | bytes 1048576 | tf_op jit(solution)/shard_map/score_2/pallas_call | solution.py:405
  20.7 1.8 %score_1.1 = (f32[256,1024]{1,0:T(8,128)S(1)}, f32[2,128]{1,0:T(2,128)S(1)}, f32[8,128]{1,0:T(8,128)S(1)}) custom-call(bf16[512,1024]{1,0:T(8,128)(2,1)S(1)} %get-tuple-element.50.own_ref, bf16[512,1024]{1,0:T(8,128)(2,1)S(1)} %normalise.1.sibling_ref, s32[1,128,128]{2,1,0:T(8,128)S(1)} %get-tuple-element.52.fwd_at_ref, ...), custom_call_target="tpu_custom_call" | custom-call | flops 1073741824 | bytes 1048576 | tf_op jit(solution)/shard_map/score_1/pallas_call | solution.py:405
  23.6 1.4 %last_first.1 = (bf16[256,1024]{1,0:T(8,128)(2,1)S(1)}, f32[256,1024]{1,0:T(8,128)S(1)}, f32[8,128]{1,0:T(8,128)S(1)}, f32[8,128]{1,0:T(8,128)S(1)}) custom-call(bf16[512,1024]{1,0:T(8,128)(2,1)S(1)} %get-tuple-element.50.own_ref, bf16[512,1024]{1,0:T(8,128)(2,1)S(1)} %normalise.1.sibling_ref, s32[1,128,128]{2,1,0:T(8,128)S(1)} %get-tuple-element.52.fwd_at_ref, ...), custom_call_target="tpu_custom_call" | custom-call | flops 536870912 | bytes 1048576 | tf_op jit(solution)/shard_map/last_first/pallas_call | solution.py:434
  25.1 1.0 %last_second.1 = (f32[256,1024]{1,0:T(8,128)S(1)}, f32[8,128]{1,0:T(8,128)S(1)}) custom-call(bf16[512,1024]{1,0:T(8,128)(2,1)S(1)} %get-tuple-element.50.own_ref, bf16[512,1024]{1,0:T(8,128)(2,1)S(1)} %normalise.1.sibling_ref, s32[1,128,128]{2,1,0:T(8,128)S(1)} %get-tuple-element.52.fwd_at_ref, ...), custom_call_target="tpu_custom_call", output_to_operand_aliasing={{0}: (4, {})} | custom-call | flops 536870912 | bytes 1048576 | tf_op jit(solution)/shard_map/last_second/pallas_call | solution.py:445
  26.3 2.5 %collective-permute-start.10 = (f32[16,128]{1,0:T(8,128)S(1)}, f32[16,128]{1,0:T(8,128)S(1)}, u32[]{:S(2)}, u32[]{:S(2)}) collective-permute-start(f32[16,128]{1,0:T(8,128)S(1)} %mean_pair.1.state_ref), channel_id=1, source_target_pairs={{0,6},{1,25},{2,4},{3,27},{4,2},{5,29},{6,0},{7,31},{8,14},{9,17},... | collective-permute-start | bytes 24584 | tf_op jit(solution)/shard_map/ppermute | solution.py:341
  29.8 1.1 %collective-permute-done.10.refs_2_ = f32[16,128]{1,0:T(8,128)S(1)} collective-permute-done((f32[16,128]{1,0:T(8,128)S(1)}, f32[16,128]{1,0:T(8,128)S(1)}, u32[]{:S(2)}, u32[]{:S(2)}) %collective-permute-start.10) | collective-permute-done | bytes 8224 | tf_op jit(solution)/shard_map/ppermute | solution.py:341
  30.8 1.6 %collective-permute-done.9.refs_1_ = f32[16,128]{1,0:T(8,128)S(1)} collective-permute-done((f32[16,128]{1,0:T(8,128)S(1)}, f32[16,128]{1,0:T(8,128)S(1)}, u32[]{:S(2)}, u32[]{:S(2)}) %collective-permute-start.9) | collective-permute-done | bytes 8224 | tf_op jit(solution)/shard_map/ppermute | solution.py:341
  34.3 2.0 %margins.1 = (f32[8,128]{1,0:T(8,128)S(1)}, f32[8,128]{1,0:T(8,128)S(1)}, f32[8,128]{1,0:T(8,128)S(1)}) custom-call(f32[256,1024]{1,0:T(8,128)S(1)} %get-tuple-element.60.refs_0_, f32[256,1024]{1,0:T(8,128)S(1)} %get-tuple-element.68.refs_1_, f32[256,1024]{1,0:T(8,128)S(1)} %get-tuple-element.69.refs_2_, f32[256,1024]{1,0:T(8,128)S(1)} %get-tuple-element.78.refs_3_, ...), custom_call_target="tpu_custom_call" | custom-call | flops 10485760 | bytes 4194304 | tf_op jit(solution)/shard_map/margins/pallas_call | solution.py:466
  36.8 0.8 %collective-permute-done.12.got_ref = f32[8,128]{1,0:T(8,128)S(1)} collective-permute-done((f32[8,128]{1,0:T(8,128)S(1)}, f32[8,128]{1,0:T(8,128)S(1)}, u32[]{:S(2)}, u32[]{:S(2)}) %collective-permute-start.12) | collective-permute-done | bytes 4128 | tf_op jit(solution)/shard_map/ppermute | solution.py:317
  37.6 2.0 %collective-permute-start.15 = (f32[16,128]{1,0:T(8,128)S(1)}, f32[16,128]{1,0:T(8,128)S(1)}, u32[]{:S(2)}, u32[]{:S(2)}) collective-permute-start(f32[16,128]{1,0:T(8,128)S(1)} %best_pair.1.state_ref), channel_id=1, source_target_pairs={{0,6},{1,25},{2,4},{3,27},{4,2},{5,29},{6,0},{7,31},{8,14},{9,17},... | collective-permute-start | bytes 24584 | tf_op jit(solution)/shard_map/ppermute | solution.py:341
  40.2 0.9 %collective-permute-start.13 = (f32[16,128]{1,0:T(8,128)S(1)}, f32[16,128]{1,0:T(8,128)S(1)}, u32[]{:S(2)}, u32[]{:S(2)}) collective-permute-start(f32[16,128]{1,0:T(8,128)S(1)} %best_pair.1.state_ref), channel_id=1, source_target_pairs={{0,4},{1,9},{2,6},{3,11},{4,0},{5,13},{6,2},{7,15},{8,12},{9,1},{1... | collective-permute-start | bytes 24584 | tf_op jit(solution)/shard_map/ppermute | solution.py:341
  41.1 1.1 %collective-permute-done.15.refs_2_ = f32[16,128]{1,0:T(8,128)S(1)} collective-permute-done((f32[16,128]{1,0:T(8,128)S(1)}, f32[16,128]{1,0:T(8,128)S(1)}, u32[]{:S(2)}, u32[]{:S(2)}) %collective-permute-start.15) | collective-permute-done | bytes 8224 | tf_op jit(solution)/shard_map/ppermute | solution.py:341
  42.2 1.1 %collective-permute-done.14.refs_1_ = f32[16,128]{1,0:T(8,128)S(1)} collective-permute-done((f32[16,128]{1,0:T(8,128)S(1)}, f32[16,128]{1,0:T(8,128)S(1)}, u32[]{:S(2)}, u32[]{:S(2)}) %collective-permute-start.14) | collective-permute-done | bytes 8224 | tf_op jit(solution)/shard_map/ppermute | solution.py:341
  44.6 0.8 %collective-permute-done.16.got_ref = f32[4,128]{1,0:T(4,128)S(1)} collective-permute-done((f32[4,128]{1,0:T(4,128)S(1)}, f32[4,128]{1,0:T(4,128)S(1)}, u32[]{:S(2)}, u32[]{:S(2)}) %collective-permute-start.16) | collective-permute-done | bytes 2080 | tf_op jit(solution)/shard_map/ppermute | solution.py:317
  (39 shorter events, 9.7 us)
Async XLA Ops:
  0.6 10.0 %collective-permute-start.3 = (bf16[512,1024]{1,0:T(8,128)(2,1)}, bf16[512,1024]{1,0:T(8,128)(2,1)S(1)}, u32[]{:S(2)}, u32[]{:S(2)}) collective-permute-start(bf16[512,1024]{1,0:T(8,128)(2,1)} %own_ref.1), channel_id=1, source_target_pairs={{0,1},{1,0},{2,3},{3,2},{4,5},{5,4},{6,7},{7,6},{8,9},{9,8},{10,11... | collective-permute-start | bytes 3145736 | tf_op jit(solution)/shard_map/ppermute | solution.py:317
  1.1 15.3 %collective-permute-start = (bf16[256,1024]{1,0:T(8,128)(2,1)}, bf16[256,1024]{1,0:T(8,128)(2,1)S(1)}, u32[]{:S(2)}, u32[]{:S(2)}) collective-permute-start(bf16[256,1024]{1,0:T(8,128)(2,1)} %refs_0_.1), channel_id=1, source_target_pairs={{0,2},{1,3},{2,0},{3,1},{4,6},{5,7},{6,4},{7,5},{8,10},{9,11},{10,... | collective-permute-start | bytes 1572872 | tf_op jit(solution)/shard_map/ppermute | solution.py:317
  3.7 1.1 %copy-start = (bf16[256,1024]{1,0:T(8,128)(2,1)S(1)}, bf16[256,1024]{1,0:T(8,128)(2,1)}, u32[]{:S(2)}) copy-start(bf16[256,1024]{1,0:T(8,128)(2,1)} %refs_0_.1) | copy-start | bytes 1572868
  4.8 1.6 %copy-start.4 = (s32[512,16]{0,1:T(8,128)S(1)}, s32[512,16]{0,1:T(8,128)}, u32[]{:S(2)}) copy-start(s32[512,16]{0,1:T(8,128)} %param.9) | copy-start | bytes 98308
  4.8 2.9 %copy-start.3 = (s32[2048,16]{0,1:T(8,128)S(1)}, s32[2048,16]{0,1:T(8,128)}, u32[]{:S(2)}) copy-start(s32[2048,16]{0,1:T(8,128)} %param.8) | copy-start | bytes 393220
  4.8 2.8 %copy-start.5 = (s32[8,8]{1,0:T(8,128)S(1)}, s32[8,8]{1,0:T(8,128)}, u32[]{:S(2)}) copy-start(s32[8,8]{1,0:T(8,128)} %pairs_ref.1) | copy-start | bytes 772
  4.8 10.6 %collective-permute-start.1 = (bf16[160,1024]{1,0:T(8,128)(2,1)S(1)}, bf16[160,1024]{1,0:T(8,128)(2,1)S(1)}, u32[]{:S(2)}, u32[]{:S(2)}) collective-permute-start(bf16[160,1024]{1,0:T(8,128)(2,1)S(1)} %get-tuple-element.48), channel_id=1, source_target_pairs={{0,4},{1,5},{2,6},{3,7},{4,0},{5,1},{6,2},{7,3},{8,12},{9,13},{10,... | collective-permute-start | bytes 983048 | tf_op jit(solution)/shard_map/ppermute | solution.py:317
  6.4 1.2 %collective-permute-start.2 = (s32[16,512]{1,0:T(8,128)S(1)}, s32[16,512]{1,0:T(8,128)S(1)}, u32[]{:S(2)}, u32[]{:S(2)}) collective-permute-start(s32[16,512]{1,0:T(8,128)S(1)} %bitcast.5), channel_id=1, source_target_pairs={{0,1},{1,0},{2,3},{3,2},{4,5},{5,4},{6,7},{7,6},{8,9},{9,8},{10,11... | collective-permute-start | bytes 98312 | tf_op jit(solution)/shard_map/ppermute | solution.py:317
  6.4 12.5 %collective-permute-start.4 = (bf16[96,1024]{1,0:T(8,128)(2,1)S(1)}, bf16[96,1024]{1,0:T(8,128)(2,1)S(1)}, u32[]{:S(2)}, u32[]{:S(2)}) collective-permute-start(bf16[96,1024]{1,0:T(8,128)(2,1)S(1)} %get-tuple-element.62), channel_id=1, source_target_pairs={{0,4},{1,5},{2,6},{3,7},{4,0},{5,1},{6,2},{7,3},{8,12},{9,13},{10,... | collective-permute-start | bytes 589832 | tf_op jit(solution)/shard_map/ppermute | solution.py:317
  7.6 1.2 %copy-start.2 = (bf16[512,1024]{1,0:T(8,128)(2,1)S(1)}, bf16[512,1024]{1,0:T(8,128)(2,1)}, u32[]{:S(2)}) copy-start(bf16[512,1024]{1,0:T(8,128)(2,1)} %own_ref.1) | copy-start | bytes 3145732
  10.6 1.0 %copy-start.1 = (bf16[256,1024]{1,0:T(8,128)(2,1)S(1)}, bf16[256,1024]{1,0:T(8,128)(2,1)}, u32[]{:S(2)}) copy-start(bf16[256,1024]{1,0:T(8,128)(2,1)} %refs_0_.1) | copy-start | bytes 1572868
  15.5 8.2 %collective-permute-start.6 = (bf16[160,1024]{1,0:T(8,128)(2,1)S(1)}, bf16[160,1024]{1,0:T(8,128)(2,1)S(1)}, u32[]{:S(2)}, u32[]{:S(2)}) collective-permute-start(bf16[160,1024]{1,0:T(8,128)(2,1)S(1)} %collective-permute-done.1.refs_1_), channel_id=1, source_target_pairs={{0,2},{1,3},{2,0},{3,1},{4,6},{5,7},{6,4},{7,5},{8,10},{9,11},{10,... | collective-permute-start | bytes 983048 | tf_op jit(solution)/shard_map/ppermute | solution.py:317
  16.5 6.7 %collective-permute-start.5 = (bf16[96,1024]{1,0:T(8,128)(2,1)S(1)}, bf16[96,1024]{1,0:T(8,128)(2,1)S(1)}, u32[]{:S(2)}, u32[]{:S(2)}) collective-permute-start(bf16[96,1024]{1,0:T(8,128)(2,1)S(1)} %slice.3), channel_id=1, source_target_pairs={{0,4},{1,5},{2,6},{3,7},{4,0},{5,1},{6,2},{7,3},{8,12},{9,13},{10,... | collective-permute-start | bytes 589832 | tf_op jit(solution)/shard_map/ppermute | solution.py:317
  25.0 1.2 %collective-permute-start.7 = (f32[8,128]{1,0:T(8,128)S(1)}, f32[8,128]{1,0:T(8,128)S(1)}, u32[]{:S(2)}, u32[]{:S(2)}) collective-permute-start(f32[8,128]{1,0:T(8,128)S(1)} %get-tuple-element.81), channel_id=1, source_target_pairs={{0,1},{1,0},{2,3},{3,2},{4,5},{5,4},{6,7},{7,6},{8,9},{9,8},{10,11... | collective-permute-start | bytes 12296 | tf_op jit(solution)/shard_map/ppermute | solution.py:317
  26.3 4.5 %collective-permute-start.10 = (f32[16,128]{1,0:T(8,128)S(1)}, f32[16,128]{1,0:T(8,128)S(1)}, u32[]{:S(2)}, u32[]{:S(2)}) collective-permute-start(f32[16,128]{1,0:T(8,128)S(1)} %mean_pair.1.state_ref), channel_id=1, source_target_pairs={{0,6},{1,25},{2,4},{3,27},{4,2},{5,29},{6,0},{7,31},{8,14},{9,17},... | collective-permute-start | bytes 24584 | tf_op jit(solution)/shard_map/ppermute | solution.py:341
  28.8 3.7 %collective-permute-start.9 = (f32[16,128]{1,0:T(8,128)S(1)}, f32[16,128]{1,0:T(8,128)S(1)}, u32[]{:S(2)}, u32[]{:S(2)}) collective-permute-start(f32[16,128]{1,0:T(8,128)S(1)} %mean_pair.1.state_ref), channel_id=1, source_target_pairs={{0,2},{1,17},{2,0},{3,19},{4,6},{5,21},{6,4},{7,23},{8,10},{9,25},... | collective-permute-start | bytes 24584 | tf_op jit(solution)/shard_map/ppermute | solution.py:341
  29.3 3.7 %collective-permute-start.8 = (f32[16,128]{1,0:T(8,128)S(1)}, f32[16,128]{1,0:T(8,128)S(1)}, u32[]{:S(2)}, u32[]{:S(2)}) collective-permute-start(f32[16,128]{1,0:T(8,128)S(1)} %mean_pair.1.state_ref), channel_id=1, source_target_pairs={{0,4},{1,9},{2,6},{3,11},{4,0},{5,13},{6,2},{7,15},{8,12},{9,1},{1... | collective-permute-start | bytes 24584 | tf_op jit(solution)/shard_map/ppermute | solution.py:341
  33.0 1.2 %collective-permute-start.11 = (f32[8,128]{1,0:T(8,128)S(1)}, f32[8,128]{1,0:T(8,128)S(1)}, u32[]{:S(2)}, u32[]{:S(2)}) collective-permute-start(f32[8,128]{1,0:T(8,128)S(1)} %get-tuple-element.83), channel_id=1, source_target_pairs={{0,1},{1,0},{2,3},{3,2},{4,5},{5,4},{6,7},{7,6},{8,9},{9,8},{10,11... | collective-permute-start | bytes 12296 | tf_op jit(solution)/shard_map/ppermute | solution.py:317
  36.3 1.3 %collective-permute-start.12 = (f32[8,128]{1,0:T(8,128)S(1)}, f32[8,128]{1,0:T(8,128)S(1)}, u32[]{:S(2)}, u32[]{:S(2)}) collective-permute-start(f32[8,128]{1,0:T(8,128)S(1)} %get-tuple-element.89), channel_id=1, source_target_pairs={{0,1},{1,0},{2,3},{3,2},{4,5},{5,4},{6,7},{7,6},{8,9},{9,8},{10,11... | collective-permute-start | bytes 12296 | tf_op jit(solution)/shard_map/ppermute | solution.py:317
  37.6 4.5 %collective-permute-start.15 = (f32[16,128]{1,0:T(8,128)S(1)}, f32[16,128]{1,0:T(8,128)S(1)}, u32[]{:S(2)}, u32[]{:S(2)}) collective-permute-start(f32[16,128]{1,0:T(8,128)S(1)} %best_pair.1.state_ref), channel_id=1, source_target_pairs={{0,6},{1,25},{2,4},{3,27},{4,2},{5,29},{6,0},{7,31},{8,14},{9,17},... | collective-permute-start | bytes 24584 | tf_op jit(solution)/shard_map/ppermute | solution.py:341
  39.6 3.7 %collective-permute-start.14 = (f32[16,128]{1,0:T(8,128)S(1)}, f32[16,128]{1,0:T(8,128)S(1)}, u32[]{:S(2)}, u32[]{:S(2)}) collective-permute-start(f32[16,128]{1,0:T(8,128)S(1)} %best_pair.1.state_ref), channel_id=1, source_target_pairs={{0,2},{1,17},{2,0},{3,19},{4,6},{5,21},{6,4},{7,23},{8,10},{9,25},... | collective-permute-start | bytes 24584 | tf_op jit(solution)/shard_map/ppermute | solution.py:341
  40.2 3.7 %collective-permute-start.13 = (f32[16,128]{1,0:T(8,128)S(1)}, f32[16,128]{1,0:T(8,128)S(1)}, u32[]{:S(2)}, u32[]{:S(2)}) collective-permute-start(f32[16,128]{1,0:T(8,128)S(1)} %best_pair.1.state_ref), channel_id=1, source_target_pairs={{0,4},{1,9},{2,6},{3,11},{4,0},{5,13},{6,2},{7,15},{8,12},{9,1},{1... | collective-permute-start | bytes 24584 | tf_op jit(solution)/shard_map/ppermute | solution.py:341
  43.9 1.5 %collective-permute-start.16 = (f32[4,128]{1,0:T(4,128)S(1)}, f32[4,128]{1,0:T(4,128)S(1)}, u32[]{:S(2)}, u32[]{:S(2)}) collective-permute-start(f32[4,128]{1,0:T(4,128)S(1)} %get-tuple-element.91), channel_id=1, source_target_pairs={{0,1},{1,0},{2,3},{3,2},{4,5},{5,4},{6,7},{7,6},{8,9},{9,8},{10,11... | collective-permute-start | bytes 6152 | tf_op jit(solution)/shard_map/ppermute | solution.py:317
